TPU v7x, 32 devices: a whole 2x2x4 slice. The times are simulated.
32 devices in a mesh: groups: 2 (over x), node: 8 (over z, y), lane: 2 (over core).
Axes of the slice: x: 2, y: 2, z: 4, core: 2. Of those that a mesh axis runs over, the one named last changes fastest.
Arguments:
- expert_hidden: bfloat16 [512, 8, 1024], P(('groups', 'node', 'lane')), parts along dimension 0, may hold values from -6 to 6
- gate_scores: float32 [512, 8], P(('groups', 'node', 'lane')), parts along dimension 0, may hold values from 0.05 to 1
- node_lists: int32 [512, 4], P(('groups', 'node', 'lane')), parts along dimension 0, may hold values from 0 to 7, all different within a row; in each aligned block of 16 rows (0 to 15, 16 to 31, ...) at most 8 rows name the same one
- expert_picks: int32 [512, 8], P(('groups', 'node', 'lane')), parts along dimension 0, may hold values from 0 to 7, as said below
- routed_down: bfloat16 [16, 1024, 3584], P(('node', 'lane')), may hold values from -0.1875 to 0.1875
- query_latent: bfloat16 [256, 64, 512], P(('groups', 'node', 'lane')), parts along dimension 0, may hold values from -6 to 6
- query_rope: bfloat16 [256, 4096], P(('groups', 'node', 'lane')), parts along dimension 0, may hold values from -100 to 100
- cache_latent: bfloat16 [256, 128, 512], P(('groups', 'node', 'lane')), parts along dimension 0, may hold values from -6 to 6
- cache_rope: bfloat16 [256, 64, 128], P(('groups', 'node', 'lane')), parts along dimension 0, may hold values from -6 to 6
- cache_lengths: int32 [256], P(('groups', 'node', 'lane')), parts along dimension 0, may hold values from 2 to 128, as said below
Outputs:
- moe_out: bfloat16 [512, 3584], P(('groups', 'node', 'lane')), parts along dimension 0
- context: bfloat16 [256, 64, 512], P(('groups', 'node', 'lane')), parts along dimension 0
There are 2 independent parts, one for each index of `groups`. A program takes and returns all parts, laid end to end along the dimension named above; an argument that names none is the same for every part. Nothing has to cross between parts.
Inputs may be any that keep to these rules, and one draw needn't show every extreme that they name: `node_lists`: each row names 4 different nodes. Among the 16 rows of one device no node is named by more than 8 rows, and in some devices' rows one node is named by exactly 8 rows. `expert_picks`: each row holds 8 different numbers; number p stands for local expert p % 2 of node node_lists[row, p // 2]. `cache_lengths`: the rows of every device include one of length 128.
All inputs are finite; a program needn't handle non-finite values.
Results may differ from a plain program's by a relative error of at most 0.005.
Values may be sent and summed in bfloat16 or wider, within the bound.
No kernel may reach another device: no remote copies, remote signals or barrier semaphores. Data moves between devices by JAX's collectives and lax.ppermute only.
A program may use at most 64 MiB of HBM per device.

v0:
```python
import jax
import jax.numpy as jnp
from jax import lax
from jax.sharding import PartitionSpec as P

NODES_TOP = 4


score_scale = 192.0 ** (-0.5)
route_scale = 2.5


def attend(query_latent, query_rope, cache_latent, cache_rope, cache_lengths):
    row_count, head_count, latent_width = query_latent.shape
    rope_width = cache_rope.shape[1]
    scores = jnp.einsum(
        "rhl,rcl->rhc", query_latent, cache_latent, preferred_element_type=jnp.float32
    )
    rope_query = query_rope.reshape(row_count, head_count, rope_width)
    scores = scores + jnp.einsum(
        "rhp,rpc->rhc", rope_query, cache_rope, preferred_element_type=jnp.float32
    )
    scores = scores * score_scale
    position = jnp.arange(cache_latent.shape[1], dtype=jnp.int32)
    valid = position[None, None, :] < cache_lengths[:, None, None]
    scores = jnp.where(valid, scores, -jnp.inf)
    highest = jnp.max(scores, axis=-1, keepdims=True)
    expd = jnp.exp(scores - highest)
    probs = (expd / jnp.sum(expd, axis=-1, keepdims=True)).astype(jnp.bfloat16)
    context = jnp.einsum("rhc,rcl->rhl", probs, cache_latent, preferred_element_type=jnp.float32)
    return context.astype(jnp.bfloat16)


def local(
    expert_hidden,
    gate_scores,
    node_lists,
    expert_picks,
    routed_down,
    query_latent,
    query_rope,
    cache_latent,
    cache_rope,
    cache_lengths,
):
    node_count = lax.axis_size("node")
    lane_count = lax.axis_size("lane")
    row_count, pick_count, hidden_width = expert_hidden.shape
    width = routed_down.shape[2]
    capacity = max(
        2, min(row_count // 2, 2 * ((row_count * NODES_TOP + node_count - 1) // node_count))
    )
    down_matrix = routed_down[0]
    combine = (route_scale * gate_scores / jnp.sum(gate_scores, axis=-1, keepdims=True)).astype(
        jnp.bfloat16
    )
    choice_ids = jnp.arange(NODES_TOP * lane_count, dtype=jnp.int32)
    pick_table = expert_picks[:, :, None] == choice_ids[None, None, :]
    slot_hidden = jnp.einsum(
        "rkq,rkh->rqh",
        pick_table.astype(jnp.bfloat16),
        expert_hidden,
        preferred_element_type=jnp.float32,
    )
    slot_hidden = slot_hidden.astype(jnp.bfloat16).reshape(
        row_count * NODES_TOP, lane_count, hidden_width
    )
    slot_weights = jnp.einsum(
        "rkq,rk->rq",
        pick_table.astype(jnp.float32),
        combine.astype(jnp.float32),
        precision=lax.Precision.HIGHEST,
    )
    slot_weights = slot_weights.reshape(row_count * NODES_TOP, lane_count)
    membership = jnp.sum(
        (node_lists[:, :, None] == jnp.arange(node_count, dtype=jnp.int32)[None, None, :]).astype(
            jnp.int32
        ),
        axis=1,
    )
    earlier = jnp.cumsum(membership, axis=0) - membership
    slots = jnp.take_along_axis(earlier, node_lists, axis=1)
    target = (node_lists * capacity + slots).reshape(-1)
    placing = target[:, None] == jnp.arange(node_count * capacity, dtype=jnp.int32)[None, :]
    placing = placing.reshape(row_count * NODES_TOP, node_count, capacity)
    send_rows = jnp.einsum(
        "pnc,plh->nlch",
        placing.astype(jnp.bfloat16),
        slot_hidden,
        preferred_element_type=jnp.float32,
    )
    send_rows = send_rows.astype(jnp.bfloat16).reshape(
        node_count * lane_count, capacity, hidden_width
    )
    send_weights = jnp.einsum(
        "pnc,pl->nlc", placing.astype(jnp.float32), slot_weights, precision=lax.Precision.HIGHEST
    )
    send_weights = send_weights.astype(jnp.bfloat16).reshape(node_count * lane_count, capacity, 1)
    received = lax.all_to_all(send_rows, ("node", "lane"), split_axis=0, concat_axis=0, tiled=True)
    weights = lax.all_to_all(
        send_weights, ("node", "lane"), split_axis=0, concat_axis=0, tiled=True
    )
    sources = received.shape[0]
    items = received.shape[1]
    output = jnp.dot(
        received.reshape(-1, hidden_width), down_matrix, preferred_element_type=jnp.float32
    )
    output = output.reshape(sources, items, width) * weights.astype(jnp.float32)
    returned = lax.all_to_all(output, ("node", "lane"), split_axis=0, concat_axis=0, tiled=True)
    returned = jnp.sum(returned.reshape(node_count, lane_count, capacity, width), axis=1)
    gathered_rows = returned.reshape(node_count * capacity, width)[target]
    routed = jnp.sum(gathered_rows.reshape(row_count, NODES_TOP, width), axis=1)
    moe_out = routed.astype(jnp.bfloat16)
    context = attend(query_latent, query_rope, cache_latent, cache_rope, cache_lengths)
    return (moe_out, context)


def solution(mesh):
    placed = (
        P(("groups", "node", "lane"), None, None),
        P(("groups", "node", "lane"), None),
        P(("groups", "node", "lane"), None),
        P(("groups", "node", "lane"), None),
        P(("node", "lane"), None, None),
        P(("groups", "node", "lane"), None, None),
        P(("groups", "node", "lane"), None),
        P(("groups", "node", "lane"), None, None),
        P(("groups", "node", "lane"), None, None),
        P(("groups", "node", "lane")),
    )
    return jax.shard_map(
        local,
        mesh=mesh,
        in_specs=placed,
        out_specs=(P(("groups", "node", "lane"), None), P(("groups", "node", "lane"), None, None)),
        check_vma=False,
    )
```

profile of v0, /device:TPU:13, one launch (start us, length us, event | category | flops | bytes accessed | tf_op | source)
XLA Modules:
  0.0 87.4 jit_solution(6203694291598042672)
XLA Ops:
  0.6 0.0 copy-start
  0.6 0.8 convert_reduce_fusion
  1.4 0.8 copy.52
  2.2 0.1 copy.56
  2.3 0.1 copy.58
  2.4 0.1 copy.59
  2.5 0.1 reshape.137
  2.6 0.0 copy-start.6
  2.6 0.0 copy-start.5
  2.6 0.0 copy-start.2
  2.6 0.8 gather_fusion.1
  3.4 0.1 reshape.140
  3.5 0.1 eq.59
  3.6 0.0 copy-done.6
  3.6 0.1 copy.51
  3.7 0.0 copy-done.5
  3.7 0.1 copy.67
  3.8 0.1 fusion.13
  4.0 0.1 reshape.121
  4.0 0.4 convolution_convert_fusion.3
  4.5 0.6 copy.63
  5.1 6.6 %all-to-all-start.1 = ((bf16[16,8,1]{1,2,0:T(2,128)(2,1)}), bf16[16,8,1]{1,2,0:T(2,128)(2,1)S(1)}, u32[]{:S(2)}, u32[]{:S(2)}) async-start(bf16[16,8,1]{1,2,0:T(2,128)(2,1)} %copy.63), calls=%async_computation.1 | async-start | bytes 16384 | tf_op jit(solution)/shard_map/all_to_all | solution.py:100
  11.6 0.0 copy-done.2
  11.6 0.2 convolution_convert_fusion.2
  11.8 0.1 reshape.118
  12.0 0.3 fusion.9
  12.2 0.7 copy.61
  13.0 2.4 %all-to-all-done.1 = bf16[16,8,1]{1,2,0:T(2,128)(2,1)S(1)} async-done(((bf16[16,8,1]{1,2,0:T(2,128)(2,1)}), bf16[16,8,1]{1,2,0:T(2,128)(2,1)S(1)}, u32[]{:S(2)}, u32[]{:S(2)}) %all-to-all-start.1) | async-done | bytes 288 | tf_op jit(solution)/shard_map/all_to_all | solution.py:100
  15.4 6.1 %all-to-all-start = ((bf16[16,8,1024]{2,1,0:T(8,128)(2,1)}), bf16[16,8,1024]{2,1,0:T(8,128)(2,1)S(1)}, u32[]{:S(2)}, u32[]{:S(2)}) async-start(bf16[16,8,1024]{2,1,0:T(8,128)(2,1)} %bitcast.4), calls=%async_computation | async-start | bytes 524288 | tf_op jit(solution)/shard_map/all_to_all | solution.py:99
  21.4 0.1 copy.64
  21.5 0.1 copy.65
  21.6 7.8 %all-to-all-done = bf16[16,8,1024]{2,1,0:T(8,128)(2,1)S(1)} async-done(((bf16[16,8,1024]{2,1,0:T(8,128)(2,1)}), bf16[16,8,1024]{2,1,0:T(8,128)(2,1)S(1)}, u32[]{:S(2)}, u32[]{:S(2)}) %all-to-all-start) | async-done | bytes 262176 | tf_op jit(solution)/shard_map/all_to_all | solution.py:99
  29.4 5.4 %fusion.3 = f32[16,8,3584]{2,1,0:T(8,128)} fusion(bf16[16,8,1024]{2,1,0:T(8,128)(2,1)S(1)} %all-to-all-done, bf16[1,1024,3584]{2,1,0:T(8,128)(2,1)} %param.14, f32[16,8]{1,0:T(8,128)S(1)} %copy.65), kind=kOutput, calls=%fused_computation.5 | convolution fusion | flops 939982848 | bytes 9437696 | tf_op jit(solution)/shard_map/dot_general | solution.py:105
  34.8 0.0 copy-start.4
  34.8 0.0 copy-start.7
  34.8 0.0 copy-start.1
  34.8 6.5 %all-to-all-start.2 = ((f32[16,8,3584]{2,1,0:T(8,128)}), f32[16,8,3584]{2,1,0:T(8,128)}, u32[]{:S(2)}, u32[]{:S(2)}) async-start(f32[16,8,3584]{2,1,0:T(8,128)} %fusion.3), calls=%async_computation.2 | async-start | bytes 3670016 | tf_op jit(solution)/shard_map/all_to_all | solution.py:109
  41.4 0.0 copy-start.3
  41.4 0.1 reshape.125
  41.5 0.0 copy-done.4
  41.5 0.2 reshape.127
  41.7 0.0 copy-done.7
  41.7 0.1 iota_compare_fusion.4
  41.8 0.0 copy-done
  41.8 0.0 copy-done.1
  41.8 0.5 fusion.26
  42.2 0.0 copy-done.3
  42.3 0.2 fusion.8
  42.5 0.2 fusion.25
  42.7 1.8 %convolution_convert_fusion = bf16[8,64,512]{2,1,0:T(8,128)(2,1)} fusion(bf16[8,128,512]{2,1,0:T(8,128)(2,1)S(1)} %copy-done, f32[8,64]{1,0:T(8,128)S(1)} %fusion.25, f32[8,64,128]{2,1,0:T(8,128)S(1)} %fusion.8), kind=kOutput, calls=%fused_computation.7 | convolution fusion | flops 67568256 | bytes 1837056 | tf_op jit(solution)/shard_map/rhc,rcl->rhl/dot_general | solution.py:30
  44.5 38.8 %all-to-all-done.2 = f32[16,8,3584]{2,1,0:T(8,128)} async-done(((f32[16,8,3584]{2,1,0:T(8,128)}), f32[16,8,3584]{2,1,0:T(8,128)}, u32[]{:S(2)}, u32[]{:S(2)}) %all-to-all-start.2) | async-done | bytes 1835040 | tf_op jit(solution)/shard_map/all_to_all | solution.py:109
  83.3 1.7 %bitcast_reduce_fusion = f32[8,8,3584]{2,1,0:T(8,128)S(1)} fusion(f32[16,8,3584]{2,1,0:T(8,128)} %all-to-all-done.2), kind=kLoop, calls=%fused_computation.6 | loop fusion | flops 229376 | bytes 2752512 | tf_op jit(solution)/shard_map/reduce_sum | solution.py:110
  85.0 0.9 %gather_fusion = f32[64,3584]{1,0:T(8,128)S(1)} fusion(f32[64,3584]{1,0:T(8,128)S(1)} %bitcast.45, s32[1024]{0:T(1024)S(1)} %pad_clamp_fusion), kind=kCustom, calls=%fused_computation | custom fusion | bytes 1835264 | tf_op jit(solution)/shard_map/gather | solution.py:111
  85.9 0.3 reshape.126
  86.2 1.2 %reduce_sum.48 = bf16[16,3584]{1,0:T(8,128)(2,1)} reduce(f32[16,4,3584]{2,1,0:T(4,128)S(1)} %reshape.126, f32[]{:T(128)} %constant.15.clone.1), dimensions={1}, to_apply=%region_4.5 | reduce | flops 172032 | bytes 1032196 | tf_op jit(solution)/shard_map/reduce_sum | solution.py:112
  (11 shorter events, 0.1 us)
Async XLA Ops:
  0.6 41.1 %copy-start = (bf16[8,128,512]{2,1,0:T(8,128)(2,1)S(1)}, bf16[8,128,512]{2,1,0:T(8,128)(2,1)}, u32[]{:S(2)}) copy-start(bf16[8,128,512]{2,1,0:T(8,128)(2,1)} %param.17) | copy-start | bytes 3145732
  2.6 1.0 %copy-start.6 = (s32[16,8]{0,1:T(8,128)S(1)}, s32[16,8]{0,1:T(8,128)}, u32[]{:S(2)}) copy-start(s32[16,8]{0,1:T(8,128)} %param.13) | copy-start | bytes 1540
  2.6 1.1 %copy-start.5 = (f32[16,8]{0,1:T(8,128)S(1)}, f32[16,8]{0,1:T(8,128)}, u32[]{:S(2)}) copy-start(f32[16,8]{0,1:T(8,128)} %param.11) | copy-start | bytes 1540
  2.6 9.0 %copy-start.2 = (bf16[16,8,1024]{2,1,0:T(8,128)(2,1)S(1)}, bf16[16,8,1024]{2,1,0:T(8,128)(2,1)}, u32[]{:S(2)}) copy-start(bf16[16,8,1024]{2,1,0:T(8,128)(2,1)} %param.10) | copy-start | bytes 786436
  5.1 10.3 %all-to-all-start.1 = ((bf16[16,8,1]{1,2,0:T(2,128)(2,1)}), bf16[16,8,1]{1,2,0:T(2,128)(2,1)S(1)}, u32[]{:S(2)}, u32[]{:S(2)}) async-start(bf16[16,8,1]{1,2,0:T(2,128)(2,1)} %copy.63), calls=%async_computation.1 | async-start | bytes 16384 | tf_op jit(solution)/shard_map/all_to_all | solution.py:100
  15.4 14.0 %all-to-all-start = ((bf16[16,8,1024]{2,1,0:T(8,128)(2,1)}), bf16[16,8,1024]{2,1,0:T(8,128)(2,1)S(1)}, u32[]{:S(2)}, u32[]{:S(2)}) async-start(bf16[16,8,1024]{2,1,0:T(8,128)(2,1)} %bitcast.4), calls=%async_computation | async-start | bytes 524288 | tf_op jit(solution)/shard_map/all_to_all | solution.py:99
  34.8 6.6 %copy-start.4 = (bf16[8,4096]{1,0:T(8,128)(2,1)S(1)}, bf16[8,4096]{1,0:T(8,128)(2,1)}, u32[]{:S(2)}) copy-start(bf16[8,4096]{1,0:T(8,128)(2,1)} %param.16) | copy-start | bytes 196612
  34.8 6.8 %copy-start.7 = (s32[8]{0:T(128)S(1)}, s32[8]{0:T(128)}, u32[]{:S(2)}) copy-start(s32[8]{0:T(128)} %param.19) | copy-start | bytes 100
  34.8 6.9 %copy-start.1 = (bf16[8,64,512]{2,1,0:T(8,128)(2,1)S(1)}, bf16[8,64,512]{2,1,0:T(8,128)(2,1)}, u32[]{:S(2)}) copy-start(bf16[8,64,512]{2,1,0:T(8,128)(2,1)} %param.15) | copy-start | bytes 1572868
  34.8 48.4 %all-to-all-start.2 = ((f32[16,8,3584]{2,1,0:T(8,128)}), f32[16,8,3584]{2,1,0:T(8,128)}, u32[]{:S(2)}, u32[]{:S(2)}) async-start(f32[16,8,3584]{2,1,0:T(8,128)} %fusion.3), calls=%async_computation.2 | async-start | bytes 3670016 | tf_op jit(solution)/shard_map/all_to_all | solution.py:109
  41.4 0.9 %copy-start.3 = (bf16[8,64,128]{2,1,0:T(8,128)(2,1)S(1)}, bf16[8,64,128]{2,1,0:T(8,128)(2,1)}, u32[]{:S(2)}) copy-start(bf16[8,64,128]{2,1,0:T(8,128)(2,1)} %param.18) | copy-start | bytes 393220
where the time goes:
time: 87.8 us; the launch traced here: 87.4 us
  waiting for transfers between devices  49 us (56%)
  starting transfers between devices  19.1 us (22%)
  matrix products  8.94 us (10%)
  local copies, waits for them, and re-layouts  5.39 us (6%)
  other arithmetic  4.13 us (5%)
    all_to_all x1, waiting for transfers between devices, local(): lax.all_to_all(output, ('node', 'lane'), split_axis=0, concat_axis=0, til...  38.8 us
    all_to_all x1, waiting for transfers between devices, local(): lax.all_to_all(send_rows, ('node', 'lane'), split_axis=0, concat_axis=0,...  7.81 us
    all_to_all x1, starting transfers between devices, local(): lax.all_to_all(send_weights, ('node', 'lane'), split_axis=0, concat_axis=...  6.55 us
    all_to_all x1, starting transfers between devices, local(): lax.all_to_all(output, ('node', 'lane'), split_axis=0, concat_axis=0, til...  6.52 us
    all_to_all x1, starting transfers between devices, local(): lax.all_to_all(send_rows, ('node', 'lane'), split_axis=0, concat_axis=0,...  6.06 us
    dot_general x1, matrix products, local(): jnp.dot(received.reshape(-1, hidden_width), down_matrix, preferred_elemen...  5.45 us
    all_to_all x1, waiting for transfers between devices, local(): lax.all_to_all(send_weights, ('node', 'lane'), split_axis=0, concat_axis=...  2.4 us
    dot_general x1, matrix products, attend(): jnp.einsum('rhc,rcl->rhl', probs, cache_latent, preferred_element_type=jn...  1.82 us
  transfers between devices with their start and end apart: 3, of which 3 were waited for; matrix products, arithmetic and copies ran while one was open for 5% of the time, Pallas kernels for 0%

commit v1 on v0

v1 whole, which is shorter than its diff:
```python
import functools

import jax
import jax.numpy as jnp
from jax import lax
from jax.experimental import pallas as pl
from jax.experimental.pallas import tpu as pltpu
from jax.sharding import PartitionSpec as P

NODES_TOP = 4


score_scale = 192.0 ** (-0.5)
route_scale = 2.5


def attend(query_latent, query_rope, cache_latent, cache_rope, cache_lengths):
    row_count, head_count, latent_width = query_latent.shape
    rope_width = cache_rope.shape[1]
    scores = jnp.einsum(
        "rhl,rcl->rhc", query_latent, cache_latent, preferred_element_type=jnp.float32
    )
    rope_query = query_rope.reshape(row_count, head_count, rope_width)
    scores = scores + jnp.einsum(
        "rhp,rpc->rhc", rope_query, cache_rope, preferred_element_type=jnp.float32
    )
    scores = scores * score_scale
    position = jnp.arange(cache_latent.shape[1], dtype=jnp.int32)
    valid = position[None, None, :] < cache_lengths[:, None, None]
    scores = jnp.where(valid, scores, -jnp.inf)
    highest = jnp.max(scores, axis=-1, keepdims=True)
    expd = jnp.exp(scores - highest)
    probs = (expd / jnp.sum(expd, axis=-1, keepdims=True)).astype(jnp.bfloat16)
    context = jnp.einsum("rhc,rcl->rhl", probs, cache_latent, preferred_element_type=jnp.float32)
    return context.astype(jnp.bfloat16)


def iota(shape, dim):
    return lax.broadcasted_iota(jnp.int32, shape, dim)


def pack_kernel(
    node_count, lane_count, capacity, scores_ref, lists_ref, picks_ref, hidden_ref, send_ref, place_ref
):
    pick_count, row_count = scores_ref.shape
    items = pick_count * row_count
    slots = node_count * capacity
    hidden_width = hidden_ref.shape[1]
    me = lax.axis_index("lane")

    def exact(a, b):
        return jnp.dot(a.astype(jnp.bfloat16), b.astype(jnp.bfloat16), preferred_element_type=jnp.float32)

    scores = scores_ref[...]
    combine = route_scale * scores / jnp.sum(scores, axis=0, keepdims=True)
    combine = combine.astype(jnp.bfloat16).astype(jnp.float32)
    picks = picks_ref[...]
    lists = lists_ref[...]
    choice = picks // lane_count
    lane = lax.rem(picks - choice * lane_count - me + lane_count, lane_count)
    node = jnp.zeros_like(picks)
    nodes = iota((node_count, row_count), 0)
    member = jnp.zeros((node_count, row_count), jnp.float32)
    for j in range(lists.shape[0]):
        node = jnp.where(choice == j, lists[j : j + 1, :], node)
        member = jnp.where(nodes == lists[j : j + 1, :], 1.0, member)
    before = iota((row_count, row_count), 0) < iota((row_count, row_count), 1)
    earlier = exact(member, jnp.where(before, 1.0, 0.0))

    spread = iota((row_count, items), 1) // pick_count == iota((row_count, items), 0)
    spread = jnp.where(spread, 1.0, 0.0)
    own_pick = lax.rem(iota((pick_count, items), 1), pick_count) == iota((pick_count, items), 0)

    def flat(values):
        wide = exact(values.astype(jnp.float32), spread)
        return jnp.sum(jnp.where(own_pick, wide, 0.0), axis=0, keepdims=True)

    weight = flat(combine)
    node_flat = flat(node).astype(jnp.int32)
    lane_flat = flat(lane).astype(jnp.int32)
    earlier_wide = exact(earlier, spread)
    named = iota((node_count, items), 0) == node_flat
    slot_flat = jnp.sum(jnp.where(named, earlier_wide, 0.0), axis=0, keepdims=True).astype(jnp.int32)
    target = node_flat * capacity + slot_flat
    at = iota((slots, items), 0) == target
    hidden = hidden_ref[...]
    for q in range(lane_count):
        placing = jnp.where(at & (lane_flat == q), weight, 0.0).astype(jnp.bfloat16)
        part = jnp.dot(placing, hidden, preferred_element_type=jnp.float32)
        send_ref[:, q * hidden_width : (q + 1) * hidden_width] = part.astype(jnp.bfloat16)

    slot_node = iota((slots, node_count), 0) // capacity == iota((slots, node_count), 1)
    marked = jnp.where(member > 0.0, earlier, -1.0)
    marked = exact(jnp.where(slot_node, 1.0, 0.0), marked)
    number = lax.rem(iota((slots, row_count), 0), capacity).astype(jnp.float32)
    place_ref[...] = jnp.where(marked == number, 1.0, 0.0).astype(jnp.bfloat16)


def expert_kernel(received_ref, *refs):
    *weight_refs, out_ref = refs
    depth = weight_refs[0].shape[0]
    total = None
    for q, weight_ref in enumerate(weight_refs):
        part = jnp.dot(
            received_ref[:, q * depth : (q + 1) * depth], weight_ref[...], preferred_element_type=jnp.float32
        )
        total = part if total is None else total + part
    out_ref[...] = total.astype(jnp.bfloat16)


def sum_kernel(place_ref, returned_ref, out_ref):
    total = lax.dot_general(
        place_ref[...], returned_ref[...], (((0,), (0,)), ((), ())), preferred_element_type=jnp.float32
    )
    out_ref[...] = total.astype(jnp.bfloat16)


def local(
    expert_hidden,
    gate_scores,
    node_lists,
    expert_picks,
    routed_down,
    query_latent,
    query_rope,
    cache_latent,
    cache_rope,
    cache_lengths,
):
    node_count = lax.axis_size("node")
    lane_count = lax.axis_size("lane")
    row_count, pick_count, hidden_width = expert_hidden.shape
    width = routed_down.shape[2]
    capacity = max(
        2, min(row_count // 2, 2 * ((row_count * NODES_TOP + node_count - 1) // node_count))
    )
    slots = node_count * capacity
    down_matrix = routed_down[0]
    matrices = [down_matrix]
    for q in range(1, lane_count):
        matrices.append(
            lax.ppermute(
                down_matrix, "lane", [((i + q) % lane_count, i) for i in range(lane_count)]
            )
        )
    send, place = pl.pallas_call(
        functools.partial(pack_kernel, node_count, lane_count, capacity),
        out_shape=(
            jax.ShapeDtypeStruct((slots, lane_count * hidden_width), jnp.bfloat16),
            jax.ShapeDtypeStruct((slots, row_count), jnp.bfloat16),
        ),
        name="pack",
    )(gate_scores.T, node_lists.T, expert_picks.T, expert_hidden.reshape(-1, hidden_width))
    received = lax.all_to_all(
        send.reshape(node_count, capacity, -1), "node", split_axis=0, concat_axis=0, tiled=True
    ).reshape(slots, -1)
    tile = 512
    output = pl.pallas_call(
        expert_kernel,
        grid=(width // tile,),
        in_specs=[pl.BlockSpec((slots, lane_count * hidden_width), lambda i: (0, 0))]
        + [pl.BlockSpec((hidden_width, tile), lambda i: (0, i))] * lane_count,
        out_specs=pl.BlockSpec((slots, tile), lambda i: (0, i)),
        out_shape=jax.ShapeDtypeStruct((slots, width), jnp.bfloat16),
        compiler_params=pltpu.CompilerParams(vmem_limit_bytes=24 * 2**20),
        name="experts",
    )(received, *matrices)
    returned = lax.all_to_all(
        output.reshape(node_count, capacity, width), "node", split_axis=0, concat_axis=0, tiled=True
    ).reshape(slots, width)
    moe_out = pl.pallas_call(
        sum_kernel,
        out_shape=jax.ShapeDtypeStruct((row_count, width), jnp.bfloat16),
        name="sum",
    )(place, returned)
    context = attend(query_latent, query_rope, cache_latent, cache_rope, cache_lengths)
    return (moe_out, context)


def solution(mesh):
    placed = (
        P(("groups", "node", "lane"), None, None),
        P(("groups", "node", "lane"), None),
        P(("groups", "node", "lane"), None),
        P(("groups", "node", "lane"), None),
        P(("node", "lane"), None, None),
        P(("groups", "node", "lane"), None, None),
        P(("groups", "node", "lane"), None),
        P(("groups", "node", "lane"), None, None),
        P(("groups", "node", "lane"), None, None),
        P(("groups", "node", "lane")),
    )
    return jax.shard_map(
        local,
        mesh=mesh,
        in_specs=placed,
        out_specs=(P(("groups", "node", "lane"), None), P(("groups", "node", "lane"), None, None)),
        check_vma=False,
    )
```

time: 87.8 us -> 50.8 us (0.58)
  the two profiles are of different devices: /device:TPU:13 before, /device:TPU:0 now
where the time goes in v1:
time: 50.8 us; the launch traced here: 50.2 us
  waiting for transfers between devices  17.9 us (35%)
  Pallas kernels  11.9 us (23%)
  starting transfers between devices  11 us (22%)
  local copies, waits for them, and re-layouts  4.9 us (10%)
  matrix products  3.5 us (7%)
  between operations  0.68 us (1%)
    all_to_all x1, waiting for transfers between devices, local(): lax.all_to_all(output.reshape(node_count, capacity, width), 'node', split...  10.9 us
    pallas_call x1, Pallas kernels, local(): pl.pallas_call(expert_kernel, grid=(width // tile,), in_specs=[pl.BlockSp...  7.84 us
    all_to_all x1, waiting for transfers between devices, local(): lax.all_to_all(send.reshape(node_count, capacity, -1), 'node', split_axis...  6.96 us
    all_to_all x1, starting transfers between devices, local(): lax.all_to_all(send.reshape(node_count, capacity, -1), 'node', split_axis...  6.92 us
    unnamed x10, local copies, waits for them, and re-layouts  3.87 us
    all_to_all x1, starting transfers between devices, local(): lax.all_to_all(output.reshape(node_count, capacity, width), 'node', split...  3.59 us
    pallas_call x1, Pallas kernels, local(): pl.pallas_call(functools.partial(pack_kernel, node_count, lane_count, cap...  2.15 us
    pallas_call x1, Pallas kernels, local(): pl.pallas_call(sum_kernel, out_shape=jax.ShapeDtypeStruct((row_count, wid...  1.91 us
  transfers between devices with their start and end apart: 3, of which 2 were waited for; matrix products, arithmetic and copies ran while one was open for 10% of the time, Pallas kernels for 4%

profile of v1, /device:TPU:0, one launch (start us, length us, event | category | flops | bytes accessed | tf_op | source)
XLA Modules:
  0.0 50.2 jit_solution(14768041148236066795)
XLA Ops:
  0.6 0.0 copy-start
  0.6 0.5 %collective-permute-start = (bf16[1024,3584]{1,0:T(8,128)(2,1)}, bf16[1024,3584]{1,0:T(8,128)(2,1)}, u32[]{:S(2)}, u32[]{:S(2)}) collective-permute-start(bf16[1024,3584]{1,0:T(8,128)(2,1)} %bitcast.16), channel_id=1, source_target_pairs={{1,0},{0,1},{3,2},{2,3},{5,4},{4,5},{7,6},{6,7},{9,8},{8,9},{11,10... | collective-permute-start | bytes 22020104 | tf_op jit(solution)/shard_map/ppermute | solution.py:142
  1.2 2.2 %pack.1 = (bf16[64,2048]{1,0:T(8,128)(2,1)}, bf16[64,16]{1,0:T(8,128)(2,1)}) custom-call(f32[8,16]{1,0:T(8,128)} %bitcast.22, s32[4,16]{1,0:T(4,128)} %bitcast.24, s32[8,16]{1,0:T(8,128)} %bitcast.23, bf16[128,1024]{1,0:T(8,128)(2,1)} %bitcast.20), custom_call_target="tpu_custom_call" | custom-call | tf_op jit(solution)/shard_map/pack/pallas_call | solution.py:146
  3.3 6.9 %all-to-all-start = ((bf16[8,8,2048]{2,1,0:T(8,128)(2,1)}), bf16[8,8,2048]{2,1,0:T(8,128)(2,1)S(1)}, u32[]{:S(2)}, u32[]{:S(2)}) async-start(bf16[8,8,2048]{2,1,0:T(8,128)(2,1)} %bitcast.21), calls=%async_computation | async-start | bytes 524288 | tf_op jit(solution)/shard_map/all_to_all | solution.py:154
  10.2 1.0 %reshape.50 = bf16[8,64,64]{2,1,0:T(8,128)(2,1)S(1)} reshape(bf16[8,4096]{1,0:T(8,128)(2,1)} %param.16) | data formatting | bytes 131072 | tf_op jit(solution)/shard_map/reshape | solution.py:23
  11.3 0.0 copy-done
  11.3 1.5 %fusion.8 = f32[8,64,128]{2,1,0:T(8,128)S(1)} fusion(bf16[8,64,512]{2,1,0:T(8,128)(2,1)} %param.15, bf16[8,128,512]{2,1,0:T(8,128)(2,1)S(1)} %copy-done), kind=kOutput, calls=%fused_computation.12 | convolution fusion | flops 67108864 | bytes 1835008 | tf_op jit(solution)/shard_map/rhl,rcl->rhc/dot_general | solution.py:20
  12.8 7.0 %all-to-all-done = bf16[8,8,2048]{2,1,0:T(8,128)(2,1)S(1)} async-done(((bf16[8,8,2048]{2,1,0:T(8,128)(2,1)}), bf16[8,8,2048]{2,1,0:T(8,128)(2,1)S(1)}, u32[]{:S(2)}, u32[]{:S(2)}) %all-to-all-start) | async-done | bytes 262176 | tf_op jit(solution)/shard_map/all_to_all | solution.py:154
  19.8 0.0 collective-permute-done.refs_1_
  19.8 0.0 copy-start.1
  19.8 3.1 %copy-done.1 = bf16[1,1024,3584]{2,1,0:T(8,128)(2,1)S(1)} copy-done((bf16[1,1024,3584]{2,1,0:T(8,128)(2,1)S(1)}, bf16[1,1024,3584]{2,1,0:T(8,128)(2,1)}, u32[]{:S(2)}) %copy-start.1) | copy-done | bytes 7340056
  22.8 0.0 copy-start.4
  22.8 0.0 copy-start.3
  22.8 7.8 %experts.1 = bf16[64,3584]{1,0:T(8,128)(2,1)} custom-call(bf16[64,2048]{1,0:T(8,128)(2,1)S(1)} %bitcast.18, bf16[1024,3584]{1,0:T(8,128)(2,1)S(1)} %bitcast.17, bf16[1024,3584]{1,0:T(8,128)(2,1)} %collective-permute-done.refs_1_), custom_call_target="tpu_custom_call" | custom-call | tf_op jit(solution)/shard_map/experts/pallas_call | solution.py:158
  30.7 3.6 %all-to-all-start.1 = ((bf16[8,8,3584]{2,1,0:T(8,128)(2,1)}), bf16[8,8,3584]{2,1,0:T(8,128)(2,1)S(1)}, u32[]{:S(2)}, u32[]{:S(2)}) async-start(bf16[8,8,3584]{2,1,0:T(8,128)(2,1)} %bitcast.7), calls=%async_computation.1 | async-start | bytes 917504 | tf_op jit(solution)/shard_map/all_to_all | solution.py:168
  34.3 0.0 copy-done.4
  34.3 0.1 iota_compare_fusion
  34.3 0.0 copy-done.3
  34.4 0.2 fusion.3
  34.5 0.2 fusion.7
  34.8 1.8 %convolution_convert_fusion = bf16[8,64,512]{2,1,0:T(8,128)(2,1)} fusion(bf16[8,128,512]{2,1,0:T(8,128)(2,1)S(1)} %copy-done, f32[8,64]{1,0:T(8,128)S(1)} %fusion.7, f32[8,64,128]{2,1,0:T(8,128)S(1)} %fusion.3), kind=kOutput, calls=%fused_computation.1 | convolution fusion | flops 67568256 | bytes 1837056 | tf_op jit(solution)/shard_map/rhc,rcl->rhl/dot_general | solution.py:34
  36.6 10.9 %all-to-all-done.1 = bf16[8,8,3584]{2,1,0:T(8,128)(2,1)S(1)} async-done(((bf16[8,8,3584]{2,1,0:T(8,128)(2,1)}), bf16[8,8,3584]{2,1,0:T(8,128)(2,1)S(1)}, u32[]{:S(2)}, u32[]{:S(2)}) %all-to-all-start.1) | async-done | bytes 458784 | tf_op jit(solution)/shard_map/all_to_all | solution.py:168
  47.5 0.0 copy-start.2
  47.5 0.8 %copy-done.2 = bf16[8,8,3584]{2,1,0:T(8,128)(2,1)} copy-done((bf16[8,8,3584]{2,1,0:T(8,128)(2,1)}, bf16[8,8,3584]{2,1,0:T(8,128)(2,1)S(1)}, u32[]{:S(2)}) %copy-start.2) | copy-done | bytes 458776
  48.3 1.9 %sum.1 = bf16[16,3584]{1,0:T(8,128)(2,1)} custom-call(bf16[64,16]{1,0:T(8,128)(2,1)} %get-tuple-element.4.place_ref, bf16[64,3584]{1,0:T(8,128)(2,1)} %bitcast.19), custom_call_target="tpu_custom_call" | custom-call | tf_op jit(solution)/shard_map/sum/pallas_call | solution.py:171
Async XLA Ops:
  0.6 10.6 %copy-start = (bf16[8,128,512]{2,1,0:T(8,128)(2,1)S(1)}, bf16[8,128,512]{2,1,0:T(8,128)(2,1)}, u32[]{:S(2)}) copy-start(bf16[8,128,512]{2,1,0:T(8,128)(2,1)} %param.17) | copy-start | bytes 3145732
  0.6 19.1 %collective-permute-start = (bf16[1024,3584]{1,0:T(8,128)(2,1)}, bf16[1024,3584]{1,0:T(8,128)(2,1)}, u32[]{:S(2)}, u32[]{:S(2)}) collective-permute-start(bf16[1024,3584]{1,0:T(8,128)(2,1)} %bitcast.16), channel_id=1, source_target_pairs={{1,0},{0,1},{3,2},{2,3},{5,4},{4,5},{7,6},{6,7},{9,8},{8,9},{11,10... | collective-permute-start | bytes 22020104 | tf_op jit(solution)/shard_map/ppermute | solution.py:142
  3.3 16.4 %all-to-all-start = ((bf16[8,8,2048]{2,1,0:T(8,128)(2,1)}), bf16[8,8,2048]{2,1,0:T(8,128)(2,1)S(1)}, u32[]{:S(2)}, u32[]{:S(2)}) async-start(bf16[8,8,2048]{2,1,0:T(8,128)(2,1)} %bitcast.21), calls=%async_computation | async-start | bytes 524288 | tf_op jit(solution)/shard_map/all_to_all | solution.py:154
  19.8 3.1 %copy-start.1 = (bf16[1,1024,3584]{2,1,0:T(8,128)(2,1)S(1)}, bf16[1,1024,3584]{2,1,0:T(8,128)(2,1)}, u32[]{:S(2)}) copy-start(bf16[1,1024,3584]{2,1,0:T(8,128)(2,1)} %param.14) | copy-start | bytes 22020100
  22.8 11.4 %copy-start.4 = (s32[8]{0:T(128)S(1)}, s32[8]{0:T(128)}, u32[]{:S(2)}) copy-start(s32[8]{0:T(128)} %param.19) | copy-start | bytes 100
  22.8 11.5 %copy-start.3 = (bf16[8,64,128]{2,1,0:T(8,128)(2,1)S(1)}, bf16[8,64,128]{2,1,0:T(8,128)(2,1)}, u32[]{:S(2)}) copy-start(bf16[8,64,128]{2,1,0:T(8,128)(2,1)} %param.18) | copy-start | bytes 393220
  30.7 16.8 %all-to-all-start.1 = ((bf16[8,8,3584]{2,1,0:T(8,128)(2,1)}), bf16[8,8,3584]{2,1,0:T(8,128)(2,1)S(1)}, u32[]{:S(2)}, u32[]{:S(2)}) async-start(bf16[8,8,3584]{2,1,0:T(8,128)(2,1)} %bitcast.7), calls=%async_computation.1 | async-start | bytes 917504 | tf_op jit(solution)/shard_map/all_to_all | solution.py:168
  47.5 0.8 %copy-start.2 = (bf16[8,8,3584]{2,1,0:T(8,128)(2,1)}, bf16[8,8,3584]{2,1,0:T(8,128)(2,1)S(1)}, u32[]{:S(2)}) copy-start(bf16[8,8,3584]{2,1,0:T(8,128)(2,1)S(1)} %all-to-all-done.1) | copy-start | bytes 1376260

commit v2 on v0

v2 whole, which is shorter than its diff:
```python
import functools

import jax
import jax.numpy as jnp
from jax import lax
from jax.experimental import pallas as pl
from jax.experimental.pallas import tpu as pltpu
from jax.sharding import PartitionSpec as P

NODES_TOP = 4
MIB = 2**20


score_scale = 192.0 ** (-0.5)
route_scale = 2.5


def attend_kernel(lengths_ref, latent_ref, rope_ref, keys_ref, rope_keys_ref, out_ref):
    for row in range(latent_ref.shape[0]):
        keys = keys_ref[row]
        scores = lax.dot_general(
            latent_ref[row], keys, (((1,), (1,)), ((), ())), preferred_element_type=jnp.float32
        )
        scores = scores + jnp.dot(rope_ref[row], rope_keys_ref[row], preferred_element_type=jnp.float32)
        scores = scores * score_scale
        valid = iota(scores.shape, 1) < lengths_ref[row]
        scores = jnp.where(valid, scores, -jnp.inf)
        expd = jnp.exp(scores - jnp.max(scores, axis=-1, keepdims=True))
        probs = (expd / jnp.sum(expd, axis=-1, keepdims=True)).astype(jnp.bfloat16)
        context = jnp.dot(probs, keys, preferred_element_type=jnp.float32)
        out_ref[row] = context.astype(jnp.bfloat16)


def attend(query_latent, query_rope, cache_latent, cache_rope, cache_lengths):
    row_count, head_count, latent_width = query_latent.shape
    rope_width, position_count = cache_rope.shape[1:]
    rope_query = query_rope.reshape(row_count, head_count, rope_width)
    products = head_count * position_count * (2 * latent_width + rope_width)
    return pl.pallas_call(
        attend_kernel,
        in_specs=[pl.BlockSpec(memory_space=pltpu.SMEM)] + [pl.BlockSpec(memory_space=pltpu.VMEM)] * 4,
        out_specs=pl.BlockSpec(memory_space=pltpu.VMEM),
        out_shape=jax.ShapeDtypeStruct(query_latent.shape, jnp.bfloat16),
        compiler_params=pltpu.CompilerParams(vmem_limit_bytes=8 * MIB),
        cost_estimate=pl.CostEstimate(
            flops=2 * row_count * products,
            bytes_accessed=2 * (2 * query_latent.size + query_rope.size + cache_latent.size + cache_rope.size),
            transcendentals=row_count * head_count * position_count,
        ),
        name="attend",
    )(cache_lengths, query_latent, rope_query, cache_latent, cache_rope)


def iota(shape, dim):
    return lax.broadcasted_iota(jnp.int32, shape, dim)


def exact(a, b):
    return jnp.dot(a.astype(jnp.bfloat16), b.astype(jnp.bfloat16), preferred_element_type=jnp.float32)


def meeting(node_count, a, b):
    return a ^ b if node_count & (node_count - 1) == 0 else (a + b) % node_count


def partner(node_count, a, number):
    return a ^ number if node_count & (node_count - 1) == 0 else (number - a) % node_count


def turn_of(node_count, lane, number):
    late = node_count - 1 - number
    turn = late // 2
    return jnp.where(late % 2 == (lane + turn) % 2, turn, -1)


def number_of(node_count, lane, turn):
    return node_count - 1 - 2 * turn - (lane + turn) % 2


def pack_kernel(node_count, lane_count, capacity, *refs):
    sources = [refs[4 * s : 4 * s + 4] for s in range(lane_count)]
    send_refs = refs[4 * lane_count : -1]
    place_ref = refs[-1]
    pick_count, row_count = sources[0][0].shape
    items = pick_count * row_count
    block = lane_count * capacity
    slots = len(send_refs) * block
    hidden_width = sources[0][3].shape[1]
    lane_here = lax.axis_index("lane")
    node_here = lax.axis_index("node")

    spread = iota((row_count, items), 1) // pick_count == iota((row_count, items), 0)
    spread = jnp.where(spread, 1.0, 0.0).astype(jnp.bfloat16)
    own_pick = lax.rem(iota((pick_count, items), 1), pick_count) == iota((pick_count, items), 0)
    before = iota((row_count, row_count), 0) < iota((row_count, row_count), 1)
    before = jnp.where(before, 1.0, 0.0)
    nodes = iota((node_count, row_count), 0)
    places = iota((slots, items), 0)

    def flat(values):
        wide = exact(values, spread)
        return jnp.sum(jnp.where(own_pick, wide, 0.0), axis=0, keepdims=True)

    parts = [None] * lane_count
    for s, (scores_ref, lists_ref, picks_ref, hidden_ref) in enumerate(sources):
        scores = scores_ref[...]
        combine = (route_scale * scores / jnp.sum(scores, axis=0, keepdims=True)).astype(jnp.bfloat16)
        picks = picks_ref[...]
        lists = lists_ref[...]
        choice = picks // lane_count
        order = lax.rem(picks - choice * lane_count - lane_here + lane_count, lane_count)
        node = jnp.zeros_like(picks)
        member = jnp.zeros((node_count, row_count), jnp.float32)
        for j in range(lists.shape[0]):
            node = jnp.where(choice == j, lists[j : j + 1, :], node)
            member = jnp.where(nodes == lists[j : j + 1, :], 1.0, member)
        earlier = exact(exact(member, before), spread)
        weight = flat(combine)
        node_and_order = flat((node * lane_count + order).astype(jnp.float32)).astype(jnp.int32)
        node_flat = node_and_order // lane_count
        order_flat = node_and_order - node_flat * lane_count
        named = iota((node_count, items), 0) == node_flat
        slot = jnp.sum(jnp.where(named, earlier, 0.0), axis=0, keepdims=True).astype(jnp.int32)
        turn = turn_of(node_count, lane_here, meeting(node_count, node_here, node_flat))
        target = jnp.where(turn >= 0, (turn * lane_count + s) * capacity + slot, -1)
        at = places == target
        hidden = hidden_ref[...]
        for q in range(lane_count):
            placing = jnp.where(at & (order_flat == q), weight, 0.0).astype(jnp.bfloat16)
            part = jnp.dot(placing, hidden, preferred_element_type=jnp.float32)
            parts[q] = part if parts[q] is None else parts[q] + part
        marks = lax.dot_general(
            jnp.where(at, 1.0, 0.0).astype(jnp.bfloat16),
            spread,
            (((1,), (1,)), ((), ())),
            preferred_element_type=jnp.float32,
        )
        place_ref[:, s * row_count : (s + 1) * row_count] = jnp.where(marks > 0.0, 1.0, 0.0)
    for q in range(lane_count):
        columns = slice(q * hidden_width, (q + 1) * hidden_width)
        for turn, send_ref in enumerate(send_refs):
            send_ref[:, columns] = parts[q][turn * block : (turn + 1) * block].astype(jnp.bfloat16)


def fetch_kernel(matrix_ref, out_ref, sem):
    copy = pltpu.make_async_copy(matrix_ref, out_ref, sem)
    copy.start()
    copy.wait()


def expert_kernel(turns, tile, *refs):
    received_refs, refs = refs[:turns], refs[turns:]
    out_refs, refs = refs[-turns - 1 : -1], refs[: -turns - 1] + refs[-1:]
    *weight_refs, rows_ref = refs
    depth, width = weight_refs[0].shape
    block = received_refs[0].shape[0]
    for turn, received_ref in enumerate(received_refs):
        rows_ref[turn * block : (turn + 1) * block, :] = received_ref[...]

    @pl.loop(0, width // tile)
    def _(i):
        columns = pl.ds(pl.multiple_of(i * tile, tile), tile)
        total = None
        for q, weight_ref in enumerate(weight_refs):
            part = jnp.dot(
                rows_ref[:, q * depth : (q + 1) * depth],
                weight_ref[:, columns],
                preferred_element_type=jnp.float32,
            )
            total = part if total is None else total + part
        total = total.astype(jnp.bfloat16)
        for turn, out_ref in enumerate(out_refs):
            out_ref[:, columns] = total[turn * block : (turn + 1) * block]


def sum_kernel(place_ref, *refs):
    *returned_refs, own_ref, other_ref, all_ref = refs
    block = returned_refs[0].shape[0]
    rows = own_ref.shape[0]
    for turn, returned_ref in enumerate(returned_refs):
        all_ref[turn * block : (turn + 1) * block, :] = returned_ref[...]
    total = lax.dot_general(
        place_ref[...].astype(jnp.bfloat16),
        all_ref[...],
        (((0,), (0,)), ((), ())),
        preferred_element_type=jnp.float32,
    )
    own_ref[...] = total[:rows]
    other_ref[...] = total[rows:]


def local(
    expert_hidden,
    gate_scores,
    node_lists,
    expert_picks,
    routed_down,
    query_latent,
    query_rope,
    cache_latent,
    cache_rope,
    cache_lengths,
):
    node_count = lax.axis_size("node")
    lane_count = lax.axis_size("lane")
    row_count, pick_count, hidden_width = expert_hidden.shape
    width = routed_down.shape[2]
    capacity = max(
        2, min(row_count // 2, 2 * ((row_count * NODES_TOP + node_count - 1) // node_count))
    )
    turns = node_count // lane_count
    block = lane_count * capacity
    slots = turns * block

    def other_core(value):
        return lax.ppermute(value, "lane", [(0, 1), (1, 0)])

    def meet(values):
        out = []
        for turn, value in enumerate(values):
            pairs = []
            for node in range(node_count):
                for lane in range(lane_count):
                    there = partner(node_count, node, number_of(node_count, lane, turn))
                    pairs.append((node * lane_count + lane, there * lane_count + lane))
            out.append(lax.ppermute(value, ("node", "lane"), pairs))
        return out

    mine = [gate_scores.T, node_lists.T, expert_picks.T, expert_hidden.reshape(-1, hidden_width)]
    theirs = [other_core(value) for value in mine]
    down_matrix, *theirs = lax.optimization_barrier((routed_down[0], *theirs))
    other_matrix = other_core(down_matrix)
    *send, place = pl.pallas_call(
        functools.partial(pack_kernel, node_count, lane_count, capacity),
        out_shape=[jax.ShapeDtypeStruct((block, lane_count * hidden_width), jnp.bfloat16)] * turns
        + [jax.ShapeDtypeStruct((slots, lane_count * row_count), jnp.float32)],
        compiler_params=pltpu.CompilerParams(vmem_limit_bytes=8 * MIB),
        name="pack",
    )(*[pltpu.with_memory_space_constraint(value, pltpu.HBM) for value in mine], *theirs)
    received = meet(send)
    whole = pl.BlockSpec(memory_space=pltpu.VMEM)
    down_matrix, _ = lax.optimization_barrier((down_matrix, place))
    own_matrix = pl.pallas_call(
        fetch_kernel,
        in_specs=[pl.BlockSpec(memory_space=pltpu.HBM)],
        out_specs=whole,
        out_shape=pltpu.VMEM(down_matrix.shape, down_matrix.dtype),
        scratch_shapes=[pltpu.SemaphoreType.DMA],
        compiler_params=pltpu.CompilerParams(vmem_limit_bytes=MIB),
        cost_estimate=pl.CostEstimate(flops=0, bytes_accessed=4 * down_matrix.size, transcendentals=0),
        name="fetch",
    )(pltpu.with_memory_space_constraint(down_matrix, pltpu.HBM))
    output = pl.pallas_call(
        functools.partial(expert_kernel, turns, 512),
        in_specs=[whole] * (turns + lane_count),
        out_specs=[whole] * turns,
        out_shape=[jax.ShapeDtypeStruct((block, width), jnp.bfloat16)] * turns,
        scratch_shapes=[pltpu.VMEM((slots, lane_count * hidden_width), jnp.bfloat16)],
        compiler_params=pltpu.CompilerParams(vmem_limit_bytes=24 * MIB),
        name="experts",
    )(*received, *[pltpu.with_memory_space_constraint(m, pltpu.VMEM) for m in (own_matrix, other_matrix)])
    returned = meet(output)
    query_latent, query_rope, cache_latent, cache_rope, cache_lengths, _ = lax.optimization_barrier(
        (query_latent, query_rope, cache_latent, cache_rope, cache_lengths, output[0])
    )
    context = attend(query_latent, query_rope, cache_latent, cache_rope, cache_lengths)
    *returned, context = lax.optimization_barrier((*returned, context))
    own, other = pl.pallas_call(
        sum_kernel,
        out_shape=[jax.ShapeDtypeStruct((row_count, width), jnp.float32)] * 2,
        scratch_shapes=[pltpu.VMEM((slots, width), jnp.bfloat16)],
        compiler_params=pltpu.CompilerParams(vmem_limit_bytes=8 * MIB),
        name="sum",
    )(place, *returned)
    moe_out = (own + other_core(other)).astype(jnp.bfloat16)
    return (moe_out, context)


def solution(mesh):
    placed = (
        P(("groups", "node", "lane"), None, None),
        P(("groups", "node", "lane"), None),
        P(("groups", "node", "lane"), None),
        P(("groups", "node", "lane"), None),
        P(("node", "lane"), None, None),
        P(("groups", "node", "lane"), None, None),
        P(("groups", "node", "lane"), None),
        P(("groups", "node", "lane"), None, None),
        P(("groups", "node", "lane"), None, None),
        P(("groups", "node", "lane")),
    )
    return jax.shard_map(
        local,
        mesh=mesh,
        in_specs=placed,
        out_specs=(P(("groups", "node", "lane"), None), P(("groups", "node", "lane"), None, None)),
        check_vma=False,
    )
```

time: 87.8 us -> 36.6 us (0.42)
  the two profiles are of different devices: /device:TPU:13 before, /device:TPU:0 now
where the time goes in v2:
time: 36.6 us; the launch traced here: 36.4 us
  starting transfers between devices  14.7 us (40%)
  Pallas kernels  12.7 us (35%)
  waiting for transfers between devices  7.36 us (20%)
  between operations  0.78 us (2%)
  other arithmetic  0.67 us (2%)
    ppermute x8, starting transfers between devices, meet(): out.append(lax.ppermute(value, ('node', 'lane'), pairs))  13.3 us
    ppermute x8, waiting for transfers between devices, meet(): out.append(lax.ppermute(value, ('node', 'lane'), pairs))  4.59 us
    pallas_call x1, Pallas kernels, attend(): pl.pallas_call(attend_kernel, in_specs=[pl.BlockSpec(memory_space=pltpu.S...  4.22 us
    pallas_call x1, Pallas kernels, local(): pl.pallas_call(functools.partial(expert_kernel, turns, 512), in_specs=[wh...  3.37 us
    pallas_call x1, Pallas kernels, local(): pl.pallas_call(fetch_kernel, in_specs=[pl.BlockSpec(memory_space=pltpu.HB...  3.09 us
    ppermute x6, waiting for transfers between devices, other_core(): return lax.ppermute(value, 'lane', [(0, 1), (1, 0)])  2.77 us
    pallas_call x1, Pallas kernels, local(): pl.pallas_call(functools.partial(pack_kernel, node_count, lane_count, cap...  1.76 us
    ppermute x6, starting transfers between devices, other_core(): return lax.ppermute(value, 'lane', [(0, 1), (1, 0)])  1.42 us
  transfers between devices with their start and end apart: 14, of which 5 were waited for; matrix products, arithmetic and copies ran while one was open for 0% of the time, Pallas kernels for 25%

profile of v2, /device:TPU:0, one launch (start us, length us, event | category | flops | bytes accessed | tf_op | source)
XLA Modules:
  0.0 36.4 jit_solution(16142309472254476404)
XLA Ops:
  0.6 0.5 %collective-permute-start.3 = (bf16[128,1024]{1,0:T(8,128)(2,1)}, bf16[128,1024]{1,0:T(8,128)(2,1)S(1)}, u32[]{:S(2)}, u32[]{:S(2)}) collective-permute-start(bf16[128,1024]{1,0:T(8,128)(2,1)} %bitcast.7), channel_id=1, source_target_pairs={{0,1},{1,0},{2,3},{3,2},{4,5},{5,4},{6,7},{7,6},{8,9},{9,8},{10,11... | collective-permute-start | bytes 786440 | tf_op jit(solution)/shard_map/ppermute | solution.py:216
  1.1 0.1 collective-permute-start
  1.2 0.4 %collective-permute-start.2 = (s32[8,16]{1,0:T(8,128)}, s32[8,16]{1,0:T(8,128)S(1)}, u32[]{:S(2)}, u32[]{:S(2)}) collective-permute-start(s32[8,16]{1,0:T(8,128)} %bitcast.11), channel_id=1, source_target_pairs={{0,1},{1,0},{2,3},{3,2},{4,5},{5,4},{6,7},{7,6},{8,9},{9,8},{10,11... | collective-permute-start | bytes 1544 | tf_op jit(solution)/shard_map/ppermute | solution.py:216
  1.7 0.1 collective-permute-start.1
  1.7 1.3 %collective-permute-done.1.refs_5_ = s32[4,16]{1,0:T(4,128)S(1)} collective-permute-done((s32[4,16]{1,0:T(4,128)}, s32[4,16]{1,0:T(4,128)S(1)}, u32[]{:S(2)}, u32[]{:S(2)}) %collective-permute-start.1) | collective-permute-done | bytes 288 | tf_op jit(solution)/shard_map/ppermute | solution.py:216
  3.0 0.0 collective-permute-done.refs_4_
  3.0 0.0 collective-permute-done.2.refs_6_
  3.0 0.0 collective-permute-done.3.refs_7_
  3.0 0.2 collective-permute-start.8
  3.3 1.8 %pack.1 = (bf16[16,2048]{1,0:T(8,128)(2,1)S(1)}, bf16[16,2048]{1,0:T(8,128)(2,1)S(1)}, bf16[16,2048]{1,0:T(8,128)(2,1)S(1)}, bf16[16,2048]{1,0:T(8,128)(2,1)S(1)}, f32[64,32]{1,0:T(8,128)S(1)}) custom-call(f32[8,16]{1,0:T(8,128)} %bitcast.10, s32[4,16]{1,0:T(4,128)} %bitcast.14, s32[8,16]{1,0:T(8,128)} %bitcast.12, bf16[128,1024]{1,0:T(8,128)(2,1)} %bitcast.8, ...), custom_call_target="tpu_custom_call" | custom-call | tf_op jit(solution)/shard_map/pack/pallas_call | solution.py:233
  5.0 5.9 %collective-permute-start.4 = (bf16[16,2048]{1,0:T(8,128)(2,1)S(1)}, bf16[16,2048]{1,0:T(8,128)(2,1)S(1)}, u32[]{:S(2)}, u32[]{:S(2)}) collective-permute-start(bf16[16,2048]{1,0:T(8,128)(2,1)S(1)} %get-tuple-element.34), channel_id=1, source_target_pairs={{0,14},{1,13},{2,12},{3,15},{4,10},{5,9},{6,8},{7,11},{8,6},{9,5},... | collective-permute-start | bytes 196616 | tf_op jit(solution)/shard_map/ppermute | solution.py:226
  10.9 0.0 collective-permute-start.5
  11.0 0.6 %collective-permute-start.6 = (bf16[16,2048]{1,0:T(8,128)(2,1)S(1)}, bf16[16,2048]{1,0:T(8,128)(2,1)S(1)}, u32[]{:S(2)}, u32[]{:S(2)}) collective-permute-start(bf16[16,2048]{1,0:T(8,128)(2,1)S(1)} %get-tuple-element.36), channel_id=1, source_target_pairs={{0,6},{1,5},{2,4},{3,7},{4,2},{5,1},{6,0},{7,3},{8,14},{9,13},{10,... | collective-permute-start | bytes 196616 | tf_op jit(solution)/shard_map/ppermute | solution.py:226
  11.6 0.7 %collective-permute-start.7 = (bf16[16,2048]{1,0:T(8,128)(2,1)S(1)}, bf16[16,2048]{1,0:T(8,128)(2,1)S(1)}, u32[]{:S(2)}, u32[]{:S(2)}) collective-permute-start(bf16[16,2048]{1,0:T(8,128)(2,1)S(1)} %get-tuple-element.37), channel_id=1, source_target_pairs={{0,0},{1,3},{2,2},{3,1},{4,4},{5,7},{6,6},{7,5},{8,8},{9,11},{10,1... | collective-permute-start | bytes 196616 | tf_op jit(solution)/shard_map/ppermute | solution.py:226
  12.3 3.1 %fetch.1.refs_4_ = bf16[1024,3584]{1,0:T(8,128)(2,1)S(1)} custom-call(bf16[1024,3584]{1,0:T(8,128)(2,1)} %bitcast.6), custom_call_target="tpu_custom_call" | custom-call | bytes 14680064 | tf_op jit(solution)/shard_map/fetch/pallas_call | solution.py:243
  15.4 0.0 copy-start.4
  15.4 0.0 copy-start
  15.4 0.0 copy-start.1
  15.4 0.0 copy-start.2
  15.4 0.0 copy-start.3
  15.4 0.0 collective-permute-done.4.refs_0_
  15.4 1.0 %collective-permute-done.5.refs_1_ = bf16[16,2048]{1,0:T(8,128)(2,1)S(1)} collective-permute-done((bf16[16,2048]{1,0:T(8,128)(2,1)S(1)}, bf16[16,2048]{1,0:T(8,128)(2,1)S(1)}, u32[]{:S(2)}, u32[]{:S(2)}) %collective-permute-start.5) | collective-permute-done | bytes 65568 | tf_op jit(solution)/shard_map/ppermute | solution.py:226
  16.5 0.8 %collective-permute-done.6.refs_2_ = bf16[16,2048]{1,0:T(8,128)(2,1)S(1)} collective-permute-done((bf16[16,2048]{1,0:T(8,128)(2,1)S(1)}, bf16[16,2048]{1,0:T(8,128)(2,1)S(1)}, u32[]{:S(2)}, u32[]{:S(2)}) %collective-permute-start.6) | collective-permute-done | bytes 65568 | tf_op jit(solution)/shard_map/ppermute | solution.py:226
  17.3 0.0 collective-permute-done.7.refs_3_
  17.3 0.0 collective-permute-done.8.refs_5_
  17.3 3.4 %experts.1 = (bf16[16,3584]{1,0:T(8,128)(2,1)S(1)}, bf16[16,3584]{1,0:T(8,128)(2,1)S(1)}, bf16[16,3584]{1,0:T(8,128)(2,1)S(1)}, bf16[16,3584]{1,0:T(8,128)(2,1)S(1)}) custom-call(bf16[16,2048]{1,0:T(8,128)(2,1)S(1)} %collective-permute-done.4.refs_0_, bf16[16,2048]{1,0:T(8,128)(2,1)S(1)} %collective-permute-done.5.refs_1_, ...), custom_call_target="tpu_custom_call" | custom-call | tf_op jit(solution)/shard_map/experts/pallas_call | solution.py:253
  20.7 1.9 %collective-permute-start.10 = (bf16[16,3584]{1,0:T(8,128)(2,1)S(1)}, bf16[16,3584]{1,0:T(8,128)(2,1)S(1)}, u32[]{:S(2)}, u32[]{:S(2)}) collective-permute-start(bf16[16,3584]{1,0:T(8,128)(2,1)S(1)} %get-tuple-element.41), channel_id=1, source_target_pairs={{0,8},{1,11},{2,10},{3,9},{4,12},{5,15},{6,14},{7,13},{8,0},{9,3},... | collective-permute-start | bytes 344072 | tf_op jit(solution)/shard_map/ppermute | solution.py:226
  22.6 2.1 %collective-permute-start.11 = (bf16[16,3584]{1,0:T(8,128)(2,1)S(1)}, bf16[16,3584]{1,0:T(8,128)(2,1)S(1)}, u32[]{:S(2)}, u32[]{:S(2)}) collective-permute-start(bf16[16,3584]{1,0:T(8,128)(2,1)S(1)} %get-tuple-element.42), channel_id=1, source_target_pairs={{0,6},{1,5},{2,4},{3,7},{4,2},{5,1},{6,0},{7,3},{8,14},{9,13},{10,... | collective-permute-start | bytes 344072 | tf_op jit(solution)/shard_map/ppermute | solution.py:226
  24.7 0.7 %collective-permute-start.12 = (bf16[16,3584]{1,0:T(8,128)(2,1)S(1)}, bf16[16,3584]{1,0:T(8,128)(2,1)S(1)}, u32[]{:S(2)}, u32[]{:S(2)}) collective-permute-start(bf16[16,3584]{1,0:T(8,128)(2,1)S(1)} %get-tuple-element.43), channel_id=1, source_target_pairs={{0,0},{1,3},{2,2},{3,1},{4,4},{5,7},{6,6},{7,5},{8,8},{9,11},{10,1... | collective-permute-start | bytes 344072 | tf_op jit(solution)/shard_map/ppermute | solution.py:226
  25.4 1.4 %collective-permute-start.9 = (bf16[16,3584]{1,0:T(8,128)(2,1)S(1)}, bf16[16,3584]{1,0:T(8,128)(2,1)S(1)}, u32[]{:S(2)}, u32[]{:S(2)}) collective-permute-start(bf16[16,3584]{1,0:T(8,128)(2,1)S(1)} %get-tuple-element.40), channel_id=1, source_target_pairs={{0,14},{1,13},{2,12},{3,15},{4,10},{5,9},{6,8},{7,11},{8,6},{9,5},... | collective-permute-start | bytes 344072 | tf_op jit(solution)/shard_map/ppermute | solution.py:226
  26.8 0.0 copy-done.4
  26.8 0.2 reshape.11.rope_ref
  26.9 0.0 copy-done
  27.0 0.0 copy-done.1
  27.0 0.0 copy-done.2
  27.0 0.0 copy-done.3
  27.0 4.2 %attend.1 = bf16[8,64,512]{2,1,0:T(8,128)(2,1)} custom-call(s32[8]{0:T(128)S(1)} %copy-done.3, bf16[8,64,512]{2,1,0:T(8,128)(2,1)S(1)} %copy-done.1, bf16[8,64,64]{2,1,0:T(8,128)(2,1)S(1)} %reshape.11.rope_ref, bf16[8,128,512]{2,1,0:T(8,128)(2,1)S(1)} %copy-done, bf16[8,64,128]{2,1,0:T(8,128)(2,1)S(1)} %copy-done.2), custom_call_target="tpu_custom_call" | custom-call | flops 142606336 | bytes 2293760 | tf_op jit(solution)/shard_map/attend/pallas_call | solution.py:39
  31.2 0.0 collective-permute-done.10.refs_1_
  31.2 0.0 collective-permute-done.11.refs_2_
  31.2 0.0 collective-permute-done.12.refs_3_
  31.2 2.7 %collective-permute-done.9.refs_0_ = bf16[16,3584]{1,0:T(8,128)(2,1)S(1)} collective-permute-done((bf16[16,3584]{1,0:T(8,128)(2,1)S(1)}, bf16[16,3584]{1,0:T(8,128)(2,1)S(1)}, u32[]{:S(2)}, u32[]{:S(2)}) %collective-permute-start.9) | collective-permute-done | bytes 114720 | tf_op jit(solution)/shard_map/ppermute | solution.py:226
  33.9 0.2 sum.1
  34.2 0.1 collective-permute-start.13
  34.2 1.5 %collective-permute-done.13 = f32[16,3584]{1,0:T(8,128)S(1)} collective-permute-done((f32[16,3584]{1,0:T(8,128)S(1)}, f32[16,3584]{1,0:T(8,128)S(1)}, u32[]{:S(2)}, u32[]{:S(2)}) %collective-permute-start.13) | collective-permute-done | bytes 229408 | tf_op jit(solution)/shard_map/ppermute | solution.py:216
  35.7 0.7 %add_convert_fusion = bf16[16,3584]{1,0:T(8,128)(2,1)} fusion(f32[16,3584]{1,0:T(8,128)S(1)} %get-tuple-element.53, f32[16,3584]{1,0:T(8,128)S(1)} %collective-permute-done.13), kind=kLoop, calls=%fused_computation | loop fusion | flops 114688 | bytes 573440 | tf_op jit(solution)/shard_map/convert_element_type | solution.py:275
Async XLA Ops:
  0.6 2.4 %collective-permute-start.3 = (bf16[128,1024]{1,0:T(8,128)(2,1)}, bf16[128,1024]{1,0:T(8,128)(2,1)S(1)}, u32[]{:S(2)}, u32[]{:S(2)}) collective-permute-start(bf16[128,1024]{1,0:T(8,128)(2,1)} %bitcast.7), channel_id=1, source_target_pairs={{0,1},{1,0},{2,3},{3,2},{4,5},{5,4},{6,7},{7,6},{8,9},{9,8},{10,11... | collective-permute-start | bytes 786440 | tf_op jit(solution)/shard_map/ppermute | solution.py:216
  1.1 1.9 %collective-permute-start = (f32[8,16]{1,0:T(8,128)}, f32[8,16]{1,0:T(8,128)S(1)}, u32[]{:S(2)}, u32[]{:S(2)}) collective-permute-start(f32[8,16]{1,0:T(8,128)} %bitcast.9), channel_id=1, source_target_pairs={{0,1},{1,0},{2,3},{3,2},{4,5},{5,4},{6,7},{7,6},{8,9},{9,8},{10,11... | collective-permute-start | bytes 1544 | tf_op jit(solution)/shard_map/ppermute | solution.py:216
  1.2 1.8 %collective-permute-start.2 = (s32[8,16]{1,0:T(8,128)}, s32[8,16]{1,0:T(8,128)S(1)}, u32[]{:S(2)}, u32[]{:S(2)}) collective-permute-start(s32[8,16]{1,0:T(8,128)} %bitcast.11), channel_id=1, source_target_pairs={{0,1},{1,0},{2,3},{3,2},{4,5},{5,4},{6,7},{7,6},{8,9},{9,8},{10,11... | collective-permute-start | bytes 1544 | tf_op jit(solution)/shard_map/ppermute | solution.py:216
  1.7 1.4 %collective-permute-start.1 = (s32[4,16]{1,0:T(4,128)}, s32[4,16]{1,0:T(4,128)S(1)}, u32[]{:S(2)}, u32[]{:S(2)}) collective-permute-start(s32[4,16]{1,0:T(4,128)} %bitcast.13), channel_id=1, source_target_pairs={{0,1},{1,0},{2,3},{3,2},{4,5},{5,4},{6,7},{7,6},{8,9},{9,8},{10,11... | collective-permute-start | bytes 776 | tf_op jit(solution)/shard_map/ppermute | solution.py:216
  3.0 14.3 %collective-permute-start.8 = (bf16[1024,3584]{1,0:T(8,128)(2,1)}, bf16[1024,3584]{1,0:T(8,128)(2,1)S(1)}, u32[]{:S(2)}, u32[]{:S(2)}) collective-permute-start(bf16[1024,3584]{1,0:T(8,128)(2,1)} %bitcast.5), channel_id=1, source_target_pairs={{0,1},{1,0},{2,3},{3,2},{4,5},{5,4},{6,7},{7,6},{8,9},{9,8},{10,11... | collective-permute-start | bytes 22020104 | tf_op jit(solution)/shard_map/ppermute | solution.py:216
  5.0 10.4 %collective-permute-start.4 = (bf16[16,2048]{1,0:T(8,128)(2,1)S(1)}, bf16[16,2048]{1,0:T(8,128)(2,1)S(1)}, u32[]{:S(2)}, u32[]{:S(2)}) collective-permute-start(bf16[16,2048]{1,0:T(8,128)(2,1)S(1)} %get-tuple-element.34), channel_id=1, source_target_pairs={{0,14},{1,13},{2,12},{3,15},{4,10},{5,9},{6,8},{7,11},{8,6},{9,5},... | collective-permute-start | bytes 196616 | tf_op jit(solution)/shard_map/ppermute | solution.py:226
  10.9 5.5 %collective-permute-start.5 = (bf16[16,2048]{1,0:T(8,128)(2,1)S(1)}, bf16[16,2048]{1,0:T(8,128)(2,1)S(1)}, u32[]{:S(2)}, u32[]{:S(2)}) collective-permute-start(bf16[16,2048]{1,0:T(8,128)(2,1)S(1)} %get-tuple-element.35), channel_id=1, source_target_pairs={{0,8},{1,11},{2,10},{3,9},{4,12},{5,15},{6,14},{7,13},{8,0},{9,3},... | collective-permute-start | bytes 196616 | tf_op jit(solution)/shard_map/ppermute | solution.py:226
  11.0 6.4 %collective-permute-start.6 = (bf16[16,2048]{1,0:T(8,128)(2,1)S(1)}, bf16[16,2048]{1,0:T(8,128)(2,1)S(1)}, u32[]{:S(2)}, u32[]{:S(2)}) collective-permute-start(bf16[16,2048]{1,0:T(8,128)(2,1)S(1)} %get-tuple-element.36), channel_id=1, source_target_pairs={{0,6},{1,5},{2,4},{3,7},{4,2},{5,1},{6,0},{7,3},{8,14},{9,13},{10,... | collective-permute-start | bytes 196616 | tf_op jit(solution)/shard_map/ppermute | solution.py:226
  11.6 5.7 %collective-permute-start.7 = (bf16[16,2048]{1,0:T(8,128)(2,1)S(1)}, bf16[16,2048]{1,0:T(8,128)(2,1)S(1)}, u32[]{:S(2)}, u32[]{:S(2)}) collective-permute-start(bf16[16,2048]{1,0:T(8,128)(2,1)S(1)} %get-tuple-element.37), channel_id=1, source_target_pairs={{0,0},{1,3},{2,2},{3,1},{4,4},{5,7},{6,6},{7,5},{8,8},{9,11},{10,1... | collective-permute-start | bytes 196616 | tf_op jit(solution)/shard_map/ppermute | solution.py:226
  15.4 11.4 %copy-start.4 = (bf16[8,4096]{1,0:T(8,128)(2,1)S(1)}, bf16[8,4096]{1,0:T(8,128)(2,1)}, u32[]{:S(2)}) copy-start(bf16[8,4096]{1,0:T(8,128)(2,1)} %param.16) | copy-start | bytes 196612
  15.4 11.6 %copy-start = (bf16[8,128,512]{2,1,0:T(8,128)(2,1)S(1)}, bf16[8,128,512]{2,1,0:T(8,128)(2,1)}, u32[]{:S(2)}) copy-start(bf16[8,128,512]{2,1,0:T(8,128)(2,1)} %keys_ref) | copy-start | bytes 3145732
  15.4 11.6 %copy-start.1 = (bf16[8,64,512]{2,1,0:T(8,128)(2,1)S(1)}, bf16[8,64,512]{2,1,0:T(8,128)(2,1)}, u32[]{:S(2)}) copy-start(bf16[8,64,512]{2,1,0:T(8,128)(2,1)} %latent_ref) | copy-start | bytes 1572868
  15.4 11.6 %copy-start.2 = (bf16[8,64,128]{2,1,0:T(8,128)(2,1)S(1)}, bf16[8,64,128]{2,1,0:T(8,128)(2,1)}, u32[]{:S(2)}) copy-start(bf16[8,64,128]{2,1,0:T(8,128)(2,1)} %rope_keys_ref) | copy-start | bytes 393220
  15.4 11.6 %copy-start.3 = (s32[8]{0:T(128)S(1)}, s32[8]{0:T(128)}, u32[]{:S(2)}) copy-start(s32[8]{0:T(128)} %lengths_ref) | copy-start | bytes 100
  20.7 10.5 %collective-permute-start.10 = (bf16[16,3584]{1,0:T(8,128)(2,1)S(1)}, bf16[16,3584]{1,0:T(8,128)(2,1)S(1)}, u32[]{:S(2)}, u32[]{:S(2)}) collective-permute-start(bf16[16,3584]{1,0:T(8,128)(2,1)S(1)} %get-tuple-element.41), channel_id=1, source_target_pairs={{0,8},{1,11},{2,10},{3,9},{4,12},{5,15},{6,14},{7,13},{8,0},{9,3},... | collective-permute-start | bytes 344072 | tf_op jit(solution)/shard_map/ppermute | solution.py:226
  22.6 8.6 %collective-permute-start.11 = (bf16[16,3584]{1,0:T(8,128)(2,1)S(1)}, bf16[16,3584]{1,0:T(8,128)(2,1)S(1)}, u32[]{:S(2)}, u32[]{:S(2)}) collective-permute-start(bf16[16,3584]{1,0:T(8,128)(2,1)S(1)} %get-tuple-element.42), channel_id=1, source_target_pairs={{0,6},{1,5},{2,4},{3,7},{4,2},{5,1},{6,0},{7,3},{8,14},{9,13},{10,... | collective-permute-start | bytes 344072 | tf_op jit(solution)/shard_map/ppermute | solution.py:226
  24.7 6.5 %collective-permute-start.12 = (bf16[16,3584]{1,0:T(8,128)(2,1)S(1)}, bf16[16,3584]{1,0:T(8,128)(2,1)S(1)}, u32[]{:S(2)}, u32[]{:S(2)}) collective-permute-start(bf16[16,3584]{1,0:T(8,128)(2,1)S(1)} %get-tuple-element.43), channel_id=1, source_target_pairs={{0,0},{1,3},{2,2},{3,1},{4,4},{5,7},{6,6},{7,5},{8,8},{9,11},{10,1... | collective-permute-start | bytes 344072 | tf_op jit(solution)/shard_map/ppermute | solution.py:226
  25.4 8.5 %collective-permute-start.9 = (bf16[16,3584]{1,0:T(8,128)(2,1)S(1)}, bf16[16,3584]{1,0:T(8,128)(2,1)S(1)}, u32[]{:S(2)}, u32[]{:S(2)}) collective-permute-start(bf16[16,3584]{1,0:T(8,128)(2,1)S(1)} %get-tuple-element.40), channel_id=1, source_target_pairs={{0,14},{1,13},{2,12},{3,15},{4,10},{5,9},{6,8},{7,11},{8,6},{9,5},... | collective-permute-start | bytes 344072 | tf_op jit(solution)/shard_map/ppermute | solution.py:226
  34.2 1.6 %collective-permute-start.13 = (f32[16,3584]{1,0:T(8,128)S(1)}, f32[16,3584]{1,0:T(8,128)S(1)}, u32[]{:S(2)}, u32[]{:S(2)}) collective-permute-start(f32[16,3584]{1,0:T(8,128)S(1)} %get-tuple-element.54), channel_id=1, source_target_pairs={{0,1},{1,0},{2,3},{3,2},{4,5},{5,4},{6,7},{7,6},{8,9},{9,8},{10,11... | collective-permute-start | bytes 688136 | tf_op jit(solution)/shard_map/ppermute | solution.py:216

commit v3 on v2

--- a/solution.py
+++ b/solution.py
@@ -9,6 +9,7 @@
 
 NODES_TOP = 4
 MIB = 2**20
+TILE = 512
 
 
 score_scale = 192.0 ** (-0.5)
@@ -16,18 +17,22 @@
 
 
 def attend_kernel(lengths_ref, latent_ref, rope_ref, keys_ref, rope_keys_ref, out_ref):
-    for row in range(latent_ref.shape[0]):
-        keys = keys_ref[row]
-        scores = lax.dot_general(
-            latent_ref[row], keys, (((1,), (1,)), ((), ())), preferred_element_type=jnp.float32
-        )
-        scores = scores + jnp.dot(rope_ref[row], rope_keys_ref[row], preferred_element_type=jnp.float32)
-        scores = scores * score_scale
-        valid = iota(scores.shape, 1) < lengths_ref[row]
-        scores = jnp.where(valid, scores, -jnp.inf)
-        expd = jnp.exp(scores - jnp.max(scores, axis=-1, keepdims=True))
-        probs = (expd / jnp.sum(expd, axis=-1, keepdims=True)).astype(jnp.bfloat16)
-        context = jnp.dot(probs, keys, preferred_element_type=jnp.float32)
+    row_count, head_count, _ = latent_ref.shape
+    scores = []
+    for row in range(row_count):
+        score = lax.dot_general(
+            latent_ref[row], keys_ref[row], (((1,), (1,)), ((), ())), preferred_element_type=jnp.float32
+        )
+        score = score + jnp.dot(rope_ref[row], rope_keys_ref[row], preferred_element_type=jnp.float32)
+        valid = iota(score.shape, 1) < lengths_ref[row]
+        scores.append(jnp.where(valid, score * score_scale, -jnp.inf))
+    scores = jnp.concatenate(scores, axis=0)
+    expd = jnp.exp(scores - jnp.max(scores, axis=-1, keepdims=True))
+    probs = (expd / jnp.sum(expd, axis=-1, keepdims=True)).astype(jnp.bfloat16)
+    for row in range(row_count):
+        context = jnp.dot(
+            probs[row * head_count : (row + 1) * head_count], keys_ref[row], preferred_element_type=jnp.float32
+        )
         out_ref[row] = context.astype(jnp.bfloat16)
 
 
@@ -67,14 +72,25 @@
     return a ^ number if node_count & (node_count - 1) == 0 else (number - a) % node_count
 
 
-def turn_of(node_count, lane, number):
-    late = node_count - 1 - number
-    turn = late // 2
-    return jnp.where(late % 2 == (lane + turn) % 2, turn, -1)
-
-
-def number_of(node_count, lane, turn):
-    return node_count - 1 - 2 * turn - (lane + turn) % 2
+def turn_of(node_count, lane_count, lane, number):
+    return jnp.where(number % lane_count == lane, (node_count - 1 - number) // lane_count, -1)
+
+
+def number_of(node_count, lane_count, lane, turn):
+    return node_count - lane_count * (turn + 1) + lane
+
+
+def load_kernel(*refs):
+    *refs, sems = refs
+    half = len(refs) // 2
+    copies = [
+        pltpu.make_async_copy(in_ref, out_ref, sems.at[i])
+        for i, (in_ref, out_ref) in enumerate(zip(refs[:half], refs[half:]))
+    ]
+    for copy in copies:
+        copy.start()
+    for copy in copies:
+        copy.wait()
 
 
 def pack_kernel(node_count, lane_count, capacity, *refs):
@@ -121,7 +137,7 @@
         order_flat = node_and_order - node_flat * lane_count
         named = iota((node_count, items), 0) == node_flat
         slot = jnp.sum(jnp.where(named, earlier, 0.0), axis=0, keepdims=True).astype(jnp.int32)
-        turn = turn_of(node_count, lane_here, meeting(node_count, node_here, node_flat))
+        turn = turn_of(node_count, lane_count, lane_here, meeting(node_count, node_here, node_flat))
         target = jnp.where(turn >= 0, (turn * lane_count + s) * capacity + slot, -1)
         at = places == target
         hidden = hidden_ref[...]
@@ -143,32 +159,42 @@
 
 
 def fetch_kernel(matrix_ref, out_ref, sem):
-    copy = pltpu.make_async_copy(matrix_ref, out_ref, sem)
+    copy = pltpu.make_async_copy(matrix_ref.at[pl.ds(0, out_ref.shape[0])], out_ref, sem)
     copy.start()
     copy.wait()
 
 
-def expert_kernel(turns, tile, *refs):
-    received_refs, refs = refs[:turns], refs[turns:]
-    out_refs, refs = refs[-turns - 1 : -1], refs[: -turns - 1] + refs[-1:]
-    *weight_refs, rows_ref = refs
-    depth, width = weight_refs[0].shape
+def own_kernel(*refs):
+    *received_refs, first_ref, matrix_ref, out_ref, second_ref, sem = refs
+    depth, width = matrix_ref.shape
+    head = first_ref.shape[0]
+    copy = pltpu.make_async_copy(matrix_ref.at[pl.ds(head, depth - head)], second_ref, sem)
+    copy.start()
+    rows = jnp.concatenate([received_ref[:, :depth] for received_ref in received_refs], axis=0)
+    for start in range(0, width, TILE):
+        columns = slice(start, start + TILE)
+        out_ref[:, columns] = jnp.dot(
+            rows[:, :head], first_ref[:, columns], preferred_element_type=jnp.float32
+        )
+    copy.wait()
+    for start in range(0, width, TILE):
+        columns = slice(start, start + TILE)
+        out_ref[:, columns] += jnp.dot(
+            rows[:, head:], second_ref[:, columns], preferred_element_type=jnp.float32
+        )
+
+
+def other_kernel(turns, *refs):
+    received_refs = refs[:turns]
+    own_ref, weight_ref, *out_refs = refs[turns:]
+    depth, width = weight_ref.shape
     block = received_refs[0].shape[0]
-    for turn, received_ref in enumerate(received_refs):
-        rows_ref[turn * block : (turn + 1) * block, :] = received_ref[...]
-
-    @pl.loop(0, width // tile)
-    def _(i):
-        columns = pl.ds(pl.multiple_of(i * tile, tile), tile)
-        total = None
-        for q, weight_ref in enumerate(weight_refs):
-            part = jnp.dot(
-                rows_ref[:, q * depth : (q + 1) * depth],
-                weight_ref[:, columns],
-                preferred_element_type=jnp.float32,
-            )
-            total = part if total is None else total + part
-        total = total.astype(jnp.bfloat16)
+    rows = jnp.concatenate([received_ref[:, depth:] for received_ref in received_refs], axis=0)
+
+    for start in range(0, width, TILE):
+        columns = slice(start, start + TILE)
+        part = jnp.dot(rows, weight_ref[:, columns], preferred_element_type=jnp.float32)
+        total = (own_ref[:, columns] + part).astype(jnp.bfloat16)
         for turn, out_ref in enumerate(out_refs):
             out_ref[:, columns] = total[turn * block : (turn + 1) * block]
 
@@ -203,7 +229,7 @@
 ):
     node_count = lax.axis_size("node")
     lane_count = lax.axis_size("lane")
-    row_count, pick_count, hidden_width = expert_hidden.shape
+    row_count, _, hidden_width = expert_hidden.shape
     width = routed_down.shape[2]
     capacity = max(
         2, min(row_count // 2, 2 * ((row_count * NODES_TOP + node_count - 1) // node_count))
@@ -221,47 +247,82 @@
             pairs = []
             for node in range(node_count):
                 for lane in range(lane_count):
-                    there = partner(node_count, node, number_of(node_count, lane, turn))
+                    there = partner(node_count, node, number_of(node_count, lane_count, lane, turn))
                     pairs.append((node * lane_count + lane, there * lane_count + lane))
             out.append(lax.ppermute(value, ("node", "lane"), pairs))
         return out
 
+    whole = pl.BlockSpec(memory_space=pltpu.VMEM)
+    outside = pl.BlockSpec(memory_space=pltpu.HBM)
+
+    def in_hbm(value):
+        return pltpu.with_memory_space_constraint(value, pltpu.HBM)
+
+    def in_vmem(value):
+        return pltpu.with_memory_space_constraint(value, pltpu.VMEM)
+
+    def params(mib):
+        return pltpu.CompilerParams(vmem_limit_bytes=mib * MIB)
+
+    own_matrix = routed_down[0]
     mine = [gate_scores.T, node_lists.T, expert_picks.T, expert_hidden.reshape(-1, hidden_width)]
     theirs = [other_core(value) for value in mine]
-    down_matrix, *theirs = lax.optimization_barrier((routed_down[0], *theirs))
-    other_matrix = other_core(down_matrix)
+    mine = pl.pallas_call(
+        load_kernel,
+        in_specs=[outside] * 4,
+        out_specs=[whole] * 4,
+        out_shape=[pltpu.VMEM(value.shape, value.dtype) for value in mine],
+        scratch_shapes=[pltpu.SemaphoreType.DMA((4,))],
+        compiler_params=params(1),
+        name="load",
+    )(*[in_hbm(value) for value in mine])
+    sent_matrix, *_ = lax.optimization_barrier((own_matrix, *theirs, mine[0]))
+    other_matrix = other_core(sent_matrix)
     *send, place = pl.pallas_call(
         functools.partial(pack_kernel, node_count, lane_count, capacity),
+        in_specs=[whole] * 8,
+        out_specs=[whole] * (turns + 1),
         out_shape=[jax.ShapeDtypeStruct((block, lane_count * hidden_width), jnp.bfloat16)] * turns
         + [jax.ShapeDtypeStruct((slots, lane_count * row_count), jnp.float32)],
-        compiler_params=pltpu.CompilerParams(vmem_limit_bytes=8 * MIB),
+        compiler_params=params(4),
         name="pack",
-    )(*[pltpu.with_memory_space_constraint(value, pltpu.HBM) for value in mine], *theirs)
+    )(*[in_vmem(value) for value in (*mine, *theirs)])
     received = meet(send)
-    whole = pl.BlockSpec(memory_space=pltpu.VMEM)
-    down_matrix, _ = lax.optimization_barrier((down_matrix, place))
-    own_matrix = pl.pallas_call(
+    own_matrix, _ = lax.optimization_barrier((own_matrix, place))
+    head = hidden_width * 3 // 4
+    first = pl.pallas_call(
         fetch_kernel,
-        in_specs=[pl.BlockSpec(memory_space=pltpu.HBM)],
+        in_specs=[outside],
         out_specs=whole,
-        out_shape=pltpu.VMEM(down_matrix.shape, down_matrix.dtype),
+        out_shape=pltpu.VMEM((head, width), own_matrix.dtype),
         scratch_shapes=[pltpu.SemaphoreType.DMA],
-        compiler_params=pltpu.CompilerParams(vmem_limit_bytes=MIB),
-        cost_estimate=pl.CostEstimate(flops=0, bytes_accessed=4 * down_matrix.size, transcendentals=0),
+        compiler_params=params(1),
+        cost_estimate=pl.CostEstimate(flops=0, bytes_accessed=4 * head * width, transcendentals=0),
         name="fetch",
-    )(pltpu.with_memory_space_constraint(down_matrix, pltpu.HBM))
+    )(in_hbm(own_matrix))
+    own_part = pl.pallas_call(
+        own_kernel,
+        in_specs=[whole] * (turns + 1) + [outside],
+        out_specs=whole,
+        out_shape=jax.ShapeDtypeStruct((slots, width), jnp.float32),
+        scratch_shapes=[
+            pltpu.VMEM((hidden_width - head, width), own_matrix.dtype),
+            pltpu.SemaphoreType.DMA,
+        ],
+        compiler_params=params(8),
+        name="own",
+    )(*received, in_vmem(first), in_hbm(own_matrix))
     output = pl.pallas_call(
-        functools.partial(expert_kernel, turns, 512),
-        in_specs=[whole] * (turns + lane_count),
+        functools.partial(other_kernel, turns),
+        in_specs=[whole] * (turns + 2),
         out_specs=[whole] * turns,
         out_shape=[jax.ShapeDtypeStruct((block, width), jnp.bfloat16)] * turns,
-        scratch_shapes=[pltpu.VMEM((slots, lane_count * hidden_width), jnp.bfloat16)],
-        compiler_params=pltpu.CompilerParams(vmem_limit_bytes=24 * MIB),
-        name="experts",
-    )(*received, *[pltpu.with_memory_space_constraint(m, pltpu.VMEM) for m in (own_matrix, other_matrix)])
+        compiler_params=params(2),
+        name="other",
+    )(*received, in_vmem(own_part), in_vmem(other_matrix))
     returned = meet(output)
     query_latent, query_rope, cache_latent, cache_rope, cache_lengths, _ = lax.optimization_barrier(
-        (query_latent, query_rope, cache_latent, cache_rope, cache_lengths, output[0])
+        (query_latent, query_rope, cache_latent, cache_rope, cache_lengths, output[-1])
     )
     context = attend(query_latent, query_rope, cache_latent, cache_rope, cache_lengths)
     *returned, context = lax.optimization_barrier((*returned, context))

time: 36.6 us -> 35.4 us (0.967)
  waiting for transfers between devices: 7.36 us -> 10.1 us
  Pallas kernels: 12.7 us -> 10.1 us
  starting transfers between devices: 14.7 us -> 13.2 us
    ppermute x8, waiting for transfers between devices: 4.59 us -> 8.75 us  [meet(): out.append(lax.ppermute(value, ('node', 'lane'), pairs))]
    pallas_call x1, Pallas kernels: 4.22 us -> 2.22 us  [attend(): pl.pallas_call(attend_kernel, in_specs=[pl.BlockSpec(memory_space=pltpu.S...]
    ppermute x8, starting transfers between devices: 13.3 us -> 11.3 us  [meet(): out.append(lax.ppermute(value, ('node', 'lane'), pairs))]
    ppermute x6, waiting for transfers between devices: 2.77 us -> 1.37 us  [other_core(): return lax.ppermute(value, 'lane', [(0, 1), (1, 0)])]
    pallas_call x1, Pallas kernels: 1.76 us -> 0.75 us  [local(): pl.pallas_call(functools.partial(pack_kernel, node_count, lane_count, cap...]
    ppermute x6, starting transfers between devices: 1.42 us -> 1.92 us  [other_core(): return lax.ppermute(value, 'lane', [(0, 1), (1, 0)])]
    pallas_call x2 -> x4, Pallas kernels: 6.46 us -> 6.94 us  [the longest x1 2.57 us: local(): pl.pallas_call(fetch_kernel, in_specs=[outside], out_specs=whole, out_sha...]
  transfers between devices with their start and end apart: 14 -> 14, of which waited for: 5 -> 5; matrix products, arithmetic and copies ran while one was open for 0% -> 0% of each run, Pallas kernels for 25% -> 24%
where the time goes in v3:
time: 35.4 us; the launch traced here: 35.2 us
  starting transfers between devices  13.2 us (37%)
  Pallas kernels  10.1 us (29%)
  waiting for transfers between devices  10.1 us (29%)
  between operations  0.8 us (2%)
  other arithmetic  0.67 us (2%)
    ppermute x8, starting transfers between devices, meet(): out.append(lax.ppermute(value, ('node', 'lane'), pairs))  11.3 us
    ppermute x8, waiting for transfers between devices, meet(): out.append(lax.ppermute(value, ('node', 'lane'), pairs))  8.75 us
    pallas_call x1, Pallas kernels, local(): pl.pallas_call(fetch_kernel, in_specs=[outside], out_specs=whole, out_sha...  2.57 us
    pallas_call x1, Pallas kernels, attend(): pl.pallas_call(attend_kernel, in_specs=[pl.BlockSpec(memory_space=pltpu.S...  2.22 us
    pallas_call x1, Pallas kernels, local(): pl.pallas_call(own_kernel, in_specs=[whole] * (turns + 1) + [outside], ou...  1.96 us
    ppermute x6, starting transfers between devices, other_core(): return lax.ppermute(value, 'lane', [(0, 1), (1, 0)])  1.92 us
    ppermute x6, waiting for transfers between devices, other_core(): return lax.ppermute(value, 'lane', [(0, 1), (1, 0)])  1.37 us
    pallas_call x1, Pallas kernels, local(): pl.pallas_call(functools.partial(other_kernel, turns), in_specs=[whole] *...  1.37 us
  transfers between devices with their start and end apart: 14, of which 5 were waited for; matrix products, arithmetic and copies ran while one was open for 0% of the time, Pallas kernels for 24%

profile of v3, /device:TPU:0, one launch (start us, length us, event | category | flops | bytes accessed | tf_op | source)
XLA Modules:
  0.0 35.2 jit_solution(1314473478074907920)
XLA Ops:
  0.6 0.5 %collective-permute-start.3 = (bf16[128,1024]{1,0:T(8,128)(2,1)}, bf16[128,1024]{1,0:T(8,128)(2,1)S(1)}, u32[]{:S(2)}, u32[]{:S(2)}) collective-permute-start(bf16[128,1024]{1,0:T(8,128)(2,1)} %bitcast.8), channel_id=1, source_target_pairs={{0,1},{1,0},{2,3},{3,2},{4,5},{5,4},{6,7},{7,6},{8,9},{9,8},{10,11... | collective-permute-start | bytes 786440 | tf_op jit(solution)/shard_map/ppermute | solution.py:242
  1.1 0.1 collective-permute-start
  1.2 0.4 %collective-permute-start.2 = (s32[8,16]{1,0:T(8,128)}, s32[8,16]{1,0:T(8,128)S(1)}, u32[]{:S(2)}, u32[]{:S(2)}) collective-permute-start(s32[8,16]{1,0:T(8,128)} %bitcast.12), channel_id=1, source_target_pairs={{0,1},{1,0},{2,3},{3,2},{4,5},{5,4},{6,7},{7,6},{8,9},{9,8},{10,11... | collective-permute-start | bytes 1544 | tf_op jit(solution)/shard_map/ppermute | solution.py:242
  1.7 0.1 collective-permute-start.1
  1.7 1.0 %load.1 = (f32[8,16]{1,0:T(8,128)S(1)}, s32[4,16]{1,0:T(4,128)S(1)}, s32[8,16]{1,0:T(8,128)S(1)}, bf16[128,1024]{1,0:T(8,128)(2,1)S(1)}) custom-call(f32[8,16]{1,0:T(8,128)} %bitcast.11, s32[4,16]{1,0:T(4,128)} %bitcast.15, s32[8,16]{1,0:T(8,128)} %bitcast.13, bf16[128,1024]{1,0:T(8,128)(2,1)} %bitcast.9), custom_call_target="tpu_custom_call" | custom-call | tf_op jit(solution)/shard_map/load/pallas_call | solution.py:270
  2.8 0.2 collective-permute-done.1.refs_5_
  3.0 0.0 collective-permute-done.refs_4_
  3.0 0.0 collective-permute-done.2.refs_6_
  3.0 0.0 collective-permute-done.3.refs_7_
  3.0 0.3 collective-permute-start.8
  3.3 0.8 %pack.1 = (bf16[16,2048]{1,0:T(8,128)(2,1)S(1)}, bf16[16,2048]{1,0:T(8,128)(2,1)S(1)}, bf16[16,2048]{1,0:T(8,128)(2,1)S(1)}, bf16[16,2048]{1,0:T(8,128)(2,1)S(1)}, f32[64,32]{1,0:T(8,128)S(1)}) custom-call(f32[8,16]{1,0:T(8,128)S(1)} %get-tuple-element.29.refs_0_, s32[4,16]{1,0:T(4,128)S(1)} %get-tuple-element.30.refs_1_, ...), custom_call_target="tpu_custom_call" | custom-call | tf_op jit(solution)/shard_map/pack/pallas_call | solution.py:281
  4.1 4.9 %collective-permute-start.4 = (bf16[16,2048]{1,0:T(8,128)(2,1)S(1)}, bf16[16,2048]{1,0:T(8,128)(2,1)S(1)}, u32[]{:S(2)}, u32[]{:S(2)}) collective-permute-start(bf16[16,2048]{1,0:T(8,128)(2,1)S(1)} %get-tuple-element.34), channel_id=1, source_target_pairs={{0,12},{1,15},{2,14},{3,13},{4,8},{5,11},{6,10},{7,9},{8,4},{9,7},... | collective-permute-start | bytes 196616 | tf_op jit(solution)/shard_map/ppermute | solution.py:252
  9.0 0.0 collective-permute-start.5
  9.0 0.6 %collective-permute-start.6 = (bf16[16,2048]{1,0:T(8,128)(2,1)S(1)}, bf16[16,2048]{1,0:T(8,128)(2,1)S(1)}, u32[]{:S(2)}, u32[]{:S(2)}) collective-permute-start(bf16[16,2048]{1,0:T(8,128)(2,1)S(1)} %get-tuple-element.36), channel_id=1, source_target_pairs={{0,4},{1,7},{2,6},{3,5},{4,0},{5,3},{6,2},{7,1},{8,12},{9,15},{10,... | collective-permute-start | bytes 196616 | tf_op jit(solution)/shard_map/ppermute | solution.py:252
  9.6 0.7 %collective-permute-start.7 = (bf16[16,2048]{1,0:T(8,128)(2,1)S(1)}, bf16[16,2048]{1,0:T(8,128)(2,1)S(1)}, u32[]{:S(2)}, u32[]{:S(2)}) collective-permute-start(bf16[16,2048]{1,0:T(8,128)(2,1)S(1)} %get-tuple-element.37), channel_id=1, source_target_pairs={{0,0},{1,3},{2,2},{3,1},{4,4},{5,7},{6,6},{7,5},{8,8},{9,11},{10,1... | collective-permute-start | bytes 196616 | tf_op jit(solution)/shard_map/ppermute | solution.py:252
  10.3 2.6 %fetch.1.refs_4_ = bf16[768,3584]{1,0:T(8,128)(2,1)S(1)} custom-call(bf16[1024,3584]{1,0:T(8,128)(2,1)} %bitcast.6), custom_call_target="tpu_custom_call" | custom-call | bytes 11010048 | tf_op jit(solution)/shard_map/fetch/pallas_call | solution.py:293
  12.9 0.0 collective-permute-done.4.refs_0_
  12.9 2.5 %collective-permute-done.5.refs_1_ = bf16[16,2048]{1,0:T(8,128)(2,1)S(1)} collective-permute-done((bf16[16,2048]{1,0:T(8,128)(2,1)S(1)}, bf16[16,2048]{1,0:T(8,128)(2,1)S(1)}, u32[]{:S(2)}, u32[]{:S(2)}) %collective-permute-start.5) | collective-permute-done | bytes 65568 | tf_op jit(solution)/shard_map/ppermute | solution.py:252
  15.4 0.0 collective-permute-done.6.refs_2_
  15.4 0.0 collective-permute-done.7.refs_3_
  15.4 2.0 %own.1.refs_4_ = f32[64,3584]{1,0:T(8,128)S(1)} custom-call(bf16[16,2048]{1,0:T(8,128)(2,1)S(1)} %collective-permute-done.4.refs_0_, bf16[16,2048]{1,0:T(8,128)(2,1)S(1)} %collective-permute-done.5.refs_1_, bf16[16,2048]{1,0:T(8,128)(2,1)S(1)} %collective-permute-done.6.refs_2_, bf16[16,2048]{1,0:T(8,128)(2,1)S(1)} %collective-permute-done.7.refs_3_, ...), custom_call_target="tpu_custom_call" | custom-call | tf_op jit(solution)/shard_map/own/pallas_call | solution.py:303
  17.3 0.0 copy-start.4
  17.4 0.0 copy-start
  17.4 0.0 copy-start.1
  17.4 0.0 copy-start.2
  17.4 0.0 copy-start.3
  17.4 0.0 collective-permute-done.8.refs_5_
  17.4 1.4 %other.1 = (bf16[16,3584]{1,0:T(8,128)(2,1)S(1)}, bf16[16,3584]{1,0:T(8,128)(2,1)S(1)}, bf16[16,3584]{1,0:T(8,128)(2,1)S(1)}, bf16[16,3584]{1,0:T(8,128)(2,1)S(1)}) custom-call(bf16[16,2048]{1,0:T(8,128)(2,1)S(1)} %collective-permute-done.4.refs_0_, bf16[16,2048]{1,0:T(8,128)(2,1)S(1)} %collective-permute-done.5.refs_1_, ...), custom_call_target="tpu_custom_call" | custom-call | tf_op jit(solution)/shard_map/other/pallas_call | solution.py:315
  18.8 2.6 %collective-permute-start.9 = (bf16[16,3584]{1,0:T(8,128)(2,1)S(1)}, bf16[16,3584]{1,0:T(8,128)(2,1)S(1)}, u32[]{:S(2)}, u32[]{:S(2)}) collective-permute-start(bf16[16,3584]{1,0:T(8,128)(2,1)S(1)} %get-tuple-element.40), channel_id=1, source_target_pairs={{0,12},{1,15},{2,14},{3,13},{4,8},{5,11},{6,10},{7,9},{8,4},{9,7},... | collective-permute-start | bytes 344072 | tf_op jit(solution)/shard_map/ppermute | solution.py:252
  21.3 0.2 collective-permute-start.10
  21.5 1.7 %collective-permute-start.11 = (bf16[16,3584]{1,0:T(8,128)(2,1)S(1)}, bf16[16,3584]{1,0:T(8,128)(2,1)S(1)}, u32[]{:S(2)}, u32[]{:S(2)}) collective-permute-start(bf16[16,3584]{1,0:T(8,128)(2,1)S(1)} %get-tuple-element.42), channel_id=1, source_target_pairs={{0,4},{1,7},{2,6},{3,5},{4,0},{5,3},{6,2},{7,1},{8,12},{9,15},{10,... | collective-permute-start | bytes 344072 | tf_op jit(solution)/shard_map/ppermute | solution.py:252
  23.2 0.7 %collective-permute-start.12 = (bf16[16,3584]{1,0:T(8,128)(2,1)S(1)}, bf16[16,3584]{1,0:T(8,128)(2,1)S(1)}, u32[]{:S(2)}, u32[]{:S(2)}) collective-permute-start(bf16[16,3584]{1,0:T(8,128)(2,1)S(1)} %get-tuple-element.43), channel_id=1, source_target_pairs={{0,0},{1,3},{2,2},{3,1},{4,4},{5,7},{6,6},{7,5},{8,8},{9,11},{10,1... | collective-permute-start | bytes 344072 | tf_op jit(solution)/shard_map/ppermute | solution.py:252
  23.9 0.0 copy-done.4
  23.9 0.2 reshape.11.rope_ref
  24.1 0.0 copy-done
  24.1 0.0 copy-done.1
  24.1 0.0 copy-done.2
  24.1 0.0 copy-done.3
  24.1 2.2 %attend.1 = bf16[8,64,512]{2,1,0:T(8,128)(2,1)} custom-call(s32[8]{0:T(128)S(1)} %copy-done.3, bf16[8,64,512]{2,1,0:T(8,128)(2,1)S(1)} %copy-done.1, bf16[8,64,64]{2,1,0:T(8,128)(2,1)S(1)} %reshape.11.rope_ref, bf16[8,128,512]{2,1,0:T(8,128)(2,1)S(1)} %copy-done, bf16[8,64,128]{2,1,0:T(8,128)(2,1)S(1)} %copy-done.2), custom_call_target="tpu_custom_call" | custom-call | flops 142606336 | bytes 2293760 | tf_op jit(solution)/shard_map/attend/pallas_call | solution.py:44
  26.4 0.2 collective-permute-done.9.refs_0_
  26.6 6.0 %collective-permute-done.10.refs_1_ = bf16[16,3584]{1,0:T(8,128)(2,1)S(1)} collective-permute-done((bf16[16,3584]{1,0:T(8,128)(2,1)S(1)}, bf16[16,3584]{1,0:T(8,128)(2,1)S(1)}, u32[]{:S(2)}, u32[]{:S(2)}) %collective-permute-start.10) | collective-permute-done | bytes 114720 | tf_op jit(solution)/shard_map/ppermute | solution.py:252
  32.6 0.0 collective-permute-done.11.refs_2_
  32.6 0.0 collective-permute-done.12.refs_3_
  32.6 0.2 sum.1
  32.9 0.5 %collective-permute-start.13 = (f32[16,3584]{1,0:T(8,128)S(1)}, f32[16,3584]{1,0:T(8,128)S(1)}, u32[]{:S(2)}, u32[]{:S(2)}) collective-permute-start(f32[16,3584]{1,0:T(8,128)S(1)} %get-tuple-element.54), channel_id=1, source_target_pairs={{0,1},{1,0},{2,3},{3,2},{4,5},{5,4},{6,7},{7,6},{8,9},{9,8},{10,11... | collective-permute-start | bytes 688136 | tf_op jit(solution)/shard_map/ppermute | solution.py:242
  33.4 1.1 %collective-permute-done.13 = f32[16,3584]{1,0:T(8,128)S(1)} collective-permute-done((f32[16,3584]{1,0:T(8,128)S(1)}, f32[16,3584]{1,0:T(8,128)S(1)}, u32[]{:S(2)}, u32[]{:S(2)}) %collective-permute-start.13) | collective-permute-done | bytes 229408 | tf_op jit(solution)/shard_map/ppermute | solution.py:242
  34.5 0.7 %add_convert_fusion = bf16[16,3584]{1,0:T(8,128)(2,1)} fusion(f32[16,3584]{1,0:T(8,128)S(1)} %get-tuple-element.53, f32[16,3584]{1,0:T(8,128)S(1)} %collective-permute-done.13), kind=kLoop, calls=%fused_computation | loop fusion | flops 114688 | bytes 573440 | tf_op jit(solution)/shard_map/convert_element_type | solution.py:336
Async XLA Ops:
  0.6 2.4 %collective-permute-start.3 = (bf16[128,1024]{1,0:T(8,128)(2,1)}, bf16[128,1024]{1,0:T(8,128)(2,1)S(1)}, u32[]{:S(2)}, u32[]{:S(2)}) collective-permute-start(bf16[128,1024]{1,0:T(8,128)(2,1)} %bitcast.8), channel_id=1, source_target_pairs={{0,1},{1,0},{2,3},{3,2},{4,5},{5,4},{6,7},{7,6},{8,9},{9,8},{10,11... | collective-permute-start | bytes 786440 | tf_op jit(solution)/shard_map/ppermute | solution.py:242
  1.1 1.9 %collective-permute-start = (f32[8,16]{1,0:T(8,128)}, f32[8,16]{1,0:T(8,128)S(1)}, u32[]{:S(2)}, u32[]{:S(2)}) collective-permute-start(f32[8,16]{1,0:T(8,128)} %bitcast.10), channel_id=1, source_target_pairs={{0,1},{1,0},{2,3},{3,2},{4,5},{5,4},{6,7},{7,6},{8,9},{9,8},{10,11... | collective-permute-start | bytes 1544 | tf_op jit(solution)/shard_map/ppermute | solution.py:242
  1.2 1.8 %collective-permute-start.2 = (s32[8,16]{1,0:T(8,128)}, s32[8,16]{1,0:T(8,128)S(1)}, u32[]{:S(2)}, u32[]{:S(2)}) collective-permute-start(s32[8,16]{1,0:T(8,128)} %bitcast.12), channel_id=1, source_target_pairs={{0,1},{1,0},{2,3},{3,2},{4,5},{5,4},{6,7},{7,6},{8,9},{9,8},{10,11... | collective-permute-start | bytes 1544 | tf_op jit(solution)/shard_map/ppermute | solution.py:242
  1.7 1.4 %collective-permute-start.1 = (s32[4,16]{1,0:T(4,128)}, s32[4,16]{1,0:T(4,128)S(1)}, u32[]{:S(2)}, u32[]{:S(2)}) collective-permute-start(s32[4,16]{1,0:T(4,128)} %bitcast.14), channel_id=1, source_target_pairs={{0,1},{1,0},{2,3},{3,2},{4,5},{5,4},{6,7},{7,6},{8,9},{9,8},{10,11... | collective-permute-start | bytes 776 | tf_op jit(solution)/shard_map/ppermute | solution.py:242
  3.0 14.4 %collective-permute-start.8 = (bf16[1024,3584]{1,0:T(8,128)(2,1)}, bf16[1024,3584]{1,0:T(8,128)(2,1)S(1)}, u32[]{:S(2)}, u32[]{:S(2)}) collective-permute-start(bf16[1024,3584]{1,0:T(8,128)(2,1)} %bitcast.5), channel_id=1, source_target_pairs={{0,1},{1,0},{2,3},{3,2},{4,5},{5,4},{6,7},{7,6},{8,9},{9,8},{10,11... | collective-permute-start | bytes 22020104 | tf_op jit(solution)/shard_map/ppermute | solution.py:242
  4.1 8.8 %collective-permute-start.4 = (bf16[16,2048]{1,0:T(8,128)(2,1)S(1)}, bf16[16,2048]{1,0:T(8,128)(2,1)S(1)}, u32[]{:S(2)}, u32[]{:S(2)}) collective-permute-start(bf16[16,2048]{1,0:T(8,128)(2,1)S(1)} %get-tuple-element.34), channel_id=1, source_target_pairs={{0,12},{1,15},{2,14},{3,13},{4,8},{5,11},{6,10},{7,9},{8,4},{9,7},... | collective-permute-start | bytes 196616 | tf_op jit(solution)/shard_map/ppermute | solution.py:252
  9.0 6.4 %collective-permute-start.5 = (bf16[16,2048]{1,0:T(8,128)(2,1)S(1)}, bf16[16,2048]{1,0:T(8,128)(2,1)S(1)}, u32[]{:S(2)}, u32[]{:S(2)}) collective-permute-start(bf16[16,2048]{1,0:T(8,128)(2,1)S(1)} %get-tuple-element.35), channel_id=1, source_target_pairs={{0,8},{1,11},{2,10},{3,9},{4,12},{5,15},{6,14},{7,13},{8,0},{9,3},... | collective-permute-start | bytes 196616 | tf_op jit(solution)/shard_map/ppermute | solution.py:252
  9.0 6.4 %collective-permute-start.6 = (bf16[16,2048]{1,0:T(8,128)(2,1)S(1)}, bf16[16,2048]{1,0:T(8,128)(2,1)S(1)}, u32[]{:S(2)}, u32[]{:S(2)}) collective-permute-start(bf16[16,2048]{1,0:T(8,128)(2,1)S(1)} %get-tuple-element.36), channel_id=1, source_target_pairs={{0,4},{1,7},{2,6},{3,5},{4,0},{5,3},{6,2},{7,1},{8,12},{9,15},{10,... | collective-permute-start | bytes 196616 | tf_op jit(solution)/shard_map/ppermute | solution.py:252
  9.6 5.7 %collective-permute-start.7 = (bf16[16,2048]{1,0:T(8,128)(2,1)S(1)}, bf16[16,2048]{1,0:T(8,128)(2,1)S(1)}, u32[]{:S(2)}, u32[]{:S(2)}) collective-permute-start(bf16[16,2048]{1,0:T(8,128)(2,1)S(1)} %get-tuple-element.37), channel_id=1, source_target_pairs={{0,0},{1,3},{2,2},{3,1},{4,4},{5,7},{6,6},{7,5},{8,8},{9,11},{10,1... | collective-permute-start | bytes 196616 | tf_op jit(solution)/shard_map/ppermute | solution.py:252
  17.3 6.6 %copy-start.4 = (bf16[8,4096]{1,0:T(8,128)(2,1)S(1)}, bf16[8,4096]{1,0:T(8,128)(2,1)}, u32[]{:S(2)}) copy-start(bf16[8,4096]{1,0:T(8,128)(2,1)} %param.16) | copy-start | bytes 196612
  17.4 6.8 %copy-start = (bf16[8,128,512]{2,1,0:T(8,128)(2,1)S(1)}, bf16[8,128,512]{2,1,0:T(8,128)(2,1)}, u32[]{:S(2)}) copy-start(bf16[8,128,512]{2,1,0:T(8,128)(2,1)} %keys_ref) | copy-start | bytes 3145732
  17.4 6.7 %copy-start.1 = (bf16[8,64,512]{2,1,0:T(8,128)(2,1)S(1)}, bf16[8,64,512]{2,1,0:T(8,128)(2,1)}, u32[]{:S(2)}) copy-start(bf16[8,64,512]{2,1,0:T(8,128)(2,1)} %latent_ref) | copy-start | bytes 1572868
  17.4 6.7 %copy-start.2 = (bf16[8,64,128]{2,1,0:T(8,128)(2,1)S(1)}, bf16[8,64,128]{2,1,0:T(8,128)(2,1)}, u32[]{:S(2)}) copy-start(bf16[8,64,128]{2,1,0:T(8,128)(2,1)} %rope_keys_ref) | copy-start | bytes 393220
  17.4 6.7 %copy-start.3 = (s32[8]{0:T(128)S(1)}, s32[8]{0:T(128)}, u32[]{:S(2)}) copy-start(s32[8]{0:T(128)} %lengths_ref) | copy-start | bytes 100
  18.8 7.8 %collective-permute-start.9 = (bf16[16,3584]{1,0:T(8,128)(2,1)S(1)}, bf16[16,3584]{1,0:T(8,128)(2,1)S(1)}, u32[]{:S(2)}, u32[]{:S(2)}) collective-permute-start(bf16[16,3584]{1,0:T(8,128)(2,1)S(1)} %get-tuple-element.40), channel_id=1, source_target_pairs={{0,12},{1,15},{2,14},{3,13},{4,8},{5,11},{6,10},{7,9},{8,4},{9,7},... | collective-permute-start | bytes 344072 | tf_op jit(solution)/shard_map/ppermute | solution.py:252
  21.3 11.3 %collective-permute-start.10 = (bf16[16,3584]{1,0:T(8,128)(2,1)S(1)}, bf16[16,3584]{1,0:T(8,128)(2,1)S(1)}, u32[]{:S(2)}, u32[]{:S(2)}) collective-permute-start(bf16[16,3584]{1,0:T(8,128)(2,1)S(1)} %get-tuple-element.41), channel_id=1, source_target_pairs={{0,8},{1,11},{2,10},{3,9},{4,12},{5,15},{6,14},{7,13},{8,0},{9,3},... | collective-permute-start | bytes 344072 | tf_op jit(solution)/shard_map/ppermute | solution.py:252
  21.5 11.1 %collective-permute-start.11 = (bf16[16,3584]{1,0:T(8,128)(2,1)S(1)}, bf16[16,3584]{1,0:T(8,128)(2,1)S(1)}, u32[]{:S(2)}, u32[]{:S(2)}) collective-permute-start(bf16[16,3584]{1,0:T(8,128)(2,1)S(1)} %get-tuple-element.42), channel_id=1, source_target_pairs={{0,4},{1,7},{2,6},{3,5},{4,0},{5,3},{6,2},{7,1},{8,12},{9,15},{10,... | collective-permute-start | bytes 344072 | tf_op jit(solution)/shard_map/ppermute | solution.py:252
  23.2 9.4 %collective-permute-start.12 = (bf16[16,3584]{1,0:T(8,128)(2,1)S(1)}, bf16[16,3584]{1,0:T(8,128)(2,1)S(1)}, u32[]{:S(2)}, u32[]{:S(2)}) collective-permute-start(bf16[16,3584]{1,0:T(8,128)(2,1)S(1)} %get-tuple-element.43), channel_id=1, source_target_pairs={{0,0},{1,3},{2,2},{3,1},{4,4},{5,7},{6,6},{7,5},{8,8},{9,11},{10,1... | collective-permute-start | bytes 344072 | tf_op jit(solution)/shard_map/ppermute | solution.py:252
  32.9 1.7 %collective-permute-start.13 = (f32[16,3584]{1,0:T(8,128)S(1)}, f32[16,3584]{1,0:T(8,128)S(1)}, u32[]{:S(2)}, u32[]{:S(2)}) collective-permute-start(f32[16,3584]{1,0:T(8,128)S(1)} %get-tuple-element.54), channel_id=1, source_target_pairs={{0,1},{1,0},{2,3},{3,2},{4,5},{5,4},{6,7},{7,6},{8,9},{9,8},{10,11... | collective-permute-start | bytes 688136 | tf_op jit(solution)/shard_map/ppermute | solution.py:242

commit v4 on v3

--- a/solution.py
+++ b/solution.py
@@ -47,11 +47,7 @@
         out_specs=pl.BlockSpec(memory_space=pltpu.VMEM),
         out_shape=jax.ShapeDtypeStruct(query_latent.shape, jnp.bfloat16),
         compiler_params=pltpu.CompilerParams(vmem_limit_bytes=8 * MIB),
-        cost_estimate=pl.CostEstimate(
-            flops=2 * row_count * products,
-            bytes_accessed=2 * (2 * query_latent.size + query_rope.size + cache_latent.size + cache_rope.size),
-            transcendentals=row_count * head_count * position_count,
-        ),
+        cost_estimate=pl.CostEstimate(flops=0, bytes_accessed=0, transcendentals=0),
         name="attend",
     )(cache_lengths, query_latent, rope_query, cache_latent, cache_rope)
 
@@ -93,74 +89,103 @@
         copy.wait()
 
 
+def spread_of(pick_count, row_count):
+    items = pick_count * row_count
+    spread = iota((row_count, items), 1) // pick_count == iota((row_count, items), 0)
+    return jnp.where(spread, 1.0, 0.0).astype(jnp.bfloat16)
+
+
+def flat(values, spread):
+    pick_count, _ = values.shape
+    _, items = spread.shape
+    own_pick = lax.rem(iota((pick_count, items), 1), pick_count) == iota((pick_count, items), 0)
+    return jnp.sum(jnp.where(own_pick, exact(values, spread), 0.0), axis=0, keepdims=True)
+
+
+def route(node_count, lane_count, lists, picks, spread):
+    _, row_count = picks.shape
+    _, items = spread.shape
+    lane_here = lax.axis_index("lane")
+    before = iota((row_count, row_count), 0) < iota((row_count, row_count), 1)
+    nodes = iota((node_count, row_count), 0)
+    choice = picks // lane_count
+    order = lax.rem(picks - choice * lane_count - lane_here + lane_count, lane_count)
+    node = jnp.zeros_like(picks)
+    member = jnp.zeros((node_count, row_count), jnp.float32)
+    for j in range(lists.shape[0]):
+        node = jnp.where(choice == j, lists[j : j + 1, :], node)
+        member = jnp.where(nodes == lists[j : j + 1, :], 1.0, member)
+    earlier = exact(exact(member, jnp.where(before, 1.0, 0.0)), spread)
+    both = flat((node * lane_count + order).astype(jnp.float32), spread).astype(jnp.int32)
+    node = both // lane_count
+    order = both - node * lane_count
+    named = iota((node_count, items), 0) == node
+    slot = jnp.sum(jnp.where(named, earlier, 0.0), axis=0, keepdims=True).astype(jnp.int32)
+    return meeting(node_count, lax.axis_index("node"), node), slot, order
+
+
+def target_of(node_count, lane_count, capacity, source, number, slot):
+    turn = turn_of(node_count, lane_count, lax.axis_index("lane"), number)
+    return jnp.where(turn >= 0, (turn * lane_count + source) * capacity + slot, -1)
+
+
 def pack_kernel(node_count, lane_count, capacity, *refs):
     sources = [refs[4 * s : 4 * s + 4] for s in range(lane_count)]
-    send_refs = refs[4 * lane_count : -1]
-    place_ref = refs[-1]
-    pick_count, row_count = sources[0][0].shape
-    items = pick_count * row_count
+    send_refs = refs[4 * lane_count :]
     block = lane_count * capacity
     slots = len(send_refs) * block
     hidden_width = sources[0][3].shape[1]
-    lane_here = lax.axis_index("lane")
-    node_here = lax.axis_index("node")
-
-    spread = iota((row_count, items), 1) // pick_count == iota((row_count, items), 0)
-    spread = jnp.where(spread, 1.0, 0.0).astype(jnp.bfloat16)
-    own_pick = lax.rem(iota((pick_count, items), 1), pick_count) == iota((pick_count, items), 0)
-    before = iota((row_count, row_count), 0) < iota((row_count, row_count), 1)
-    before = jnp.where(before, 1.0, 0.0)
-    nodes = iota((node_count, row_count), 0)
-    places = iota((slots, items), 0)
-
-    def flat(values):
-        wide = exact(values, spread)
-        return jnp.sum(jnp.where(own_pick, wide, 0.0), axis=0, keepdims=True)
-
+    spread = spread_of(*sources[0][0].shape)
+    places = iota((slots, spread.shape[1]), 0)
     parts = [None] * lane_count
     for s, (scores_ref, lists_ref, picks_ref, hidden_ref) in enumerate(sources):
         scores = scores_ref[...]
         combine = (route_scale * scores / jnp.sum(scores, axis=0, keepdims=True)).astype(jnp.bfloat16)
-        picks = picks_ref[...]
-        lists = lists_ref[...]
-        choice = picks // lane_count
-        order = lax.rem(picks - choice * lane_count - lane_here + lane_count, lane_count)
-        node = jnp.zeros_like(picks)
-        member = jnp.zeros((node_count, row_count), jnp.float32)
-        for j in range(lists.shape[0]):
-            node = jnp.where(choice == j, lists[j : j + 1, :], node)
-            member = jnp.where(nodes == lists[j : j + 1, :], 1.0, member)
-        earlier = exact(exact(member, before), spread)
-        weight = flat(combine)
-        node_and_order = flat((node * lane_count + order).astype(jnp.float32)).astype(jnp.int32)
-        node_flat = node_and_order // lane_count
-        order_flat = node_and_order - node_flat * lane_count
-        named = iota((node_count, items), 0) == node_flat
-        slot = jnp.sum(jnp.where(named, earlier, 0.0), axis=0, keepdims=True).astype(jnp.int32)
-        turn = turn_of(node_count, lane_count, lane_here, meeting(node_count, node_here, node_flat))
-        target = jnp.where(turn >= 0, (turn * lane_count + s) * capacity + slot, -1)
-        at = places == target
+        weight = flat(combine, spread)
+        number, slot, order = route(node_count, lane_count, lists_ref[...], picks_ref[...], spread)
+        at = places == target_of(node_count, lane_count, capacity, s, number, slot)
         hidden = hidden_ref[...]
         for q in range(lane_count):
-            placing = jnp.where(at & (order_flat == q), weight, 0.0).astype(jnp.bfloat16)
+            placing = jnp.where(at & (order == q), weight, 0.0).astype(jnp.bfloat16)
             part = jnp.dot(placing, hidden, preferred_element_type=jnp.float32)
             parts[q] = part if parts[q] is None else parts[q] + part
+    for q in range(lane_count):
+        columns = slice(q * hidden_width, (q + 1) * hidden_width)
+        for turn, send_ref in enumerate(send_refs):
+            send_ref[:, columns] = parts[q][turn * block : (turn + 1) * block].astype(jnp.bfloat16)
+
+
+def fetch_kernel(node_count, lane_count, capacity, split, matrix_ref, *refs):
+    *refs, out_ref, place_ref, split_ref, sem = refs
+    copy = pltpu.make_async_copy(matrix_ref.at[pl.ds(0, out_ref.shape[0])], out_ref, sem)
+    copy.start()
+    pick_count, row_count = refs[1].shape
+    spread = spread_of(pick_count, row_count)
+    items = pick_count * row_count
+
+    def marked(at):
         marks = lax.dot_general(
             jnp.where(at, 1.0, 0.0).astype(jnp.bfloat16),
             spread,
             (((1,), (1,)), ((), ())),
             preferred_element_type=jnp.float32,
         )
-        place_ref[:, s * row_count : (s + 1) * row_count] = jnp.where(marks > 0.0, 1.0, 0.0)
-    for q in range(lane_count):
-        columns = slice(q * hidden_width, (q + 1) * hidden_width)
-        for turn, send_ref in enumerate(send_refs):
-            send_ref[:, columns] = parts[q][turn * block : (turn + 1) * block].astype(jnp.bfloat16)
-
-
-def fetch_kernel(matrix_ref, out_ref, sem):
-    copy = pltpu.make_async_copy(matrix_ref.at[pl.ds(0, out_ref.shape[0])], out_ref, sem)
-    copy.start()
+        return jnp.where(marks > 0.0, 1.0, 0.0)
+
+    for s in range(lane_count):
+        lists_ref, picks_ref = refs[2 * s : 2 * s + 2]
+        number, slot, _ = route(node_count, lane_count, lists_ref[...], picks_ref[...], spread)
+        target = target_of(node_count, lane_count, capacity, s, number, slot)
+        place_ref[:, s * row_count : (s + 1) * row_count] = marked(
+            iota((place_ref.shape[0], items), 0) == target
+        )
+        if s == 0:
+            for q in range(lane_count):
+                lane = lax.rem(lax.axis_index("lane") + q, lane_count)
+                there = number == number_of(node_count, lane_count, lane, split)
+                split_ref[q * capacity : (q + 1) * capacity, :] = marked(
+                    iota((capacity, items), 0) == jnp.where(there, slot, -1)
+                )
     copy.wait()
 
 
@@ -188,31 +213,53 @@
     received_refs = refs[:turns]
     own_ref, weight_ref, *out_refs = refs[turns:]
     depth, width = weight_ref.shape
-    block = received_refs[0].shape[0]
     rows = jnp.concatenate([received_ref[:, depth:] for received_ref in received_refs], axis=0)
 
     for start in range(0, width, TILE):
         columns = slice(start, start + TILE)
         part = jnp.dot(rows, weight_ref[:, columns], preferred_element_type=jnp.float32)
-        total = (own_ref[:, columns] + part).astype(jnp.bfloat16)
-        for turn, out_ref in enumerate(out_refs):
-            out_ref[:, columns] = total[turn * block : (turn + 1) * block]
-
-
-def sum_kernel(place_ref, *refs):
-    *returned_refs, own_ref, other_ref, all_ref = refs
+        total = own_ref[:, columns] + part
+        start_row = 0
+        for out_ref in out_refs:
+            rows_here = out_ref.shape[0]
+            out_ref[:, columns] = total[start_row : start_row + rows_here].astype(jnp.bfloat16)
+            start_row += rows_here
+
+
+def sum_kernel(split, pieces, place_ref, *refs):
+    *refs, all_ref = refs
+    returned_refs, own_ref, other_refs = refs[:-1-pieces], refs[-1-pieces], refs[-pieces:]
     block = returned_refs[0].shape[0]
     rows = own_ref.shape[0]
-    for turn, returned_ref in enumerate(returned_refs):
-        all_ref[turn * block : (turn + 1) * block, :] = returned_ref[...]
+    for i, returned_ref in enumerate(returned_refs):
+        all_ref[i * block : (i + 1) * block, :] = returned_ref[...]
+    place = place_ref[...]
+    place = jnp.concatenate([place[: split * block], place[(split + 1) * block :]], axis=0)
     total = lax.dot_general(
-        place_ref[...].astype(jnp.bfloat16),
+        place.astype(jnp.bfloat16),
         all_ref[...],
         (((0,), (0,)), ((), ())),
         preferred_element_type=jnp.float32,
     )
     own_ref[...] = total[:rows]
-    other_ref[...] = total[rows:]
+    start = 0
+    for other_ref in other_refs:
+        other_ref[...] = total[rows:, start : start + other_ref.shape[1]].astype(other_ref.dtype)
+        start += other_ref.shape[1]
+
+
+def last_kernel(pieces, own_ref, place_ref, *refs):
+    other_refs, returned_refs, out_ref = refs[:pieces], refs[pieces:-1], refs[-1]
+    slots = returned_refs[0].shape[0]
+    total = own_ref[...] + jnp.concatenate([other_ref[...].astype(jnp.float32) for other_ref in other_refs], axis=1)
+    for i, returned_ref in enumerate(returned_refs):
+        total = total + lax.dot_general(
+            place_ref[i * slots : (i + 1) * slots, :].astype(jnp.bfloat16),
+            returned_ref[...],
+            (((0,), (0,)), ((), ())),
+            preferred_element_type=jnp.float32,
+        )
+    out_ref[...] = total.astype(jnp.bfloat16)
 
 
 def local(
@@ -241,16 +288,13 @@
     def other_core(value):
         return lax.ppermute(value, "lane", [(0, 1), (1, 0)])
 
-    def meet(values):
-        out = []
-        for turn, value in enumerate(values):
-            pairs = []
-            for node in range(node_count):
-                for lane in range(lane_count):
-                    there = partner(node_count, node, number_of(node_count, lane_count, lane, turn))
-                    pairs.append((node * lane_count + lane, there * lane_count + lane))
-            out.append(lax.ppermute(value, ("node", "lane"), pairs))
-        return out
+    def meet(value, turn, across=0):
+        pairs = []
+        for node in range(node_count):
+            for lane in range(lane_count):
+                there = partner(node_count, node, number_of(node_count, lane_count, lane, turn))
+                pairs.append((node * lane_count + lane, there * lane_count + (lane + across) % lane_count))
+        return lax.ppermute(value, ("node", "lane"), pairs)
 
     whole = pl.BlockSpec(memory_space=pltpu.VMEM)
     outside = pl.BlockSpec(memory_space=pltpu.HBM)
@@ -278,28 +322,32 @@
     )(*[in_hbm(value) for value in mine])
     sent_matrix, *_ = lax.optimization_barrier((own_matrix, *theirs, mine[0]))
     other_matrix = other_core(sent_matrix)
-    *send, place = pl.pallas_call(
+    split = turns // 2 - 1
+    send = pl.pallas_call(
         functools.partial(pack_kernel, node_count, lane_count, capacity),
         in_specs=[whole] * 8,
-        out_specs=[whole] * (turns + 1),
-        out_shape=[jax.ShapeDtypeStruct((block, lane_count * hidden_width), jnp.bfloat16)] * turns
-        + [jax.ShapeDtypeStruct((slots, lane_count * row_count), jnp.float32)],
+        out_specs=[whole] * turns,
+        out_shape=[jax.ShapeDtypeStruct((block, lane_count * hidden_width), jnp.bfloat16)] * turns,
         compiler_params=params(4),
         name="pack",
     )(*[in_vmem(value) for value in (*mine, *theirs)])
-    received = meet(send)
-    own_matrix, _ = lax.optimization_barrier((own_matrix, place))
+    received = [meet(value, turn) for turn, value in enumerate(send)]
+    late_matrix, _ = lax.optimization_barrier((own_matrix, send[-1]))
     head = hidden_width * 3 // 4
-    first = pl.pallas_call(
-        fetch_kernel,
-        in_specs=[outside],
-        out_specs=whole,
-        out_shape=pltpu.VMEM((head, width), own_matrix.dtype),
+    first, place, split_place = pl.pallas_call(
+        functools.partial(fetch_kernel, node_count, lane_count, capacity, split),
+        in_specs=[outside] + [whole] * 4,
+        out_specs=[whole] * 3,
+        out_shape=[
+            pltpu.VMEM((head, width), own_matrix.dtype),
+            jax.ShapeDtypeStruct((slots, lane_count * row_count), jnp.float32),
+            jax.ShapeDtypeStruct((block, row_count), jnp.float32),
+        ],
         scratch_shapes=[pltpu.SemaphoreType.DMA],
-        compiler_params=params(1),
+        compiler_params=params(2),
         cost_estimate=pl.CostEstimate(flops=0, bytes_accessed=4 * head * width, transcendentals=0),
         name="fetch",
-    )(in_hbm(own_matrix))
+    )(in_hbm(late_matrix), *[in_vmem(value) for value in (*mine[1:3], *theirs[1:3])])
     own_part = pl.pallas_call(
         own_kernel,
         in_specs=[whole] * (turns + 1) + [outside],
@@ -311,29 +359,46 @@
         ],
         compiler_params=params(8),
         name="own",
-    )(*received, in_vmem(first), in_hbm(own_matrix))
+    )(*received, in_vmem(first), in_hbm(late_matrix))
+    pieces = [block] * split + [capacity] * lane_count + [block] * (turns - split - 1)
     output = pl.pallas_call(
         functools.partial(other_kernel, turns),
         in_specs=[whole] * (turns + 2),
-        out_specs=[whole] * turns,
-        out_shape=[jax.ShapeDtypeStruct((block, width), jnp.bfloat16)] * turns,
+        out_specs=[whole] * len(pieces),
+        out_shape=[jax.ShapeDtypeStruct((rows, width), jnp.bfloat16) for rows in pieces],
         compiler_params=params(2),
         name="other",
     )(*received, in_vmem(own_part), in_vmem(other_matrix))
-    returned = meet(output)
+    returned = [meet(value, turn) for turn, value in enumerate(output[:split])]
+    last = [meet(output[split + across], split, across) for across in range(lane_count)]
+    returned += [meet(value, turn) for turn, value in enumerate(output[split + lane_count :], split + 1)]
     query_latent, query_rope, cache_latent, cache_rope, cache_lengths, _ = lax.optimization_barrier(
         (query_latent, query_rope, cache_latent, cache_rope, cache_lengths, output[-1])
     )
     context = attend(query_latent, query_rope, cache_latent, cache_rope, cache_lengths)
     *returned, context = lax.optimization_barrier((*returned, context))
-    own, other = pl.pallas_call(
-        sum_kernel,
-        out_shape=[jax.ShapeDtypeStruct((row_count, width), jnp.float32)] * 2,
-        scratch_shapes=[pltpu.VMEM((slots, width), jnp.bfloat16)],
-        compiler_params=pltpu.CompilerParams(vmem_limit_bytes=8 * MIB),
+    tiles = width // 128
+    widths = [128 * ((i + 1) * tiles // 3 - i * tiles // 3) for i in range(3)]
+    own, *others = pl.pallas_call(
+        functools.partial(sum_kernel, split, len(widths)),
+        in_specs=[whole] * turns,
+        out_specs=[whole] * (1 + len(widths)),
+        out_shape=[jax.ShapeDtypeStruct((row_count, width), jnp.float32)]
+        + [jax.ShapeDtypeStruct((row_count, piece), jnp.bfloat16) for piece in widths],
+        scratch_shapes=[pltpu.VMEM((slots - block, width), jnp.bfloat16)],
+        compiler_params=params(8),
+        cost_estimate=pl.CostEstimate(flops=0, bytes_accessed=0, transcendentals=0),
         name="sum",
     )(place, *returned)
-    moe_out = (own + other_core(other)).astype(jnp.bfloat16)
+    others = [in_vmem(other_core(value)) for value in others]
+    moe_out = pl.pallas_call(
+        functools.partial(last_kernel, len(widths)),
+        in_specs=[whole] * (2 + len(widths) + lane_count),
+        out_specs=whole,
+        out_shape=jax.ShapeDtypeStruct((row_count, width), jnp.bfloat16),
+        compiler_params=params(2),
+        name="last",
+    )(in_vmem(own), split_place, *others, *[in_vmem(value) for value in last])
     return (moe_out, context)
 
 

time: 35.4 us -> 34.4 us (0.972)
  waiting for transfers between devices: 10.1 us -> 3.88 us
  starting transfers between devices: 13.2 us -> 18.4 us
  Pallas kernels: 10.1 us -> 10.8 us
  other arithmetic: 0.67 us -> 0 us
    ppermute x8 -> x9, waiting for transfers between devices: 8.75 us -> 2.49 us  [meet(): return lax.ppermute(value, ('node', 'lane'), pairs)]
    ppermute x8 -> x9, starting transfers between devices: 11.3 us -> 16.4 us  [meet(): return lax.ppermute(value, ('node', 'lane'), pairs)]
    pallas_call x2 -> x3, Pallas kernels: 2.81 us -> 3.71 us  [the longest x1 2.58 us: local(): pl.pallas_call(functools.partial(fetch_kernel, node_count, lane_count, ca...]
    convert_element_type x1 -> x0, other arithmetic: 0.67 us -> none  [local(): moe_out = (own + other_core(other)).astype(jnp.bfloat16)]
    ppermute x6 -> x8, starting transfers between devices: 1.92 us -> 2.03 us  [other_core(): return lax.ppermute(value, 'lane', [(0, 1), (1, 0)])]
    ppermute x6 -> x8, waiting for transfers between devices: 1.37 us -> 1.39 us  [other_core(): return lax.ppermute(value, 'lane', [(0, 1), (1, 0)])]
  transfers between devices with their start and end apart: 14 -> 17, of which waited for: 5 -> 4; matrix products, arithmetic and copies ran while one was open for 0% -> 1% of each run, Pallas kernels for 24% -> 25%
where the time goes in v4:
time: 34.4 us; the launch traced here: 34.2 us
  starting transfers between devices  18.4 us (53%)
  Pallas kernels  10.8 us (31%)
  waiting for transfers between devices  3.88 us (11%)
  between operations  0.82 us (2%)
    ppermute x9, starting transfers between devices, meet(): return lax.ppermute(value, ('node', 'lane'), pairs)  16.4 us
    pallas_call x1, Pallas kernels, local(): pl.pallas_call(functools.partial(fetch_kernel, node_count, lane_count, ca...  2.58 us
    ppermute x9, waiting for transfers between devices, meet(): return lax.ppermute(value, ('node', 'lane'), pairs)  2.49 us
    pallas_call x1, Pallas kernels, attend(): pl.pallas_call(attend_kernel, in_specs=[pl.BlockSpec(memory_space=pltpu.S...  2.22 us
    ppermute x8, starting transfers between devices, other_core(): return lax.ppermute(value, 'lane', [(0, 1), (1, 0)])  2.03 us
    pallas_call x1, Pallas kernels, local(): pl.pallas_call(own_kernel, in_specs=[whole] * (turns + 1) + [outside], ou...  1.96 us
    ppermute x8, waiting for transfers between devices, other_core(): return lax.ppermute(value, 'lane', [(0, 1), (1, 0)])  1.39 us
    pallas_call x1, Pallas kernels, local(): pl.pallas_call(functools.partial(other_kernel, turns), in_specs=[whole] *...  1.37 us
  transfers between devices with their start and end apart: 17, of which 4 were waited for; matrix products, arithmetic and copies ran while one was open for 1% of the time, Pallas kernels for 25%

profile of v4, /device:TPU:0, one launch (start us, length us, event | category | flops | bytes accessed | tf_op | source)
XLA Modules:
  0.0 34.2 jit_solution(553277984561874539)
XLA Ops:
  0.6 0.5 %collective-permute-start.3 = (bf16[128,1024]{1,0:T(8,128)(2,1)}, bf16[128,1024]{1,0:T(8,128)(2,1)S(1)}, u32[]{:S(2)}, u32[]{:S(2)}) collective-permute-start(bf16[128,1024]{1,0:T(8,128)(2,1)} %bitcast.8), channel_id=1, source_target_pairs={{0,1},{1,0},{2,3},{3,2},{4,5},{5,4},{6,7},{7,6},{8,9},{9,8},{10,11... | collective-permute-start | bytes 786440 | tf_op jit(solution)/shard_map/ppermute | solution.py:289
  1.1 0.1 collective-permute-start
  1.2 0.4 %collective-permute-start.2 = (s32[8,16]{1,0:T(8,128)}, s32[8,16]{1,0:T(8,128)S(1)}, u32[]{:S(2)}, u32[]{:S(2)}) collective-permute-start(s32[8,16]{1,0:T(8,128)} %bitcast.12), channel_id=1, source_target_pairs={{0,1},{1,0},{2,3},{3,2},{4,5},{5,4},{6,7},{7,6},{8,9},{9,8},{10,11... | collective-permute-start | bytes 1544 | tf_op jit(solution)/shard_map/ppermute | solution.py:289
  1.7 0.1 collective-permute-start.1
  1.7 1.0 %load.1 = (f32[8,16]{1,0:T(8,128)S(1)}, s32[4,16]{1,0:T(4,128)S(1)}, s32[8,16]{1,0:T(8,128)S(1)}, bf16[128,1024]{1,0:T(8,128)(2,1)S(1)}) custom-call(f32[8,16]{1,0:T(8,128)} %bitcast.11, s32[4,16]{1,0:T(4,128)} %bitcast.15, s32[8,16]{1,0:T(8,128)} %bitcast.13, bf16[128,1024]{1,0:T(8,128)(2,1)} %bitcast.9), custom_call_target="tpu_custom_call" | custom-call | tf_op jit(solution)/shard_map/load/pallas_call | solution.py:314
  2.8 0.2 collective-permute-done.1.refs_5_.refs_2_
  3.0 0.0 collective-permute-done.refs_4_
  3.0 0.0 collective-permute-done.2.refs_6_.refs_3_
  3.0 0.0 collective-permute-done.3.refs_7_
  3.0 0.3 collective-permute-start.8
  3.3 0.5 %pack.1 = (bf16[16,2048]{1,0:T(8,128)(2,1)S(1)}, bf16[16,2048]{1,0:T(8,128)(2,1)S(1)}, bf16[16,2048]{1,0:T(8,128)(2,1)S(1)}, bf16[16,2048]{1,0:T(8,128)(2,1)S(1)}) custom-call(f32[8,16]{1,0:T(8,128)S(1)} %get-tuple-element.33.refs_0_, s32[4,16]{1,0:T(4,128)S(1)} %get-tuple-element.34.refs_1_.refs_0_, s32[8,16]{1,0:T(8,128)S(1)} %get-tuple-element.35.refs_2_.refs_1_, ...), custom_call_target="tpu_custom_call" | custom-call | tf_op jit(solution)/shard_map/pack/pallas_call | solution.py:326
  3.9 5.0 %collective-permute-start.4 = (bf16[16,2048]{1,0:T(8,128)(2,1)S(1)}, bf16[16,2048]{1,0:T(8,128)(2,1)S(1)}, u32[]{:S(2)}, u32[]{:S(2)}) collective-permute-start(bf16[16,2048]{1,0:T(8,128)(2,1)S(1)} %get-tuple-element.40), channel_id=1, source_target_pairs={{0,12},{1,15},{2,14},{3,13},{4,8},{5,11},{6,10},{7,9},{8,4},{9,7},... | collective-permute-start | bytes 196616 | tf_op jit(solution)/shard_map/ppermute | solution.py:297
  8.8 0.0 collective-permute-start.5
  8.8 0.6 %collective-permute-start.6 = (bf16[16,2048]{1,0:T(8,128)(2,1)S(1)}, bf16[16,2048]{1,0:T(8,128)(2,1)S(1)}, u32[]{:S(2)}, u32[]{:S(2)}) collective-permute-start(bf16[16,2048]{1,0:T(8,128)(2,1)S(1)} %get-tuple-element.42), channel_id=1, source_target_pairs={{0,4},{1,7},{2,6},{3,5},{4,0},{5,3},{6,2},{7,1},{8,12},{9,15},{10,... | collective-permute-start | bytes 196616 | tf_op jit(solution)/shard_map/ppermute | solution.py:297
  9.5 0.7 %collective-permute-start.7 = (bf16[16,2048]{1,0:T(8,128)(2,1)S(1)}, bf16[16,2048]{1,0:T(8,128)(2,1)S(1)}, u32[]{:S(2)}, u32[]{:S(2)}) collective-permute-start(bf16[16,2048]{1,0:T(8,128)(2,1)S(1)} %get-tuple-element.37), channel_id=1, source_target_pairs={{0,0},{1,3},{2,2},{3,1},{4,4},{5,7},{6,6},{7,5},{8,8},{9,11},{10,1... | collective-permute-start | bytes 196616 | tf_op jit(solution)/shard_map/ppermute | solution.py:297
  10.1 2.6 %fetch.1 = (bf16[768,3584]{1,0:T(8,128)(2,1)S(1)}, f32[64,32]{1,0:T(8,128)S(1)}, f32[16,16]{1,0:T(8,128)S(1)}) custom-call(bf16[1024,3584]{1,0:T(8,128)(2,1)} %bitcast.6, s32[4,16]{1,0:T(4,128)S(1)} %get-tuple-element.34.refs_1_.refs_0_, s32[8,16]{1,0:T(8,128)S(1)} %get-tuple-element.35.refs_2_.refs_1_, s32[4,16]{1,0:T(4,128)S(1)} %collective-permute-done.1.refs_5_.refs_2_, ...), custom_call_target="tpu_custom_call" | custom-call | bytes 11010048 | tf_op jit(solution)/shard_map/fetch/pallas_call | solution.py:337
  12.7 0.0 collective-permute-done.4.refs_0_
  12.7 2.5 %collective-permute-done.5.refs_1_ = bf16[16,2048]{1,0:T(8,128)(2,1)S(1)} collective-permute-done((bf16[16,2048]{1,0:T(8,128)(2,1)S(1)}, bf16[16,2048]{1,0:T(8,128)(2,1)S(1)}, u32[]{:S(2)}, u32[]{:S(2)}) %collective-permute-start.5) | collective-permute-done | bytes 65568 | tf_op jit(solution)/shard_map/ppermute | solution.py:297
  15.2 0.0 collective-permute-done.6.refs_2_
  15.2 0.0 collective-permute-done.7.refs_3_
  15.2 2.0 %own.1.refs_4_ = f32[64,3584]{1,0:T(8,128)S(1)} custom-call(bf16[16,2048]{1,0:T(8,128)(2,1)S(1)} %collective-permute-done.4.refs_0_, bf16[16,2048]{1,0:T(8,128)(2,1)S(1)} %collective-permute-done.5.refs_1_, bf16[16,2048]{1,0:T(8,128)(2,1)S(1)} %collective-permute-done.6.refs_2_, bf16[16,2048]{1,0:T(8,128)(2,1)S(1)} %collective-permute-done.7.refs_3_, ...), custom_call_target="tpu_custom_call" | custom-call | tf_op jit(solution)/shard_map/own/pallas_call | solution.py:351
  17.2 0.0 copy-start.4
  17.2 0.0 copy-start
  17.2 0.0 copy-start.1
  17.2 0.0 copy-start.2
  17.2 0.0 copy-start.3
  17.2 0.0 collective-permute-done.8.refs_5_
  17.2 1.4 %other.1 = (bf16[16,3584]{1,0:T(8,128)(2,1)S(1)}, bf16[8,3584]{1,0:T(8,128)(2,1)S(1)}, bf16[8,3584]{1,0:T(8,128)(2,1)S(1)}, bf16[16,3584]{1,0:T(8,128)(2,1)S(1)}, bf16[16,3584]{1,0:T(8,128)(2,1)S(1)}) custom-call(bf16[16,2048]{1,0:T(8,128)(2,1)S(1)} %collective-permute-done.4.refs_0_, bf16[16,2048]{1,0:T(8,128)(2,1)S(1)} %collective-permute-done.5.refs_1_, ...), custom_call_target="tpu_custom_call" | custom-call | tf_op jit(solution)/shard_map/other/pallas_call | solution.py:364
  18.6 2.6 %collective-permute-start.9 = (bf16[16,3584]{1,0:T(8,128)(2,1)S(1)}, bf16[16,3584]{1,0:T(8,128)(2,1)S(1)}, u32[]{:S(2)}, u32[]{:S(2)}) collective-permute-start(bf16[16,3584]{1,0:T(8,128)(2,1)S(1)} %get-tuple-element.45), channel_id=1, source_target_pairs={{0,12},{1,15},{2,14},{3,13},{4,8},{5,11},{6,10},{7,9},{8,4},{9,7},... | collective-permute-start | bytes 344072 | tf_op jit(solution)/shard_map/ppermute | solution.py:297
  21.2 0.0 collective-permute-start.10
  21.2 0.7 %collective-permute-start.11 = (bf16[16,3584]{1,0:T(8,128)(2,1)S(1)}, bf16[16,3584]{1,0:T(8,128)(2,1)S(1)}, u32[]{:S(2)}, u32[]{:S(2)}) collective-permute-start(bf16[16,3584]{1,0:T(8,128)(2,1)S(1)} %get-tuple-element.47), channel_id=1, source_target_pairs={{0,0},{1,3},{2,2},{3,1},{4,4},{5,7},{6,6},{7,5},{8,8},{9,11},{10,1... | collective-permute-start | bytes 344072 | tf_op jit(solution)/shard_map/ppermute | solution.py:297
  21.9 1.9 %collective-permute-start.15 = (bf16[8,3584]{1,0:T(8,128)(2,1)S(1)}, bf16[8,3584]{1,0:T(8,128)(2,1)S(1)}, u32[]{:S(2)}, u32[]{:S(2)}) collective-permute-start(bf16[8,3584]{1,0:T(8,128)(2,1)S(1)} %get-tuple-element.61), channel_id=1, source_target_pairs={{0,8},{1,11},{2,10},{3,9},{4,12},{5,15},{6,14},{7,13},{8,0},{9,3},... | collective-permute-start | bytes 172040 | tf_op jit(solution)/shard_map/ppermute | solution.py:297
  23.8 5.0 %collective-permute-start.16 = (bf16[8,3584]{1,0:T(8,128)(2,1)S(1)}, bf16[8,3584]{1,0:T(8,128)(2,1)S(1)}, u32[]{:S(2)}, u32[]{:S(2)}) collective-permute-start(bf16[8,3584]{1,0:T(8,128)(2,1)S(1)} %get-tuple-element.62), channel_id=1, source_target_pairs={{0,9},{1,10},{2,11},{3,8},{4,13},{5,14},{6,15},{7,12},{8,1},{9,2},... | collective-permute-start | bytes 172040 | tf_op jit(solution)/shard_map/ppermute | solution.py:297
  28.8 0.0 copy-done.4
  28.8 0.2 reshape.11.rope_ref
  29.0 0.0 copy-done
  29.0 0.0 copy-done.1
  29.0 0.0 copy-done.2
  29.0 0.0 copy-done.3
  29.0 2.2 %attend.1 = bf16[8,64,512]{2,1,0:T(8,128)(2,1)} custom-call(s32[8]{0:T(128)S(1)} %copy-done.3, bf16[8,64,512]{2,1,0:T(8,128)(2,1)S(1)} %copy-done.1, bf16[8,64,64]{2,1,0:T(8,128)(2,1)S(1)} %reshape.11.rope_ref, bf16[8,128,512]{2,1,0:T(8,128)(2,1)S(1)} %copy-done, bf16[8,64,128]{2,1,0:T(8,128)(2,1)S(1)} %copy-done.2), custom_call_target="tpu_custom_call" | custom-call | tf_op jit(solution)/shard_map/attend/pallas_call | solution.py:44
  31.2 0.0 collective-permute-done.9.refs_0_
  31.2 0.0 collective-permute-done.10.refs_1_
  31.2 0.0 collective-permute-done.11.refs_2_
  31.2 0.2 sum.1
  31.5 0.1 collective-permute-start.14
  31.6 0.5 %collective-permute-start.12 = (bf16[16,1152]{1,0:T(8,128)(2,1)S(1)}, bf16[16,1152]{1,0:T(8,128)(2,1)S(1)}, u32[]{:S(2)}, u32[]{:S(2)}) collective-permute-start(bf16[16,1152]{1,0:T(8,128)(2,1)S(1)} %get-tuple-element.58), channel_id=1, source_target_pairs={{0,1},{1,0},{2,3},{3,2},{4,5},{5,4},{6,7},{7,6},{8,9},{9,8},{10,11... | collective-permute-start | bytes 110600 | tf_op jit(solution)/shard_map/ppermute | solution.py:289
  32.1 0.1 collective-permute-start.13
  32.1 0.0 collective-permute-done.15.refs_3_
  32.1 0.0 collective-permute-done.16.refs_4_
  32.1 0.8 %collective-permute-done.12.refs_0_ = bf16[16,1152]{1,0:T(8,128)(2,1)S(1)} collective-permute-done((bf16[16,1152]{1,0:T(8,128)(2,1)S(1)}, bf16[16,1152]{1,0:T(8,128)(2,1)S(1)}, u32[]{:S(2)}, u32[]{:S(2)}) %collective-permute-start.12) | collective-permute-done | bytes 36896 | tf_op jit(solution)/shard_map/ppermute | solution.py:289
  32.9 0.3 %collective-permute-done.13.refs_1_ = bf16[16,1152]{1,0:T(8,128)(2,1)S(1)} collective-permute-done((bf16[16,1152]{1,0:T(8,128)(2,1)S(1)}, bf16[16,1152]{1,0:T(8,128)(2,1)S(1)}, u32[]{:S(2)}, u32[]{:S(2)}) %collective-permute-start.13) | collective-permute-done | bytes 36896 | tf_op jit(solution)/shard_map/ppermute | solution.py:289
  33.3 0.0 collective-permute-done.14.refs_2_
  33.3 0.9 %last.1 = bf16[16,3584]{1,0:T(8,128)(2,1)} custom-call(f32[16,3584]{1,0:T(8,128)S(1)} %get-tuple-element.56.own_ref, f32[16,16]{1,0:T(8,128)S(1)} %get-tuple-element.57.place_ref, bf16[16,1152]{1,0:T(8,128)(2,1)S(1)} %collective-permute-done.12.refs_0_, bf16[16,1152]{1,0:T(8,128)(2,1)S(1)} %collective-permute-done.13.refs_1_, ...), custom_call_target="tpu_custom_call" | custom-call | tf_op jit(solution)/shard_map/last/pallas_call | solution.py:394
Async XLA Ops:
  0.6 2.4 %collective-permute-start.3 = (bf16[128,1024]{1,0:T(8,128)(2,1)}, bf16[128,1024]{1,0:T(8,128)(2,1)S(1)}, u32[]{:S(2)}, u32[]{:S(2)}) collective-permute-start(bf16[128,1024]{1,0:T(8,128)(2,1)} %bitcast.8), channel_id=1, source_target_pairs={{0,1},{1,0},{2,3},{3,2},{4,5},{5,4},{6,7},{7,6},{8,9},{9,8},{10,11... | collective-permute-start | bytes 786440 | tf_op jit(solution)/shard_map/ppermute | solution.py:289
  1.1 1.9 %collective-permute-start = (f32[8,16]{1,0:T(8,128)}, f32[8,16]{1,0:T(8,128)S(1)}, u32[]{:S(2)}, u32[]{:S(2)}) collective-permute-start(f32[8,16]{1,0:T(8,128)} %bitcast.10), channel_id=1, source_target_pairs={{0,1},{1,0},{2,3},{3,2},{4,5},{5,4},{6,7},{7,6},{8,9},{9,8},{10,11... | collective-permute-start | bytes 1544 | tf_op jit(solution)/shard_map/ppermute | solution.py:289
  1.2 1.8 %collective-permute-start.2 = (s32[8,16]{1,0:T(8,128)}, s32[8,16]{1,0:T(8,128)S(1)}, u32[]{:S(2)}, u32[]{:S(2)}) collective-permute-start(s32[8,16]{1,0:T(8,128)} %bitcast.12), channel_id=1, source_target_pairs={{0,1},{1,0},{2,3},{3,2},{4,5},{5,4},{6,7},{7,6},{8,9},{9,8},{10,11... | collective-permute-start | bytes 1544 | tf_op jit(solution)/shard_map/ppermute | solution.py:289
  1.7 1.4 %collective-permute-start.1 = (s32[4,16]{1,0:T(4,128)}, s32[4,16]{1,0:T(4,128)S(1)}, u32[]{:S(2)}, u32[]{:S(2)}) collective-permute-start(s32[4,16]{1,0:T(4,128)} %bitcast.14), channel_id=1, source_target_pairs={{0,1},{1,0},{2,3},{3,2},{4,5},{5,4},{6,7},{7,6},{8,9},{9,8},{10,11... | collective-permute-start | bytes 776 | tf_op jit(solution)/shard_map/ppermute | solution.py:289
  3.0 14.2 %collective-permute-start.8 = (bf16[1024,3584]{1,0:T(8,128)(2,1)}, bf16[1024,3584]{1,0:T(8,128)(2,1)S(1)}, u32[]{:S(2)}, u32[]{:S(2)}) collective-permute-start(bf16[1024,3584]{1,0:T(8,128)(2,1)} %bitcast.5), channel_id=1, source_target_pairs={{0,1},{1,0},{2,3},{3,2},{4,5},{5,4},{6,7},{7,6},{8,9},{9,8},{10,11... | collective-permute-start | bytes 22020104 | tf_op jit(solution)/shard_map/ppermute | solution.py:289
  3.9 8.9 %collective-permute-start.4 = (bf16[16,2048]{1,0:T(8,128)(2,1)S(1)}, bf16[16,2048]{1,0:T(8,128)(2,1)S(1)}, u32[]{:S(2)}, u32[]{:S(2)}) collective-permute-start(bf16[16,2048]{1,0:T(8,128)(2,1)S(1)} %get-tuple-element.40), channel_id=1, source_target_pairs={{0,12},{1,15},{2,14},{3,13},{4,8},{5,11},{6,10},{7,9},{8,4},{9,7},... | collective-permute-start | bytes 196616 | tf_op jit(solution)/shard_map/ppermute | solution.py:297
  8.8 6.4 %collective-permute-start.5 = (bf16[16,2048]{1,0:T(8,128)(2,1)S(1)}, bf16[16,2048]{1,0:T(8,128)(2,1)S(1)}, u32[]{:S(2)}, u32[]{:S(2)}) collective-permute-start(bf16[16,2048]{1,0:T(8,128)(2,1)S(1)} %get-tuple-element.41), channel_id=1, source_target_pairs={{0,8},{1,11},{2,10},{3,9},{4,12},{5,15},{6,14},{7,13},{8,0},{9,3},... | collective-permute-start | bytes 196616 | tf_op jit(solution)/shard_map/ppermute | solution.py:297
  8.8 6.4 %collective-permute-start.6 = (bf16[16,2048]{1,0:T(8,128)(2,1)S(1)}, bf16[16,2048]{1,0:T(8,128)(2,1)S(1)}, u32[]{:S(2)}, u32[]{:S(2)}) collective-permute-start(bf16[16,2048]{1,0:T(8,128)(2,1)S(1)} %get-tuple-element.42), channel_id=1, source_target_pairs={{0,4},{1,7},{2,6},{3,5},{4,0},{5,3},{6,2},{7,1},{8,12},{9,15},{10,... | collective-permute-start | bytes 196616 | tf_op jit(solution)/shard_map/ppermute | solution.py:297
  9.5 5.7 %collective-permute-start.7 = (bf16[16,2048]{1,0:T(8,128)(2,1)S(1)}, bf16[16,2048]{1,0:T(8,128)(2,1)S(1)}, u32[]{:S(2)}, u32[]{:S(2)}) collective-permute-start(bf16[16,2048]{1,0:T(8,128)(2,1)S(1)} %get-tuple-element.37), channel_id=1, source_target_pairs={{0,0},{1,3},{2,2},{3,1},{4,4},{5,7},{6,6},{7,5},{8,8},{9,11},{10,1... | collective-permute-start | bytes 196616 | tf_op jit(solution)/shard_map/ppermute | solution.py:297
  17.2 11.6 %copy-start.4 = (bf16[8,4096]{1,0:T(8,128)(2,1)S(1)}, bf16[8,4096]{1,0:T(8,128)(2,1)}, u32[]{:S(2)}) copy-start(bf16[8,4096]{1,0:T(8,128)(2,1)} %param.16) | copy-start | bytes 196612
  17.2 11.8 %copy-start = (bf16[8,128,512]{2,1,0:T(8,128)(2,1)S(1)}, bf16[8,128,512]{2,1,0:T(8,128)(2,1)}, u32[]{:S(2)}) copy-start(bf16[8,128,512]{2,1,0:T(8,128)(2,1)} %keys_ref) | copy-start | bytes 3145732
  17.2 11.8 %copy-start.1 = (bf16[8,64,512]{2,1,0:T(8,128)(2,1)S(1)}, bf16[8,64,512]{2,1,0:T(8,128)(2,1)}, u32[]{:S(2)}) copy-start(bf16[8,64,512]{2,1,0:T(8,128)(2,1)} %latent_ref) | copy-start | bytes 1572868
  17.2 11.8 %copy-start.2 = (bf16[8,64,128]{2,1,0:T(8,128)(2,1)S(1)}, bf16[8,64,128]{2,1,0:T(8,128)(2,1)}, u32[]{:S(2)}) copy-start(bf16[8,64,128]{2,1,0:T(8,128)(2,1)} %rope_keys_ref) | copy-start | bytes 393220
  17.2 11.8 %copy-start.3 = (s32[8]{0:T(128)S(1)}, s32[8]{0:T(128)}, u32[]{:S(2)}) copy-start(s32[8]{0:T(128)} %lengths_ref) | copy-start | bytes 100
  18.6 12.6 %collective-permute-start.9 = (bf16[16,3584]{1,0:T(8,128)(2,1)S(1)}, bf16[16,3584]{1,0:T(8,128)(2,1)S(1)}, u32[]{:S(2)}, u32[]{:S(2)}) collective-permute-start(bf16[16,3584]{1,0:T(8,128)(2,1)S(1)} %get-tuple-element.45), channel_id=1, source_target_pairs={{0,12},{1,15},{2,14},{3,13},{4,8},{5,11},{6,10},{7,9},{8,4},{9,7},... | collective-permute-start | bytes 344072 | tf_op jit(solution)/shard_map/ppermute | solution.py:297
  21.2 10.0 %collective-permute-start.10 = (bf16[16,3584]{1,0:T(8,128)(2,1)S(1)}, bf16[16,3584]{1,0:T(8,128)(2,1)S(1)}, u32[]{:S(2)}, u32[]{:S(2)}) collective-permute-start(bf16[16,3584]{1,0:T(8,128)(2,1)S(1)} %get-tuple-element.46), channel_id=1, source_target_pairs={{0,4},{1,7},{2,6},{3,5},{4,0},{5,3},{6,2},{7,1},{8,12},{9,15},{10,... | collective-permute-start | bytes 344072 | tf_op jit(solution)/shard_map/ppermute | solution.py:297
  21.2 10.0 %collective-permute-start.11 = (bf16[16,3584]{1,0:T(8,128)(2,1)S(1)}, bf16[16,3584]{1,0:T(8,128)(2,1)S(1)}, u32[]{:S(2)}, u32[]{:S(2)}) collective-permute-start(bf16[16,3584]{1,0:T(8,128)(2,1)S(1)} %get-tuple-element.47), channel_id=1, source_target_pairs={{0,0},{1,3},{2,2},{3,1},{4,4},{5,7},{6,6},{7,5},{8,8},{9,11},{10,1... | collective-permute-start | bytes 344072 | tf_op jit(solution)/shard_map/ppermute | solution.py:297
  21.9 10.2 %collective-permute-start.15 = (bf16[8,3584]{1,0:T(8,128)(2,1)S(1)}, bf16[8,3584]{1,0:T(8,128)(2,1)S(1)}, u32[]{:S(2)}, u32[]{:S(2)}) collective-permute-start(bf16[8,3584]{1,0:T(8,128)(2,1)S(1)} %get-tuple-element.61), channel_id=1, source_target_pairs={{0,8},{1,11},{2,10},{3,9},{4,12},{5,15},{6,14},{7,13},{8,0},{9,3},... | collective-permute-start | bytes 172040 | tf_op jit(solution)/shard_map/ppermute | solution.py:297
  23.8 8.3 %collective-permute-start.16 = (bf16[8,3584]{1,0:T(8,128)(2,1)S(1)}, bf16[8,3584]{1,0:T(8,128)(2,1)S(1)}, u32[]{:S(2)}, u32[]{:S(2)}) collective-permute-start(bf16[8,3584]{1,0:T(8,128)(2,1)S(1)} %get-tuple-element.62), channel_id=1, source_target_pairs={{0,9},{1,10},{2,11},{3,8},{4,13},{5,14},{6,15},{7,12},{8,1},{9,2},... | collective-permute-start | bytes 172040 | tf_op jit(solution)/shard_map/ppermute | solution.py:297
  31.5 1.8 %collective-permute-start.14 = (bf16[16,1280]{1,0:T(8,128)(2,1)S(1)}, bf16[16,1280]{1,0:T(8,128)(2,1)S(1)}, u32[]{:S(2)}, u32[]{:S(2)}) collective-permute-start(bf16[16,1280]{1,0:T(8,128)(2,1)S(1)} %get-tuple-element.60), channel_id=1, source_target_pairs={{0,1},{1,0},{2,3},{3,2},{4,5},{5,4},{6,7},{7,6},{8,9},{9,8},{10,11... | collective-permute-start | bytes 122888 | tf_op jit(solution)/shard_map/ppermute | solution.py:289
  31.6 1.4 %collective-permute-start.12 = (bf16[16,1152]{1,0:T(8,128)(2,1)S(1)}, bf16[16,1152]{1,0:T(8,128)(2,1)S(1)}, u32[]{:S(2)}, u32[]{:S(2)}) collective-permute-start(bf16[16,1152]{1,0:T(8,128)(2,1)S(1)} %get-tuple-element.58), channel_id=1, source_target_pairs={{0,1},{1,0},{2,3},{3,2},{4,5},{5,4},{6,7},{7,6},{8,9},{9,8},{10,11... | collective-permute-start | bytes 110600 | tf_op jit(solution)/shard_map/ppermute | solution.py:289
  32.1 1.2 %collective-permute-start.13 = (bf16[16,1152]{1,0:T(8,128)(2,1)S(1)}, bf16[16,1152]{1,0:T(8,128)(2,1)S(1)}, u32[]{:S(2)}, u32[]{:S(2)}) collective-permute-start(bf16[16,1152]{1,0:T(8,128)(2,1)S(1)} %get-tuple-element.59), channel_id=1, source_target_pairs={{0,1},{1,0},{2,3},{3,2},{4,5},{5,4},{6,7},{7,6},{8,9},{9,8},{10,11... | collective-permute-start | bytes 110600 | tf_op jit(solution)/shard_map/ppermute | solution.py:289

commit v5 on v4

--- a/solution.py
+++ b/solution.py
@@ -18,12 +18,27 @@
 
 def attend_kernel(lengths_ref, latent_ref, rope_ref, keys_ref, rope_keys_ref, out_ref):
     row_count, head_count, _ = latent_ref.shape
+    rope_width, position_count = rope_keys_ref.shape[1:]
+    lanes = max(128, rope_width)
+    heads = lanes // rope_width
+    groups = rope_ref.shape[1] // lanes
+    rope = rope_ref[...].astype(jnp.float32)
+    rope = jnp.concatenate([rope[:, i * lanes : (i + 1) * lanes] for i in range(groups)], axis=0)
+    shape = (row_count * head_count, groups * row_count)
+    head = lax.rem(iota(shape, 0), head_count)
+    picked = iota(shape, 1) == head // heads * row_count + iota(shape, 0) // head_count
+    rope = exact(jnp.where(picked, 1.0, 0.0), rope)
+    kept = iota(rope.shape, 1) // rope_width == lax.rem(iota(rope.shape, 0), heads)
+    rope = jnp.where(kept, rope, 0.0).astype(jnp.bfloat16)
     scores = []
     for row in range(row_count):
         score = lax.dot_general(
             latent_ref[row], keys_ref[row], (((1,), (1,)), ((), ())), preferred_element_type=jnp.float32
         )
-        score = score + jnp.dot(rope_ref[row], rope_keys_ref[row], preferred_element_type=jnp.float32)
+        rope_keys = jnp.concatenate([rope_keys_ref[row]] * heads, axis=0)
+        score = score + jnp.dot(
+            rope[row * head_count : (row + 1) * head_count], rope_keys, preferred_element_type=jnp.float32
+        )
         valid = iota(score.shape, 1) < lengths_ref[row]
         scores.append(jnp.where(valid, score * score_scale, -jnp.inf))
     scores = jnp.concatenate(scores, axis=0)
@@ -37,19 +52,14 @@
 
 
 def attend(query_latent, query_rope, cache_latent, cache_rope, cache_lengths):
-    row_count, head_count, latent_width = query_latent.shape
-    rope_width, position_count = cache_rope.shape[1:]
-    rope_query = query_rope.reshape(row_count, head_count, rope_width)
-    products = head_count * position_count * (2 * latent_width + rope_width)
     return pl.pallas_call(
         attend_kernel,
         in_specs=[pl.BlockSpec(memory_space=pltpu.SMEM)] + [pl.BlockSpec(memory_space=pltpu.VMEM)] * 4,
         out_specs=pl.BlockSpec(memory_space=pltpu.VMEM),
         out_shape=jax.ShapeDtypeStruct(query_latent.shape, jnp.bfloat16),
         compiler_params=pltpu.CompilerParams(vmem_limit_bytes=8 * MIB),
-        cost_estimate=pl.CostEstimate(flops=0, bytes_accessed=0, transcendentals=0),
         name="attend",
-    )(cache_lengths, query_latent, rope_query, cache_latent, cache_rope)
+    )(cache_lengths, query_latent, query_rope, cache_latent, cache_rope)
 
 
 def iota(shape, dim):
@@ -69,10 +79,16 @@
 
 
 def turn_of(node_count, lane_count, lane, number):
-    return jnp.where(number % lane_count == lane, (node_count - 1 - number) // lane_count, -1)
+    far = node_count // lane_count // 2
+    turn = (node_count - 1 - number) // lane_count
+    turn = jnp.where((lane == 0) & (turn < far), far - 1 - turn, turn)
+    return jnp.where(number % lane_count == lane, turn, -1)
 
 
 def number_of(node_count, lane_count, lane, turn):
+    far = node_count // lane_count // 2
+    if turn < far:
+        turn = jnp.where(lane == 0, far - 1 - turn, turn) if isinstance(lane, jax.Array) else (turn, far - 1 - turn)[lane == 0]
     return node_count - lane_count * (turn + 1) + lane
 
 
@@ -155,10 +171,8 @@
             send_ref[:, columns] = parts[q][turn * block : (turn + 1) * block].astype(jnp.bfloat16)
 
 
-def fetch_kernel(node_count, lane_count, capacity, split, matrix_ref, *refs):
-    *refs, out_ref, place_ref, split_ref, sem = refs
-    copy = pltpu.make_async_copy(matrix_ref.at[pl.ds(0, out_ref.shape[0])], out_ref, sem)
-    copy.start()
+def place_kernel(node_count, lane_count, capacity, split, *refs):
+    *refs, place_ref, split_ref = refs
     pick_count, row_count = refs[1].shape
     spread = spread_of(pick_count, row_count)
     items = pick_count * row_count
@@ -186,27 +200,15 @@
                 split_ref[q * capacity : (q + 1) * capacity, :] = marked(
                     iota((capacity, items), 0) == jnp.where(there, slot, -1)
                 )
-    copy.wait()
 
 
 def own_kernel(*refs):
-    *received_refs, first_ref, matrix_ref, out_ref, second_ref, sem = refs
+    *received_refs, matrix_ref, out_ref = refs
     depth, width = matrix_ref.shape
-    head = first_ref.shape[0]
-    copy = pltpu.make_async_copy(matrix_ref.at[pl.ds(head, depth - head)], second_ref, sem)
-    copy.start()
     rows = jnp.concatenate([received_ref[:, :depth] for received_ref in received_refs], axis=0)
     for start in range(0, width, TILE):
         columns = slice(start, start + TILE)
-        out_ref[:, columns] = jnp.dot(
-            rows[:, :head], first_ref[:, columns], preferred_element_type=jnp.float32
-        )
-    copy.wait()
-    for start in range(0, width, TILE):
-        columns = slice(start, start + TILE)
-        out_ref[:, columns] += jnp.dot(
-            rows[:, head:], second_ref[:, columns], preferred_element_type=jnp.float32
-        )
+        out_ref[:, columns] = jnp.dot(rows, matrix_ref[:, columns], preferred_element_type=jnp.float32)
 
 
 def other_kernel(turns, *refs):
@@ -329,37 +331,23 @@
         out_specs=[whole] * turns,
         out_shape=[jax.ShapeDtypeStruct((block, lane_count * hidden_width), jnp.bfloat16)] * turns,
         compiler_params=params(4),
+        cost_estimate=pl.CostEstimate(flops=6 * 10**9, bytes_accessed=0, transcendentals=0),
         name="pack",
     )(*[in_vmem(value) for value in (*mine, *theirs)])
     received = [meet(value, turn) for turn, value in enumerate(send)]
-    late_matrix, _ = lax.optimization_barrier((own_matrix, send[-1]))
-    head = hidden_width * 3 // 4
-    first, place, split_place = pl.pallas_call(
-        functools.partial(fetch_kernel, node_count, lane_count, capacity, split),
-        in_specs=[outside] + [whole] * 4,
-        out_specs=[whole] * 3,
-        out_shape=[
-            pltpu.VMEM((head, width), own_matrix.dtype),
-            jax.ShapeDtypeStruct((slots, lane_count * row_count), jnp.float32),
-            jax.ShapeDtypeStruct((block, row_count), jnp.float32),
-        ],
-        scratch_shapes=[pltpu.SemaphoreType.DMA],
-        compiler_params=params(2),
-        cost_estimate=pl.CostEstimate(flops=0, bytes_accessed=4 * head * width, transcendentals=0),
-        name="fetch",
-    )(in_hbm(late_matrix), *[in_vmem(value) for value in (*mine[1:3], *theirs[1:3])])
+    *attention, _ = lax.optimization_barrier(
+        (query_latent, query_rope, cache_latent, cache_rope, cache_lengths, send[-1])
+    )
+    context = attend(*attention)
+    *received, context = lax.optimization_barrier((*received, context))
     own_part = pl.pallas_call(
         own_kernel,
-        in_specs=[whole] * (turns + 1) + [outside],
+        in_specs=[whole] * (turns + 1),
         out_specs=whole,
         out_shape=jax.ShapeDtypeStruct((slots, width), jnp.float32),
-        scratch_shapes=[
-            pltpu.VMEM((hidden_width - head, width), own_matrix.dtype),
-            pltpu.SemaphoreType.DMA,
-        ],
-        compiler_params=params(8),
+        compiler_params=params(2),
         name="own",
-    )(*received, in_vmem(first), in_hbm(late_matrix))
+    )(*received, in_vmem(own_matrix))
     pieces = [block] * split + [capacity] * lane_count + [block] * (turns - split - 1)
     output = pl.pallas_call(
         functools.partial(other_kernel, turns),
@@ -372,11 +360,18 @@
     returned = [meet(value, turn) for turn, value in enumerate(output[:split])]
     last = [meet(output[split + across], split, across) for across in range(lane_count)]
     returned += [meet(value, turn) for turn, value in enumerate(output[split + lane_count :], split + 1)]
-    query_latent, query_rope, cache_latent, cache_rope, cache_lengths, _ = lax.optimization_barrier(
-        (query_latent, query_rope, cache_latent, cache_rope, cache_lengths, output[-1])
-    )
-    context = attend(query_latent, query_rope, cache_latent, cache_rope, cache_lengths)
-    *returned, context = lax.optimization_barrier((*returned, context))
+    late, _ = lax.optimization_barrier((mine[1], output[-1]))
+    place, split_place = pl.pallas_call(
+        functools.partial(place_kernel, node_count, lane_count, capacity, split),
+        in_specs=[whole] * 4,
+        out_specs=[whole] * 2,
+        out_shape=[
+            jax.ShapeDtypeStruct((slots, lane_count * row_count), jnp.float32),
+            jax.ShapeDtypeStruct((block, row_count), jnp.float32),
+        ],
+        compiler_params=params(2),
+        name="place",
+    )(*[in_vmem(value) for value in (late, mine[2], *theirs[1:3])])
     tiles = width // 128
     widths = [128 * ((i + 1) * tiles // 3 - i * tiles // 3) for i in range(3)]
     own, *others = pl.pallas_call(

time: 34.4 us -> 33.4 us (0.971)
  Pallas kernels: 10.8 us -> 8.5 us
  starting transfers between devices: 18.4 us -> 19.7 us
    pallas_call x2, Pallas kernels: 4.55 us -> 2.05 us  [the longest x1 1.37 us: local(): pl.pallas_call(own_kernel, in_specs=[whole] * (turns + 1), out_specs=whol...]
    ppermute x9, starting transfers between devices: 16.4 us -> 17.7 us  [meet(): return lax.ppermute(value, ('node', 'lane'), pairs)]
    ppermute x9, waiting for transfers between devices: 2.49 us -> 2.94 us  [meet(): return lax.ppermute(value, ('node', 'lane'), pairs)]
  transfers between devices with their start and end apart: 17 -> 17, of which waited for: 4 -> 6; matrix products, arithmetic and copies ran while one was open for 1% -> 0% of each run, Pallas kernels for 25% -> 19%
where the time goes in v5:
time: 33.4 us; the launch traced here: 33.2 us
  starting transfers between devices  19.7 us (59%)
  Pallas kernels  8.5 us (25%)
  waiting for transfers between devices  4.11 us (12%)
  between operations  0.82 us (2%)
    ppermute x9, starting transfers between devices, meet(): return lax.ppermute(value, ('node', 'lane'), pairs)  17.7 us
    ppermute x9, waiting for transfers between devices, meet(): return lax.ppermute(value, ('node', 'lane'), pairs)  2.94 us
    pallas_call x1, Pallas kernels, attend(): pl.pallas_call(attend_kernel, in_specs=[pl.BlockSpec(memory_space=pltpu.S...  2.36 us
    ppermute x8, starting transfers between devices, other_core(): return lax.ppermute(value, 'lane', [(0, 1), (1, 0)])  2.03 us
    pallas_call x1, Pallas kernels, local(): pl.pallas_call(functools.partial(other_kernel, turns), in_specs=[whole] *...  1.38 us
    pallas_call x1, Pallas kernels, local(): pl.pallas_call(own_kernel, in_specs=[whole] * (turns + 1), out_specs=whol...  1.37 us
    ppermute x8, waiting for transfers between devices, other_core(): return lax.ppermute(value, 'lane', [(0, 1), (1, 0)])  1.17 us
    pallas_call x1, Pallas kernels, local(): pl.pallas_call(load_kernel, in_specs=[outside] * 4, out_specs=[whole] * 4...  1.03 us
  transfers between devices with their start and end apart: 17, of which 6 were waited for; matrix products, arithmetic and copies ran while one was open for 0% of the time, Pallas kernels for 19%

profile of v5, /device:TPU:0, one launch (start us, length us, event | category | flops | bytes accessed | tf_op | source)
XLA Modules:
  0.0 33.2 jit_solution(12761959928019754615)
XLA Ops:
  0.6 0.5 %collective-permute-start.3 = (bf16[128,1024]{1,0:T(8,128)(2,1)}, bf16[128,1024]{1,0:T(8,128)(2,1)S(1)}, u32[]{:S(2)}, u32[]{:S(2)}) collective-permute-start(bf16[128,1024]{1,0:T(8,128)(2,1)} %bitcast.9), channel_id=1, source_target_pairs={{0,1},{1,0},{2,3},{3,2},{4,5},{5,4},{6,7},{7,6},{8,9},{9,8},{10,11... | collective-permute-start | bytes 786440 | tf_op jit(solution)/shard_map/ppermute | solution.py:291
  1.1 0.1 collective-permute-start
  1.2 0.4 %collective-permute-start.2 = (s32[8,16]{1,0:T(8,128)}, s32[8,16]{1,0:T(8,128)S(1)}, u32[]{:S(2)}, u32[]{:S(2)}) collective-permute-start(s32[8,16]{1,0:T(8,128)} %bitcast.13), channel_id=1, source_target_pairs={{0,1},{1,0},{2,3},{3,2},{4,5},{5,4},{6,7},{7,6},{8,9},{9,8},{10,11... | collective-permute-start | bytes 1544 | tf_op jit(solution)/shard_map/ppermute | solution.py:291
  1.7 0.1 collective-permute-start.1
  1.7 1.0 %load.1 = (f32[8,16]{1,0:T(8,128)S(1)}, s32[4,16]{1,0:T(4,128)S(1)}, s32[8,16]{1,0:T(8,128)S(1)}, bf16[128,1024]{1,0:T(8,128)(2,1)S(1)}) custom-call(f32[8,16]{1,0:T(8,128)} %bitcast.12, s32[4,16]{1,0:T(4,128)} %bitcast.16, s32[8,16]{1,0:T(8,128)} %bitcast.14, bf16[128,1024]{1,0:T(8,128)(2,1)} %bitcast.10), custom_call_target="tpu_custom_call" | custom-call | tf_op jit(solution)/shard_map/load/pallas_call | solution.py:316
  2.8 0.2 collective-permute-done.1.refs_5_.refs_2_
  3.0 0.0 collective-permute-done.refs_4_
  3.0 0.0 collective-permute-done.2.refs_6_.refs_3_
  3.0 0.0 collective-permute-done.3.refs_7_
  3.0 0.3 collective-permute-start.8
  3.3 0.0 slice-start
  3.3 0.0 copy-start
  3.3 0.0 copy-start.1
  3.3 0.0 copy-start.2
  3.3 0.0 copy-start.3
  3.3 0.0 copy-start.4
  3.4 0.0 slice-start.1
  3.4 0.5 %pack.1 = (bf16[16,2048]{1,0:T(8,128)(2,1)S(1)}, bf16[16,2048]{1,0:T(8,128)(2,1)S(1)}, bf16[16,2048]{1,0:T(8,128)(2,1)S(1)}, bf16[16,2048]{1,0:T(8,128)(2,1)S(1)}) custom-call(f32[8,16]{1,0:T(8,128)S(1)} %get-tuple-element.34.refs_0_, s32[4,16]{1,0:T(4,128)S(1)} %get-tuple-element.52.refs_1_.refs_0_, s32[8,16]{1,0:T(8,128)S(1)} %get-tuple-element.35.refs_2_.refs_1_, ...), custom_call_target="tpu_custom_call" | custom-call | flops 6000000000 | tf_op jit(solution)/shard_map/pack/pallas_call | solution.py:328
  3.9 3.9 %collective-permute-start.4 = (bf16[16,2048]{1,0:T(8,128)(2,1)S(1)}, bf16[16,2048]{1,0:T(8,128)(2,1)S(1)}, u32[]{:S(2)}, u32[]{:S(2)}) collective-permute-start(bf16[16,2048]{1,0:T(8,128)(2,1)S(1)} %get-tuple-element.37), channel_id=1, source_target_pairs={{0,8},{1,15},{2,10},{3,13},{4,12},{5,11},{6,14},{7,9},{8,0},{9,7},... | collective-permute-start | bytes 196616 | tf_op jit(solution)/shard_map/ppermute | solution.py:299
  7.9 1.4 %collective-permute-start.5 = (bf16[16,2048]{1,0:T(8,128)(2,1)S(1)}, bf16[16,2048]{1,0:T(8,128)(2,1)S(1)}, u32[]{:S(2)}, u32[]{:S(2)}) collective-permute-start(bf16[16,2048]{1,0:T(8,128)(2,1)S(1)} %get-tuple-element.38), channel_id=1, source_target_pairs={{0,12},{1,11},{2,14},{3,9},{4,8},{5,15},{6,10},{7,13},{8,4},{9,3},... | collective-permute-start | bytes 196616 | tf_op jit(solution)/shard_map/ppermute | solution.py:299
  9.2 0.2 collective-permute-start.6
  9.4 0.7 %collective-permute-start.7 = (bf16[16,2048]{1,0:T(8,128)(2,1)S(1)}, bf16[16,2048]{1,0:T(8,128)(2,1)S(1)}, u32[]{:S(2)}, u32[]{:S(2)}) collective-permute-start(bf16[16,2048]{1,0:T(8,128)(2,1)S(1)} %get-tuple-element.40), channel_id=1, source_target_pairs={{0,0},{1,3},{2,2},{3,1},{4,4},{5,7},{6,6},{7,5},{8,8},{9,11},{10,1... | collective-permute-start | bytes 196616 | tf_op jit(solution)/shard_map/ppermute | solution.py:299
  10.1 0.0 copy-done
  10.1 0.0 copy-done.1
  10.1 0.0 copy-done.2
  10.1 0.0 copy-done.3
  10.1 0.0 copy-done.4
  10.2 2.4 %attend.1 = bf16[8,64,512]{2,1,0:T(8,128)(2,1)} custom-call(s32[8]{0:T(128)S(1)} %copy-done.4, bf16[8,64,512]{2,1,0:T(8,128)(2,1)S(1)} %copy-done.1, bf16[8,4096]{1,0:T(8,128)(2,1)S(1)} %copy-done.3, bf16[8,128,512]{2,1,0:T(8,128)(2,1)S(1)} %copy-done, bf16[8,64,128]{2,1,0:T(8,128)(2,1)S(1)} %copy-done.2), custom_call_target="tpu_custom_call" | custom-call | tf_op jit(solution)/shard_map/attend/pallas_call | solution.py:55
  12.5 0.0 collective-permute-done.4.refs_0_
  12.5 1.5 %collective-permute-done.5.refs_1_ = bf16[16,2048]{1,0:T(8,128)(2,1)S(1)} collective-permute-done((bf16[16,2048]{1,0:T(8,128)(2,1)S(1)}, bf16[16,2048]{1,0:T(8,128)(2,1)S(1)}, u32[]{:S(2)}, u32[]{:S(2)}) %collective-permute-start.5) | collective-permute-done | bytes 65568 | tf_op jit(solution)/shard_map/ppermute | solution.py:299
  14.0 1.2 %collective-permute-done.6.refs_2_ = bf16[16,2048]{1,0:T(8,128)(2,1)S(1)} collective-permute-done((bf16[16,2048]{1,0:T(8,128)(2,1)S(1)}, bf16[16,2048]{1,0:T(8,128)(2,1)S(1)}, u32[]{:S(2)}, u32[]{:S(2)}) %collective-permute-start.6) | collective-permute-done | bytes 65568 | tf_op jit(solution)/shard_map/ppermute | solution.py:299
  15.2 0.0 collective-permute-done.7.refs_3_
  15.2 0.0 slice-done
  15.2 0.0 slice-done.1
  15.2 1.4 %own.1.refs_4_ = f32[64,3584]{1,0:T(8,128)S(1)} custom-call(bf16[16,2048]{1,0:T(8,128)(2,1)S(1)} %collective-permute-done.4.refs_0_, bf16[16,2048]{1,0:T(8,128)(2,1)S(1)} %collective-permute-done.5.refs_1_, bf16[16,2048]{1,0:T(8,128)(2,1)S(1)} %collective-permute-done.6.refs_2_, bf16[16,2048]{1,0:T(8,128)(2,1)S(1)} %collective-permute-done.7.refs_3_, ...), custom_call_target="tpu_custom_call" | custom-call | tf_op jit(solution)/shard_map/own/pallas_call | solution.py:343
  16.6 0.0 collective-permute-done.8.refs_5_
  16.6 1.4 %other.1 = (bf16[16,3584]{1,0:T(8,128)(2,1)S(1)}, bf16[8,3584]{1,0:T(8,128)(2,1)S(1)}, bf16[8,3584]{1,0:T(8,128)(2,1)S(1)}, bf16[16,3584]{1,0:T(8,128)(2,1)S(1)}, bf16[16,3584]{1,0:T(8,128)(2,1)S(1)}) custom-call(bf16[16,2048]{1,0:T(8,128)(2,1)S(1)} %collective-permute-done.4.refs_0_, bf16[16,2048]{1,0:T(8,128)(2,1)S(1)} %collective-permute-done.5.refs_1_, ...), custom_call_target="tpu_custom_call" | custom-call | tf_op jit(solution)/shard_map/other/pallas_call | solution.py:352
  18.0 2.2 %collective-permute-start.9 = (bf16[16,3584]{1,0:T(8,128)(2,1)S(1)}, bf16[16,3584]{1,0:T(8,128)(2,1)S(1)}, u32[]{:S(2)}, u32[]{:S(2)}) collective-permute-start(bf16[16,3584]{1,0:T(8,128)(2,1)S(1)} %get-tuple-element.54), channel_id=1, source_target_pairs={{0,8},{1,15},{2,10},{3,13},{4,12},{5,11},{6,14},{7,9},{8,0},{9,7},... | collective-permute-start | bytes 344072 | tf_op jit(solution)/shard_map/ppermute | solution.py:299
  20.2 1.6 %collective-permute-start.10 = (bf16[16,3584]{1,0:T(8,128)(2,1)S(1)}, bf16[16,3584]{1,0:T(8,128)(2,1)S(1)}, u32[]{:S(2)}, u32[]{:S(2)}) collective-permute-start(bf16[16,3584]{1,0:T(8,128)(2,1)S(1)} %get-tuple-element.55), channel_id=1, source_target_pairs={{0,4},{1,7},{2,6},{3,5},{4,0},{5,3},{6,2},{7,1},{8,12},{9,15},{10,... | collective-permute-start | bytes 344072 | tf_op jit(solution)/shard_map/ppermute | solution.py:299
  21.8 0.7 %collective-permute-start.11 = (bf16[16,3584]{1,0:T(8,128)(2,1)S(1)}, bf16[16,3584]{1,0:T(8,128)(2,1)S(1)}, u32[]{:S(2)}, u32[]{:S(2)}) collective-permute-start(bf16[16,3584]{1,0:T(8,128)(2,1)S(1)} %get-tuple-element.51), channel_id=1, source_target_pairs={{0,0},{1,3},{2,2},{3,1},{4,4},{5,7},{6,6},{7,5},{8,8},{9,11},{10,1... | collective-permute-start | bytes 344072 | tf_op jit(solution)/shard_map/ppermute | solution.py:299
  22.5 0.7 %collective-permute-start.15 = (bf16[8,3584]{1,0:T(8,128)(2,1)S(1)}, bf16[8,3584]{1,0:T(8,128)(2,1)S(1)}, u32[]{:S(2)}, u32[]{:S(2)}) collective-permute-start(bf16[8,3584]{1,0:T(8,128)(2,1)S(1)} %get-tuple-element.61), channel_id=1, source_target_pairs={{0,12},{1,11},{2,14},{3,9},{4,8},{5,15},{6,10},{7,13},{8,4},{9,3},... | collective-permute-start | bytes 172040 | tf_op jit(solution)/shard_map/ppermute | solution.py:299
  23.2 6.3 %collective-permute-start.16 = (bf16[8,3584]{1,0:T(8,128)(2,1)S(1)}, bf16[8,3584]{1,0:T(8,128)(2,1)S(1)}, u32[]{:S(2)}, u32[]{:S(2)}) collective-permute-start(bf16[8,3584]{1,0:T(8,128)(2,1)S(1)} %get-tuple-element.62), channel_id=1, source_target_pairs={{0,13},{1,10},{2,15},{3,8},{4,9},{5,14},{6,11},{7,12},{8,5},{9,2},... | collective-permute-start | bytes 172040 | tf_op jit(solution)/shard_map/ppermute | solution.py:299
  29.5 0.7 %place.1 = (f32[64,32]{1,0:T(8,128)S(1)}, f32[16,16]{1,0:T(8,128)S(1)}) custom-call(s32[4,16]{1,0:T(4,128)S(1)} %get-tuple-element.52.refs_1_.refs_0_, s32[8,16]{1,0:T(8,128)S(1)} %get-tuple-element.35.refs_2_.refs_1_, s32[4,16]{1,0:T(4,128)S(1)} %collective-permute-done.1.refs_5_.refs_2_, s32[8,16]{1,0:T(8,128)S(1)} %collective-permute-done.2.refs_6_.refs_3_), custom_call_target="tpu_custom_call" | custom-call | tf_op jit(solution)/shard_map/place/pallas_call | solution.py:364
  30.2 0.0 collective-permute-done.9.refs_0_
  30.2 0.0 collective-permute-done.10.refs_1_
  30.2 0.0 collective-permute-done.11.refs_2_
  30.3 0.2 sum.1
  30.5 0.1 collective-permute-start.14
  30.6 0.5 %collective-permute-start.12 = (bf16[16,1152]{1,0:T(8,128)(2,1)S(1)}, bf16[16,1152]{1,0:T(8,128)(2,1)S(1)}, u32[]{:S(2)}, u32[]{:S(2)}) collective-permute-start(bf16[16,1152]{1,0:T(8,128)(2,1)S(1)} %get-tuple-element.58), channel_id=1, source_target_pairs={{0,1},{1,0},{2,3},{3,2},{4,5},{5,4},{6,7},{7,6},{8,9},{9,8},{10,11... | collective-permute-start | bytes 110600 | tf_op jit(solution)/shard_map/ppermute | solution.py:291
  31.1 0.1 collective-permute-start.13
  31.2 0.0 collective-permute-done.15.refs_3_
  31.2 0.2 collective-permute-done.16.refs_4_
  31.4 0.6 %collective-permute-done.12.refs_0_ = bf16[16,1152]{1,0:T(8,128)(2,1)S(1)} collective-permute-done((bf16[16,1152]{1,0:T(8,128)(2,1)S(1)}, bf16[16,1152]{1,0:T(8,128)(2,1)S(1)}, u32[]{:S(2)}, u32[]{:S(2)}) %collective-permute-start.12) | collective-permute-done | bytes 36896 | tf_op jit(solution)/shard_map/ppermute | solution.py:291
  31.9 0.3 %collective-permute-done.13.refs_1_ = bf16[16,1152]{1,0:T(8,128)(2,1)S(1)} collective-permute-done((bf16[16,1152]{1,0:T(8,128)(2,1)S(1)}, bf16[16,1152]{1,0:T(8,128)(2,1)S(1)}, u32[]{:S(2)}, u32[]{:S(2)}) %collective-permute-start.13) | collective-permute-done | bytes 36896 | tf_op jit(solution)/shard_map/ppermute | solution.py:291
  32.3 0.0 collective-permute-done.14.refs_2_
  32.3 0.9 %last.1 = bf16[16,3584]{1,0:T(8,128)(2,1)} custom-call(f32[16,3584]{1,0:T(8,128)S(1)} %get-tuple-element.56.own_ref, f32[16,16]{1,0:T(8,128)S(1)} %get-tuple-element.57.place_ref, bf16[16,1152]{1,0:T(8,128)(2,1)S(1)} %collective-permute-done.12.refs_0_, bf16[16,1152]{1,0:T(8,128)(2,1)S(1)} %collective-permute-done.13.refs_1_, ...), custom_call_target="tpu_custom_call" | custom-call | tf_op jit(solution)/shard_map/last/pallas_call | solution.py:389
  (1 shorter events, 0.0 us)
Async XLA Ops:
  0.6 2.4 %collective-permute-start.3 = (bf16[128,1024]{1,0:T(8,128)(2,1)}, bf16[128,1024]{1,0:T(8,128)(2,1)S(1)}, u32[]{:S(2)}, u32[]{:S(2)}) collective-permute-start(bf16[128,1024]{1,0:T(8,128)(2,1)} %bitcast.9), channel_id=1, source_target_pairs={{0,1},{1,0},{2,3},{3,2},{4,5},{5,4},{6,7},{7,6},{8,9},{9,8},{10,11... | collective-permute-start | bytes 786440 | tf_op jit(solution)/shard_map/ppermute | solution.py:291
  1.1 1.9 %collective-permute-start = (f32[8,16]{1,0:T(8,128)}, f32[8,16]{1,0:T(8,128)S(1)}, u32[]{:S(2)}, u32[]{:S(2)}) collective-permute-start(f32[8,16]{1,0:T(8,128)} %bitcast.11), channel_id=1, source_target_pairs={{0,1},{1,0},{2,3},{3,2},{4,5},{5,4},{6,7},{7,6},{8,9},{9,8},{10,11... | collective-permute-start | bytes 1544 | tf_op jit(solution)/shard_map/ppermute | solution.py:291
  1.2 1.8 %collective-permute-start.2 = (s32[8,16]{1,0:T(8,128)}, s32[8,16]{1,0:T(8,128)S(1)}, u32[]{:S(2)}, u32[]{:S(2)}) collective-permute-start(s32[8,16]{1,0:T(8,128)} %bitcast.13), channel_id=1, source_target_pairs={{0,1},{1,0},{2,3},{3,2},{4,5},{5,4},{6,7},{7,6},{8,9},{9,8},{10,11... | collective-permute-start | bytes 1544 | tf_op jit(solution)/shard_map/ppermute | solution.py:291
  1.7 1.4 %collective-permute-start.1 = (s32[4,16]{1,0:T(4,128)}, s32[4,16]{1,0:T(4,128)S(1)}, u32[]{:S(2)}, u32[]{:S(2)}) collective-permute-start(s32[4,16]{1,0:T(4,128)} %bitcast.15), channel_id=1, source_target_pairs={{0,1},{1,0},{2,3},{3,2},{4,5},{5,4},{6,7},{7,6},{8,9},{9,8},{10,11... | collective-permute-start | bytes 776 | tf_op jit(solution)/shard_map/ppermute | solution.py:291
  3.0 13.6 %collective-permute-start.8 = (bf16[1024,3584]{1,0:T(8,128)(2,1)}, bf16[1024,3584]{1,0:T(8,128)(2,1)S(1)}, u32[]{:S(2)}, u32[]{:S(2)}) collective-permute-start(bf16[1024,3584]{1,0:T(8,128)(2,1)} %bitcast.5), channel_id=1, source_target_pairs={{0,1},{1,0},{2,3},{3,2},{4,5},{5,4},{6,7},{7,6},{8,9},{9,8},{10,11... | collective-permute-start | bytes 22020104 | tf_op jit(solution)/shard_map/ppermute | solution.py:291
  3.3 11.9 %slice-start = ((s8[7340032]{0:T(1024)(128)(4,1)}), s8[4194304]{0:T(1024)(128)(4,1)S(1)}, s32[]{:S(2)}) async-start(s8[7340032]{0:T(1024)(128)(4,1)} %bitcast.6), calls=%async_computation | async-start | bytes 8388608
  3.3 6.8 %copy-start = (bf16[8,128,512]{2,1,0:T(8,128)(2,1)S(1)}, bf16[8,128,512]{2,1,0:T(8,128)(2,1)}, u32[]{:S(2)}) copy-start(bf16[8,128,512]{2,1,0:T(8,128)(2,1)} %keys_ref) | copy-start | bytes 3145732
  3.3 6.8 %copy-start.1 = (bf16[8,64,512]{2,1,0:T(8,128)(2,1)S(1)}, bf16[8,64,512]{2,1,0:T(8,128)(2,1)}, u32[]{:S(2)}) copy-start(bf16[8,64,512]{2,1,0:T(8,128)(2,1)} %latent_ref) | copy-start | bytes 1572868
  3.3 6.8 %copy-start.2 = (bf16[8,64,128]{2,1,0:T(8,128)(2,1)S(1)}, bf16[8,64,128]{2,1,0:T(8,128)(2,1)}, u32[]{:S(2)}) copy-start(bf16[8,64,128]{2,1,0:T(8,128)(2,1)} %rope_keys_ref) | copy-start | bytes 393220
  3.3 6.8 %copy-start.3 = (bf16[8,4096]{1,0:T(8,128)(2,1)S(1)}, bf16[8,4096]{1,0:T(8,128)(2,1)}, u32[]{:S(2)}) copy-start(bf16[8,4096]{1,0:T(8,128)(2,1)} %rope_ref) | copy-start | bytes 196612
  3.3 6.8 %copy-start.4 = (s32[8]{0:T(128)S(1)}, s32[8]{0:T(128)}, u32[]{:S(2)}) copy-start(s32[8]{0:T(128)} %lengths_ref) | copy-start | bytes 100
  3.4 11.9 %slice-start.1 = ((s8[7340032]{0:T(1024)(128)(4,1)}), s8[3145728]{0:T(1024)(128)(4,1)S(1)}, s32[]{:S(2)}) async-start(s8[7340032]{0:T(1024)(128)(4,1)} %bitcast.6), calls=%async_computation.1 | async-start | bytes 6291456
  3.9 8.6 %collective-permute-start.4 = (bf16[16,2048]{1,0:T(8,128)(2,1)S(1)}, bf16[16,2048]{1,0:T(8,128)(2,1)S(1)}, u32[]{:S(2)}, u32[]{:S(2)}) collective-permute-start(bf16[16,2048]{1,0:T(8,128)(2,1)S(1)} %get-tuple-element.37), channel_id=1, source_target_pairs={{0,8},{1,15},{2,10},{3,13},{4,12},{5,11},{6,14},{7,9},{8,0},{9,7},... | collective-permute-start | bytes 196616 | tf_op jit(solution)/shard_map/ppermute | solution.py:299
  7.9 6.2 %collective-permute-start.5 = (bf16[16,2048]{1,0:T(8,128)(2,1)S(1)}, bf16[16,2048]{1,0:T(8,128)(2,1)S(1)}, u32[]{:S(2)}, u32[]{:S(2)}) collective-permute-start(bf16[16,2048]{1,0:T(8,128)(2,1)S(1)} %get-tuple-element.38), channel_id=1, source_target_pairs={{0,12},{1,11},{2,14},{3,9},{4,8},{5,15},{6,10},{7,13},{8,4},{9,3},... | collective-permute-start | bytes 196616 | tf_op jit(solution)/shard_map/ppermute | solution.py:299
  9.2 6.0 %collective-permute-start.6 = (bf16[16,2048]{1,0:T(8,128)(2,1)S(1)}, bf16[16,2048]{1,0:T(8,128)(2,1)S(1)}, u32[]{:S(2)}, u32[]{:S(2)}) collective-permute-start(bf16[16,2048]{1,0:T(8,128)(2,1)S(1)} %get-tuple-element.39), channel_id=1, source_target_pairs={{0,4},{1,7},{2,6},{3,5},{4,0},{5,3},{6,2},{7,1},{8,12},{9,15},{10,... | collective-permute-start | bytes 196616 | tf_op jit(solution)/shard_map/ppermute | solution.py:299
  9.4 5.8 %collective-permute-start.7 = (bf16[16,2048]{1,0:T(8,128)(2,1)S(1)}, bf16[16,2048]{1,0:T(8,128)(2,1)S(1)}, u32[]{:S(2)}, u32[]{:S(2)}) collective-permute-start(bf16[16,2048]{1,0:T(8,128)(2,1)S(1)} %get-tuple-element.40), channel_id=1, source_target_pairs={{0,0},{1,3},{2,2},{3,1},{4,4},{5,7},{6,6},{7,5},{8,8},{9,11},{10,1... | collective-permute-start | bytes 196616 | tf_op jit(solution)/shard_map/ppermute | solution.py:299
  18.0 12.2 %collective-permute-start.9 = (bf16[16,3584]{1,0:T(8,128)(2,1)S(1)}, bf16[16,3584]{1,0:T(8,128)(2,1)S(1)}, u32[]{:S(2)}, u32[]{:S(2)}) collective-permute-start(bf16[16,3584]{1,0:T(8,128)(2,1)S(1)} %get-tuple-element.54), channel_id=1, source_target_pairs={{0,8},{1,15},{2,10},{3,13},{4,12},{5,11},{6,14},{7,9},{8,0},{9,7},... | collective-permute-start | bytes 344072 | tf_op jit(solution)/shard_map/ppermute | solution.py:299
  20.2 10.0 %collective-permute-start.10 = (bf16[16,3584]{1,0:T(8,128)(2,1)S(1)}, bf16[16,3584]{1,0:T(8,128)(2,1)S(1)}, u32[]{:S(2)}, u32[]{:S(2)}) collective-permute-start(bf16[16,3584]{1,0:T(8,128)(2,1)S(1)} %get-tuple-element.55), channel_id=1, source_target_pairs={{0,4},{1,7},{2,6},{3,5},{4,0},{5,3},{6,2},{7,1},{8,12},{9,15},{10,... | collective-permute-start | bytes 344072 | tf_op jit(solution)/shard_map/ppermute | solution.py:299
  21.8 8.4 %collective-permute-start.11 = (bf16[16,3584]{1,0:T(8,128)(2,1)S(1)}, bf16[16,3584]{1,0:T(8,128)(2,1)S(1)}, u32[]{:S(2)}, u32[]{:S(2)}) collective-permute-start(bf16[16,3584]{1,0:T(8,128)(2,1)S(1)} %get-tuple-element.51), channel_id=1, source_target_pairs={{0,0},{1,3},{2,2},{3,1},{4,4},{5,7},{6,6},{7,5},{8,8},{9,11},{10,1... | collective-permute-start | bytes 344072 | tf_op jit(solution)/shard_map/ppermute | solution.py:299
  22.5 8.7 %collective-permute-start.15 = (bf16[8,3584]{1,0:T(8,128)(2,1)S(1)}, bf16[8,3584]{1,0:T(8,128)(2,1)S(1)}, u32[]{:S(2)}, u32[]{:S(2)}) collective-permute-start(bf16[8,3584]{1,0:T(8,128)(2,1)S(1)} %get-tuple-element.61), channel_id=1, source_target_pairs={{0,12},{1,11},{2,14},{3,9},{4,8},{5,15},{6,10},{7,13},{8,4},{9,3},... | collective-permute-start | bytes 172040 | tf_op jit(solution)/shard_map/ppermute | solution.py:299
  23.2 8.2 %collective-permute-start.16 = (bf16[8,3584]{1,0:T(8,128)(2,1)S(1)}, bf16[8,3584]{1,0:T(8,128)(2,1)S(1)}, u32[]{:S(2)}, u32[]{:S(2)}) collective-permute-start(bf16[8,3584]{1,0:T(8,128)(2,1)S(1)} %get-tuple-element.62), channel_id=1, source_target_pairs={{0,13},{1,10},{2,15},{3,8},{4,9},{5,14},{6,11},{7,12},{8,5},{9,2},... | collective-permute-start | bytes 172040 | tf_op jit(solution)/shard_map/ppermute | solution.py:299
  30.5 1.8 %collective-permute-start.14 = (bf16[16,1280]{1,0:T(8,128)(2,1)S(1)}, bf16[16,1280]{1,0:T(8,128)(2,1)S(1)}, u32[]{:S(2)}, u32[]{:S(2)}) collective-permute-start(bf16[16,1280]{1,0:T(8,128)(2,1)S(1)} %get-tuple-element.60), channel_id=1, source_target_pairs={{0,1},{1,0},{2,3},{3,2},{4,5},{5,4},{6,7},{7,6},{8,9},{9,8},{10,11... | collective-permute-start | bytes 122888 | tf_op jit(solution)/shard_map/ppermute | solution.py:291
  30.6 1.4 %collective-permute-start.12 = (bf16[16,1152]{1,0:T(8,128)(2,1)S(1)}, bf16[16,1152]{1,0:T(8,128)(2,1)S(1)}, u32[]{:S(2)}, u32[]{:S(2)}) collective-permute-start(bf16[16,1152]{1,0:T(8,128)(2,1)S(1)} %get-tuple-element.58), channel_id=1, source_target_pairs={{0,1},{1,0},{2,3},{3,2},{4,5},{5,4},{6,7},{7,6},{8,9},{9,8},{10,11... | collective-permute-start | bytes 110600 | tf_op jit(solution)/shard_map/ppermute | solution.py:291
  31.1 1.2 %collective-permute-start.13 = (bf16[16,1152]{1,0:T(8,128)(2,1)S(1)}, bf16[16,1152]{1,0:T(8,128)(2,1)S(1)}, u32[]{:S(2)}, u32[]{:S(2)}) collective-permute-start(bf16[16,1152]{1,0:T(8,128)(2,1)S(1)} %get-tuple-element.59), channel_id=1, source_target_pairs={{0,1},{1,0},{2,3},{3,2},{4,5},{5,4},{6,7},{7,6},{8,9},{9,8},{10,11... | collective-permute-start | bytes 110600 | tf_op jit(solution)/shard_map/ppermute | solution.py:291

commit v6 on v5

--- a/solution.py
+++ b/solution.py
@@ -79,16 +79,18 @@
 
 
 def turn_of(node_count, lane_count, lane, number):
-    far = node_count // lane_count // 2
-    turn = (node_count - 1 - number) // lane_count
-    turn = jnp.where((lane == 0) & (turn < far), far - 1 - turn, turn)
-    return jnp.where(number % lane_count == lane, turn, -1)
+    half = node_count // 2
+    far_turn = (number - half) // lane_count
+    far_lane = (number - half + lane_count - 1 + far_turn * (lane_count - 1)) % lane_count
+    near_turn = (node_count - 1 - number) // lane_count
+    turn = jnp.where(number >= half, far_turn, near_turn)
+    return jnp.where(jnp.where(number >= half, far_lane, number % lane_count) == lane, turn, -1)
 
 
 def number_of(node_count, lane_count, lane, turn):
-    far = node_count // lane_count // 2
-    if turn < far:
-        turn = jnp.where(lane == 0, far - 1 - turn, turn) if isinstance(lane, jax.Array) else (turn, far - 1 - turn)[lane == 0]
+    half = node_count // 2
+    if turn < half // lane_count:
+        return half + lane_count * turn + (turn + 1 + lane) % lane_count
     return node_count - lane_count * (turn + 1) + lane
 
 

time: 33.4 us -> 32.8 us (0.982)
  waiting for transfers between devices: 4.11 us -> 3.34 us
    ppermute x8, waiting for transfers between devices: 1.17 us -> 0.27 us  [other_core(): return lax.ppermute(value, 'lane', [(0, 1), (1, 0)])]
  transfers between devices with their start and end apart: 17 -> 17, of which waited for: 6 -> 3; matrix products, arithmetic and copies ran while one was open for 0% -> 0% of each run, Pallas kernels for 19% -> 19%
where the time goes in v6:
time: 32.8 us; the launch traced here: 32.6 us
  starting transfers between devices  19.9 us (61%)
  Pallas kernels  8.5 us (26%)
  waiting for transfers between devices  3.34 us (10%)
  between operations  0.83 us (3%)
    ppermute x9, starting transfers between devices, meet(): return lax.ppermute(value, ('node', 'lane'), pairs)  17.8 us
    ppermute x9, waiting for transfers between devices, meet(): return lax.ppermute(value, ('node', 'lane'), pairs)  3.07 us
    pallas_call x1, Pallas kernels, attend(): pl.pallas_call(attend_kernel, in_specs=[pl.BlockSpec(memory_space=pltpu.S...  2.37 us
    ppermute x8, starting transfers between devices, other_core(): return lax.ppermute(value, 'lane', [(0, 1), (1, 0)])  2.03 us
    pallas_call x1, Pallas kernels, local(): pl.pallas_call(functools.partial(other_kernel, turns), in_specs=[whole] *...  1.38 us
    pallas_call x1, Pallas kernels, local(): pl.pallas_call(own_kernel, in_specs=[whole] * (turns + 1), out_specs=whol...  1.37 us
    pallas_call x1, Pallas kernels, local(): pl.pallas_call(load_kernel, in_specs=[outside] * 4, out_specs=[whole] * 4...  1.03 us
    pallas_call x1, Pallas kernels, local(): pl.pallas_call(functools.partial(last_kernel, len(widths)), in_specs=[who...  0.89 us
  transfers between devices with their start and end apart: 17, of which 3 were waited for; matrix products, arithmetic and copies ran while one was open for 0% of the time, Pallas kernels for 19%

profile of v6, /device:TPU:0, one launch (start us, length us, event | category | flops | bytes accessed | tf_op | source)
XLA Modules:
  0.0 32.6 jit_solution(7857101057971410506)
XLA Ops:
  0.6 0.5 %collective-permute-start.3 = (bf16[128,1024]{1,0:T(8,128)(2,1)}, bf16[128,1024]{1,0:T(8,128)(2,1)S(1)}, u32[]{:S(2)}, u32[]{:S(2)}) collective-permute-start(bf16[128,1024]{1,0:T(8,128)(2,1)} %bitcast.9), channel_id=1, source_target_pairs={{0,1},{1,0},{2,3},{3,2},{4,5},{5,4},{6,7},{7,6},{8,9},{9,8},{10,11... | collective-permute-start | bytes 786440 | tf_op jit(solution)/shard_map/ppermute | solution.py:293
  1.1 0.1 collective-permute-start
  1.2 0.4 %collective-permute-start.2 = (s32[8,16]{1,0:T(8,128)}, s32[8,16]{1,0:T(8,128)S(1)}, u32[]{:S(2)}, u32[]{:S(2)}) collective-permute-start(s32[8,16]{1,0:T(8,128)} %bitcast.13), channel_id=1, source_target_pairs={{0,1},{1,0},{2,3},{3,2},{4,5},{5,4},{6,7},{7,6},{8,9},{9,8},{10,11... | collective-permute-start | bytes 1544 | tf_op jit(solution)/shard_map/ppermute | solution.py:293
  1.7 0.1 collective-permute-start.1
  1.7 1.0 %load.1 = (f32[8,16]{1,0:T(8,128)S(1)}, s32[4,16]{1,0:T(4,128)S(1)}, s32[8,16]{1,0:T(8,128)S(1)}, bf16[128,1024]{1,0:T(8,128)(2,1)S(1)}) custom-call(f32[8,16]{1,0:T(8,128)} %bitcast.12, s32[4,16]{1,0:T(4,128)} %bitcast.16, s32[8,16]{1,0:T(8,128)} %bitcast.14, bf16[128,1024]{1,0:T(8,128)(2,1)} %bitcast.10), custom_call_target="tpu_custom_call" | custom-call | tf_op jit(solution)/shard_map/load/pallas_call | solution.py:318
  2.8 0.2 collective-permute-done.1.refs_5_.refs_2_
  3.0 0.0 collective-permute-done.refs_4_
  3.0 0.0 collective-permute-done.2.refs_6_.refs_3_
  3.0 0.0 collective-permute-done.3.refs_7_
  3.0 0.3 collective-permute-start.8
  3.3 0.0 slice-start
  3.3 0.0 copy-start
  3.3 0.0 copy-start.1
  3.3 0.0 copy-start.2
  3.3 0.0 copy-start.3
  3.3 0.0 copy-start.4
  3.4 0.0 slice-start.1
  3.4 0.5 %pack.1 = (bf16[16,2048]{1,0:T(8,128)(2,1)S(1)}, bf16[16,2048]{1,0:T(8,128)(2,1)S(1)}, bf16[16,2048]{1,0:T(8,128)(2,1)S(1)}, bf16[16,2048]{1,0:T(8,128)(2,1)S(1)}) custom-call(f32[8,16]{1,0:T(8,128)S(1)} %get-tuple-element.34.refs_0_, s32[4,16]{1,0:T(4,128)S(1)} %get-tuple-element.52.refs_1_.refs_0_, s32[8,16]{1,0:T(8,128)S(1)} %get-tuple-element.35.refs_2_.refs_1_, ...), custom_call_target="tpu_custom_call" | custom-call | flops 6000000000 | tf_op jit(solution)/shard_map/pack/pallas_call | solution.py:330
  3.9 4.9 %collective-permute-start.4 = (bf16[16,2048]{1,0:T(8,128)(2,1)S(1)}, bf16[16,2048]{1,0:T(8,128)(2,1)S(1)}, u32[]{:S(2)}, u32[]{:S(2)}) collective-permute-start(bf16[16,2048]{1,0:T(8,128)(2,1)S(1)} %get-tuple-element.37), channel_id=1, source_target_pairs={{0,10},{1,9},{2,8},{3,11},{4,14},{5,13},{6,12},{7,15},{8,2},{9,1},... | collective-permute-start | bytes 196616 | tf_op jit(solution)/shard_map/ppermute | solution.py:301
  8.8 1.3 %collective-permute-start.5 = (bf16[16,2048]{1,0:T(8,128)(2,1)S(1)}, bf16[16,2048]{1,0:T(8,128)(2,1)S(1)}, u32[]{:S(2)}, u32[]{:S(2)}) collective-permute-start(bf16[16,2048]{1,0:T(8,128)(2,1)S(1)} %get-tuple-element.38), channel_id=1, source_target_pairs={{0,12},{1,15},{2,14},{3,13},{4,8},{5,11},{6,10},{7,9},{8,4},{9,7},... | collective-permute-start | bytes 196616 | tf_op jit(solution)/shard_map/ppermute | solution.py:301
  10.2 0.2 collective-permute-start.6
  10.4 0.7 %collective-permute-start.7 = (bf16[16,2048]{1,0:T(8,128)(2,1)S(1)}, bf16[16,2048]{1,0:T(8,128)(2,1)S(1)}, u32[]{:S(2)}, u32[]{:S(2)}) collective-permute-start(bf16[16,2048]{1,0:T(8,128)(2,1)S(1)} %get-tuple-element.40), channel_id=1, source_target_pairs={{0,0},{1,3},{2,2},{3,1},{4,4},{5,7},{6,6},{7,5},{8,8},{9,11},{10,1... | collective-permute-start | bytes 196616 | tf_op jit(solution)/shard_map/ppermute | solution.py:301
  11.1 0.0 copy-done
  11.1 0.0 copy-done.1
  11.1 0.0 copy-done.2
  11.1 0.0 copy-done.3
  11.1 0.0 copy-done.4
  11.1 2.4 %attend.1 = bf16[8,64,512]{2,1,0:T(8,128)(2,1)} custom-call(s32[8]{0:T(128)S(1)} %copy-done.4, bf16[8,64,512]{2,1,0:T(8,128)(2,1)S(1)} %copy-done.1, bf16[8,4096]{1,0:T(8,128)(2,1)S(1)} %copy-done.3, bf16[8,128,512]{2,1,0:T(8,128)(2,1)S(1)} %copy-done, bf16[8,64,128]{2,1,0:T(8,128)(2,1)S(1)} %copy-done.2), custom_call_target="tpu_custom_call" | custom-call | tf_op jit(solution)/shard_map/attend/pallas_call | solution.py:55
  13.5 0.0 collective-permute-done.4.refs_0_
  13.5 1.8 %collective-permute-done.5.refs_1_ = bf16[16,2048]{1,0:T(8,128)(2,1)S(1)} collective-permute-done((bf16[16,2048]{1,0:T(8,128)(2,1)S(1)}, bf16[16,2048]{1,0:T(8,128)(2,1)S(1)}, u32[]{:S(2)}, u32[]{:S(2)}) %collective-permute-start.5) | collective-permute-done | bytes 65568 | tf_op jit(solution)/shard_map/ppermute | solution.py:301
  15.3 0.0 collective-permute-done.6.refs_2_
  15.3 0.0 collective-permute-done.7.refs_3_
  15.3 0.0 slice-done
  15.3 0.0 slice-done.1
  15.3 1.4 %own.1.refs_4_ = f32[64,3584]{1,0:T(8,128)S(1)} custom-call(bf16[16,2048]{1,0:T(8,128)(2,1)S(1)} %collective-permute-done.4.refs_0_, bf16[16,2048]{1,0:T(8,128)(2,1)S(1)} %collective-permute-done.5.refs_1_, bf16[16,2048]{1,0:T(8,128)(2,1)S(1)} %collective-permute-done.6.refs_2_, bf16[16,2048]{1,0:T(8,128)(2,1)S(1)} %collective-permute-done.7.refs_3_, ...), custom_call_target="tpu_custom_call" | custom-call | tf_op jit(solution)/shard_map/own/pallas_call | solution.py:345
  16.7 0.0 collective-permute-done.8.refs_5_
  16.7 1.4 %other.1 = (bf16[16,3584]{1,0:T(8,128)(2,1)S(1)}, bf16[8,3584]{1,0:T(8,128)(2,1)S(1)}, bf16[8,3584]{1,0:T(8,128)(2,1)S(1)}, bf16[16,3584]{1,0:T(8,128)(2,1)S(1)}, bf16[16,3584]{1,0:T(8,128)(2,1)S(1)}) custom-call(bf16[16,2048]{1,0:T(8,128)(2,1)S(1)} %collective-permute-done.4.refs_0_, bf16[16,2048]{1,0:T(8,128)(2,1)S(1)} %collective-permute-done.5.refs_1_, ...), custom_call_target="tpu_custom_call" | custom-call | tf_op jit(solution)/shard_map/other/pallas_call | solution.py:354
  18.1 3.1 %collective-permute-start.9 = (bf16[16,3584]{1,0:T(8,128)(2,1)S(1)}, bf16[16,3584]{1,0:T(8,128)(2,1)S(1)}, u32[]{:S(2)}, u32[]{:S(2)}) collective-permute-start(bf16[16,3584]{1,0:T(8,128)(2,1)S(1)} %get-tuple-element.54), channel_id=1, source_target_pairs={{0,10},{1,9},{2,8},{3,11},{4,14},{5,13},{6,12},{7,15},{8,2},{9,1},... | collective-permute-start | bytes 344072 | tf_op jit(solution)/shard_map/ppermute | solution.py:301
  21.2 1.6 %collective-permute-start.10 = (bf16[16,3584]{1,0:T(8,128)(2,1)S(1)}, bf16[16,3584]{1,0:T(8,128)(2,1)S(1)}, u32[]{:S(2)}, u32[]{:S(2)}) collective-permute-start(bf16[16,3584]{1,0:T(8,128)(2,1)S(1)} %get-tuple-element.55), channel_id=1, source_target_pairs={{0,4},{1,7},{2,6},{3,5},{4,0},{5,3},{6,2},{7,1},{8,12},{9,15},{10,... | collective-permute-start | bytes 344072 | tf_op jit(solution)/shard_map/ppermute | solution.py:301
  22.8 0.7 %collective-permute-start.11 = (bf16[16,3584]{1,0:T(8,128)(2,1)S(1)}, bf16[16,3584]{1,0:T(8,128)(2,1)S(1)}, u32[]{:S(2)}, u32[]{:S(2)}) collective-permute-start(bf16[16,3584]{1,0:T(8,128)(2,1)S(1)} %get-tuple-element.51), channel_id=1, source_target_pairs={{0,0},{1,3},{2,2},{3,1},{4,4},{5,7},{6,6},{7,5},{8,8},{9,11},{10,1... | collective-permute-start | bytes 344072 | tf_op jit(solution)/shard_map/ppermute | solution.py:301
  23.4 0.6 %collective-permute-start.15 = (bf16[8,3584]{1,0:T(8,128)(2,1)S(1)}, bf16[8,3584]{1,0:T(8,128)(2,1)S(1)}, u32[]{:S(2)}, u32[]{:S(2)}) collective-permute-start(bf16[8,3584]{1,0:T(8,128)(2,1)S(1)} %get-tuple-element.61), channel_id=1, source_target_pairs={{0,12},{1,15},{2,14},{3,13},{4,8},{5,11},{6,10},{7,9},{8,4},{9,7},... | collective-permute-start | bytes 172040 | tf_op jit(solution)/shard_map/ppermute | solution.py:301
  24.0 4.8 %collective-permute-start.16 = (bf16[8,3584]{1,0:T(8,128)(2,1)S(1)}, bf16[8,3584]{1,0:T(8,128)(2,1)S(1)}, u32[]{:S(2)}, u32[]{:S(2)}) collective-permute-start(bf16[8,3584]{1,0:T(8,128)(2,1)S(1)} %get-tuple-element.62), channel_id=1, source_target_pairs={{0,13},{1,14},{2,15},{3,12},{4,9},{5,10},{6,11},{7,8},{8,5},{9,6},... | collective-permute-start | bytes 172040 | tf_op jit(solution)/shard_map/ppermute | solution.py:301
  28.8 0.7 %place.1 = (f32[64,32]{1,0:T(8,128)S(1)}, f32[16,16]{1,0:T(8,128)S(1)}) custom-call(s32[4,16]{1,0:T(4,128)S(1)} %get-tuple-element.52.refs_1_.refs_0_, s32[8,16]{1,0:T(8,128)S(1)} %get-tuple-element.35.refs_2_.refs_1_, s32[4,16]{1,0:T(4,128)S(1)} %collective-permute-done.1.refs_5_.refs_2_, s32[8,16]{1,0:T(8,128)S(1)} %collective-permute-done.2.refs_6_.refs_3_), custom_call_target="tpu_custom_call" | custom-call | tf_op jit(solution)/shard_map/place/pallas_call | solution.py:366
  29.5 0.0 collective-permute-done.9.refs_0_
  29.5 0.0 collective-permute-done.10.refs_1_
  29.5 0.0 collective-permute-done.11.refs_2_
  29.5 0.2 sum.1
  29.7 0.1 collective-permute-start.14
  29.8 0.5 %collective-permute-start.12 = (bf16[16,1152]{1,0:T(8,128)(2,1)S(1)}, bf16[16,1152]{1,0:T(8,128)(2,1)S(1)}, u32[]{:S(2)}, u32[]{:S(2)}) collective-permute-start(bf16[16,1152]{1,0:T(8,128)(2,1)S(1)} %get-tuple-element.58), channel_id=1, source_target_pairs={{0,1},{1,0},{2,3},{3,2},{4,5},{5,4},{6,7},{7,6},{8,9},{9,8},{10,11... | collective-permute-start | bytes 110600 | tf_op jit(solution)/shard_map/ppermute | solution.py:293
  30.3 0.1 collective-permute-start.13
  30.4 0.0 collective-permute-done.15.refs_3_
  30.4 1.2 %collective-permute-done.16.refs_4_ = bf16[8,3584]{1,0:T(8,128)(2,1)S(1)} collective-permute-done((bf16[8,3584]{1,0:T(8,128)(2,1)S(1)}, bf16[8,3584]{1,0:T(8,128)(2,1)S(1)}, u32[]{:S(2)}, u32[]{:S(2)}) %collective-permute-start.16) | collective-permute-done | bytes 57376 | tf_op jit(solution)/shard_map/ppermute | solution.py:301
  31.7 0.0 collective-permute-done.12.refs_0_
  31.7 0.0 collective-permute-done.13.refs_1_
  31.7 0.0 collective-permute-done.14.refs_2_
  31.7 0.9 %last.1 = bf16[16,3584]{1,0:T(8,128)(2,1)} custom-call(f32[16,3584]{1,0:T(8,128)S(1)} %get-tuple-element.56.own_ref, f32[16,16]{1,0:T(8,128)S(1)} %get-tuple-element.57.place_ref, bf16[16,1152]{1,0:T(8,128)(2,1)S(1)} %collective-permute-done.12.refs_0_, bf16[16,1152]{1,0:T(8,128)(2,1)S(1)} %collective-permute-done.13.refs_1_, ...), custom_call_target="tpu_custom_call" | custom-call | tf_op jit(solution)/shard_map/last/pallas_call | solution.py:391
  (1 shorter events, 0.0 us)
Async XLA Ops:
  0.6 2.4 %collective-permute-start.3 = (bf16[128,1024]{1,0:T(8,128)(2,1)}, bf16[128,1024]{1,0:T(8,128)(2,1)S(1)}, u32[]{:S(2)}, u32[]{:S(2)}) collective-permute-start(bf16[128,1024]{1,0:T(8,128)(2,1)} %bitcast.9), channel_id=1, source_target_pairs={{0,1},{1,0},{2,3},{3,2},{4,5},{5,4},{6,7},{7,6},{8,9},{9,8},{10,11... | collective-permute-start | bytes 786440 | tf_op jit(solution)/shard_map/ppermute | solution.py:293
  1.1 1.9 %collective-permute-start = (f32[8,16]{1,0:T(8,128)}, f32[8,16]{1,0:T(8,128)S(1)}, u32[]{:S(2)}, u32[]{:S(2)}) collective-permute-start(f32[8,16]{1,0:T(8,128)} %bitcast.11), channel_id=1, source_target_pairs={{0,1},{1,0},{2,3},{3,2},{4,5},{5,4},{6,7},{7,6},{8,9},{9,8},{10,11... | collective-permute-start | bytes 1544 | tf_op jit(solution)/shard_map/ppermute | solution.py:293
  1.2 1.8 %collective-permute-start.2 = (s32[8,16]{1,0:T(8,128)}, s32[8,16]{1,0:T(8,128)S(1)}, u32[]{:S(2)}, u32[]{:S(2)}) collective-permute-start(s32[8,16]{1,0:T(8,128)} %bitcast.13), channel_id=1, source_target_pairs={{0,1},{1,0},{2,3},{3,2},{4,5},{5,4},{6,7},{7,6},{8,9},{9,8},{10,11... | collective-permute-start | bytes 1544 | tf_op jit(solution)/shard_map/ppermute | solution.py:293
  1.7 1.4 %collective-permute-start.1 = (s32[4,16]{1,0:T(4,128)}, s32[4,16]{1,0:T(4,128)S(1)}, u32[]{:S(2)}, u32[]{:S(2)}) collective-permute-start(s32[4,16]{1,0:T(4,128)} %bitcast.15), channel_id=1, source_target_pairs={{0,1},{1,0},{2,3},{3,2},{4,5},{5,4},{6,7},{7,6},{8,9},{9,8},{10,11... | collective-permute-start | bytes 776 | tf_op jit(solution)/shard_map/ppermute | solution.py:293
  3.0 13.6 %collective-permute-start.8 = (bf16[1024,3584]{1,0:T(8,128)(2,1)}, bf16[1024,3584]{1,0:T(8,128)(2,1)S(1)}, u32[]{:S(2)}, u32[]{:S(2)}) collective-permute-start(bf16[1024,3584]{1,0:T(8,128)(2,1)} %bitcast.5), channel_id=1, source_target_pairs={{0,1},{1,0},{2,3},{3,2},{4,5},{5,4},{6,7},{7,6},{8,9},{9,8},{10,11... | collective-permute-start | bytes 22020104 | tf_op jit(solution)/shard_map/ppermute | solution.py:293
  3.3 12.0 %slice-start = ((s8[7340032]{0:T(1024)(128)(4,1)}), s8[4194304]{0:T(1024)(128)(4,1)S(1)}, s32[]{:S(2)}) async-start(s8[7340032]{0:T(1024)(128)(4,1)} %bitcast.6), calls=%async_computation | async-start | bytes 8388608
  3.3 7.7 %copy-start = (bf16[8,128,512]{2,1,0:T(8,128)(2,1)S(1)}, bf16[8,128,512]{2,1,0:T(8,128)(2,1)}, u32[]{:S(2)}) copy-start(bf16[8,128,512]{2,1,0:T(8,128)(2,1)} %keys_ref) | copy-start | bytes 3145732
  3.3 7.7 %copy-start.1 = (bf16[8,64,512]{2,1,0:T(8,128)(2,1)S(1)}, bf16[8,64,512]{2,1,0:T(8,128)(2,1)}, u32[]{:S(2)}) copy-start(bf16[8,64,512]{2,1,0:T(8,128)(2,1)} %latent_ref) | copy-start | bytes 1572868
  3.3 7.8 %copy-start.2 = (bf16[8,64,128]{2,1,0:T(8,128)(2,1)S(1)}, bf16[8,64,128]{2,1,0:T(8,128)(2,1)}, u32[]{:S(2)}) copy-start(bf16[8,64,128]{2,1,0:T(8,128)(2,1)} %rope_keys_ref) | copy-start | bytes 393220
  3.3 7.8 %copy-start.3 = (bf16[8,4096]{1,0:T(8,128)(2,1)S(1)}, bf16[8,4096]{1,0:T(8,128)(2,1)}, u32[]{:S(2)}) copy-start(bf16[8,4096]{1,0:T(8,128)(2,1)} %rope_ref) | copy-start | bytes 196612
  3.3 7.8 %copy-start.4 = (s32[8]{0:T(128)S(1)}, s32[8]{0:T(128)}, u32[]{:S(2)}) copy-start(s32[8]{0:T(128)} %lengths_ref) | copy-start | bytes 100
  3.4 11.9 %slice-start.1 = ((s8[7340032]{0:T(1024)(128)(4,1)}), s8[3145728]{0:T(1024)(128)(4,1)S(1)}, s32[]{:S(2)}) async-start(s8[7340032]{0:T(1024)(128)(4,1)} %bitcast.6), calls=%async_computation.1 | async-start | bytes 6291456
  3.9 9.6 %collective-permute-start.4 = (bf16[16,2048]{1,0:T(8,128)(2,1)S(1)}, bf16[16,2048]{1,0:T(8,128)(2,1)S(1)}, u32[]{:S(2)}, u32[]{:S(2)}) collective-permute-start(bf16[16,2048]{1,0:T(8,128)(2,1)S(1)} %get-tuple-element.37), channel_id=1, source_target_pairs={{0,10},{1,9},{2,8},{3,11},{4,14},{5,13},{6,12},{7,15},{8,2},{9,1},... | collective-permute-start | bytes 196616 | tf_op jit(solution)/shard_map/ppermute | solution.py:301
  8.8 6.5 %collective-permute-start.5 = (bf16[16,2048]{1,0:T(8,128)(2,1)S(1)}, bf16[16,2048]{1,0:T(8,128)(2,1)S(1)}, u32[]{:S(2)}, u32[]{:S(2)}) collective-permute-start(bf16[16,2048]{1,0:T(8,128)(2,1)S(1)} %get-tuple-element.38), channel_id=1, source_target_pairs={{0,12},{1,15},{2,14},{3,13},{4,8},{5,11},{6,10},{7,9},{8,4},{9,7},... | collective-permute-start | bytes 196616 | tf_op jit(solution)/shard_map/ppermute | solution.py:301
  10.2 5.1 %collective-permute-start.6 = (bf16[16,2048]{1,0:T(8,128)(2,1)S(1)}, bf16[16,2048]{1,0:T(8,128)(2,1)S(1)}, u32[]{:S(2)}, u32[]{:S(2)}) collective-permute-start(bf16[16,2048]{1,0:T(8,128)(2,1)S(1)} %get-tuple-element.39), channel_id=1, source_target_pairs={{0,4},{1,7},{2,6},{3,5},{4,0},{5,3},{6,2},{7,1},{8,12},{9,15},{10,... | collective-permute-start | bytes 196616 | tf_op jit(solution)/shard_map/ppermute | solution.py:301
  10.4 4.9 %collective-permute-start.7 = (bf16[16,2048]{1,0:T(8,128)(2,1)S(1)}, bf16[16,2048]{1,0:T(8,128)(2,1)S(1)}, u32[]{:S(2)}, u32[]{:S(2)}) collective-permute-start(bf16[16,2048]{1,0:T(8,128)(2,1)S(1)} %get-tuple-element.40), channel_id=1, source_target_pairs={{0,0},{1,3},{2,2},{3,1},{4,4},{5,7},{6,6},{7,5},{8,8},{9,11},{10,1... | collective-permute-start | bytes 196616 | tf_op jit(solution)/shard_map/ppermute | solution.py:301
  18.1 11.4 %collective-permute-start.9 = (bf16[16,3584]{1,0:T(8,128)(2,1)S(1)}, bf16[16,3584]{1,0:T(8,128)(2,1)S(1)}, u32[]{:S(2)}, u32[]{:S(2)}) collective-permute-start(bf16[16,3584]{1,0:T(8,128)(2,1)S(1)} %get-tuple-element.54), channel_id=1, source_target_pairs={{0,10},{1,9},{2,8},{3,11},{4,14},{5,13},{6,12},{7,15},{8,2},{9,1},... | collective-permute-start | bytes 344072 | tf_op jit(solution)/shard_map/ppermute | solution.py:301
  21.2 8.3 %collective-permute-start.10 = (bf16[16,3584]{1,0:T(8,128)(2,1)S(1)}, bf16[16,3584]{1,0:T(8,128)(2,1)S(1)}, u32[]{:S(2)}, u32[]{:S(2)}) collective-permute-start(bf16[16,3584]{1,0:T(8,128)(2,1)S(1)} %get-tuple-element.55), channel_id=1, source_target_pairs={{0,4},{1,7},{2,6},{3,5},{4,0},{5,3},{6,2},{7,1},{8,12},{9,15},{10,... | collective-permute-start | bytes 344072 | tf_op jit(solution)/shard_map/ppermute | solution.py:301
  22.8 6.7 %collective-permute-start.11 = (bf16[16,3584]{1,0:T(8,128)(2,1)S(1)}, bf16[16,3584]{1,0:T(8,128)(2,1)S(1)}, u32[]{:S(2)}, u32[]{:S(2)}) collective-permute-start(bf16[16,3584]{1,0:T(8,128)(2,1)S(1)} %get-tuple-element.51), channel_id=1, source_target_pairs={{0,0},{1,3},{2,2},{3,1},{4,4},{5,7},{6,6},{7,5},{8,8},{9,11},{10,1... | collective-permute-start | bytes 344072 | tf_op jit(solution)/shard_map/ppermute | solution.py:301
  23.4 7.0 %collective-permute-start.15 = (bf16[8,3584]{1,0:T(8,128)(2,1)S(1)}, bf16[8,3584]{1,0:T(8,128)(2,1)S(1)}, u32[]{:S(2)}, u32[]{:S(2)}) collective-permute-start(bf16[8,3584]{1,0:T(8,128)(2,1)S(1)} %get-tuple-element.61), channel_id=1, source_target_pairs={{0,12},{1,15},{2,14},{3,13},{4,8},{5,11},{6,10},{7,9},{8,4},{9,7},... | collective-permute-start | bytes 172040 | tf_op jit(solution)/shard_map/ppermute | solution.py:301
  24.0 7.7 %collective-permute-start.16 = (bf16[8,3584]{1,0:T(8,128)(2,1)S(1)}, bf16[8,3584]{1,0:T(8,128)(2,1)S(1)}, u32[]{:S(2)}, u32[]{:S(2)}) collective-permute-start(bf16[8,3584]{1,0:T(8,128)(2,1)S(1)} %get-tuple-element.62), channel_id=1, source_target_pairs={{0,13},{1,14},{2,15},{3,12},{4,9},{5,10},{6,11},{7,8},{8,5},{9,6},... | collective-permute-start | bytes 172040 | tf_op jit(solution)/shard_map/ppermute | solution.py:301
  29.7 1.9 %collective-permute-start.14 = (bf16[16,1280]{1,0:T(8,128)(2,1)S(1)}, bf16[16,1280]{1,0:T(8,128)(2,1)S(1)}, u32[]{:S(2)}, u32[]{:S(2)}) collective-permute-start(bf16[16,1280]{1,0:T(8,128)(2,1)S(1)} %get-tuple-element.60), channel_id=1, source_target_pairs={{0,1},{1,0},{2,3},{3,2},{4,5},{5,4},{6,7},{7,6},{8,9},{9,8},{10,11... | collective-permute-start | bytes 122888 | tf_op jit(solution)/shard_map/ppermute | solution.py:293
  29.8 1.8 %collective-permute-start.12 = (bf16[16,1152]{1,0:T(8,128)(2,1)S(1)}, bf16[16,1152]{1,0:T(8,128)(2,1)S(1)}, u32[]{:S(2)}, u32[]{:S(2)}) collective-permute-start(bf16[16,1152]{1,0:T(8,128)(2,1)S(1)} %get-tuple-element.58), channel_id=1, source_target_pairs={{0,1},{1,0},{2,3},{3,2},{4,5},{5,4},{6,7},{7,6},{8,9},{9,8},{10,11... | collective-permute-start | bytes 110600 | tf_op jit(solution)/shard_map/ppermute | solution.py:293
  30.3 1.3 %collective-permute-start.13 = (bf16[16,1152]{1,0:T(8,128)(2,1)S(1)}, bf16[16,1152]{1,0:T(8,128)(2,1)S(1)}, u32[]{:S(2)}, u32[]{:S(2)}) collective-permute-start(bf16[16,1152]{1,0:T(8,128)(2,1)S(1)} %get-tuple-element.59), channel_id=1, source_target_pairs={{0,1},{1,0},{2,3},{3,2},{4,5},{5,4},{6,7},{7,6},{8,9},{9,8},{10,11... | collective-permute-start | bytes 110600 | tf_op jit(solution)/shard_map/ppermute | solution.py:293

commit v7 on v6

--- a/solution.py
+++ b/solution.py
@@ -81,7 +81,7 @@
 def turn_of(node_count, lane_count, lane, number):
     half = node_count // 2
     far_turn = (number - half) // lane_count
-    far_lane = (number - half + lane_count - 1 + far_turn * (lane_count - 1)) % lane_count
+    far_lane = lane_count - 1 - (number - half) % lane_count
     near_turn = (node_count - 1 - number) // lane_count
     turn = jnp.where(number >= half, far_turn, near_turn)
     return jnp.where(jnp.where(number >= half, far_lane, number % lane_count) == lane, turn, -1)
@@ -90,7 +90,7 @@
 def number_of(node_count, lane_count, lane, turn):
     half = node_count // 2
     if turn < half // lane_count:
-        return half + lane_count * turn + (turn + 1 + lane) % lane_count
+        return half + lane_count * turn + lane_count - 1 - lane
     return node_count - lane_count * (turn + 1) + lane
 
 
@@ -253,17 +253,23 @@
 
 
 def last_kernel(pieces, own_ref, place_ref, *refs):
-    other_refs, returned_refs, out_ref = refs[:pieces], refs[pieces:-1], refs[-1]
-    slots = returned_refs[0].shape[0]
-    total = own_ref[...] + jnp.concatenate([other_ref[...].astype(jnp.float32) for other_ref in other_refs], axis=1)
-    for i, returned_ref in enumerate(returned_refs):
+    other_refs, returned_refs, (out_ref, rows_ref, sems) = refs[:pieces], refs[pieces:-3], refs[-3:]
+    place = place_ref[...].astype(jnp.bfloat16)
+    copies = []
+    start = 0
+    for i, other_ref in enumerate(other_refs):
+        columns = slice(start, start + other_ref.shape[1])
+        start = columns.stop
+        returned = jnp.concatenate([returned_ref[:, columns] for returned_ref in returned_refs], axis=0)
+        total = own_ref[:, columns] + other_ref[...].astype(jnp.float32)
         total = total + lax.dot_general(
-            place_ref[i * slots : (i + 1) * slots, :].astype(jnp.bfloat16),
-            returned_ref[...],
-            (((0,), (0,)), ((), ())),
-            preferred_element_type=jnp.float32,
-        )
-    out_ref[...] = total.astype(jnp.bfloat16)
+            place, returned, (((0,), (0,)), ((), ())), preferred_element_type=jnp.float32
+        )
+        rows_ref[:, columns] = total.astype(jnp.bfloat16)
+        copies.append(pltpu.make_async_copy(rows_ref.at[:, columns], out_ref.at[:, columns], sems.at[i]))
+        copies[-1].start()
+    for copy in copies:
+        copy.wait()
 
 
 def local(
@@ -391,8 +397,12 @@
     moe_out = pl.pallas_call(
         functools.partial(last_kernel, len(widths)),
         in_specs=[whole] * (2 + len(widths) + lane_count),
-        out_specs=whole,
+        out_specs=pl.BlockSpec(memory_space=pl.ANY),
         out_shape=jax.ShapeDtypeStruct((row_count, width), jnp.bfloat16),
+        scratch_shapes=[
+            pltpu.VMEM((row_count, width), jnp.bfloat16),
+            pltpu.SemaphoreType.DMA((len(widths),)),
+        ],
         compiler_params=params(2),
         name="last",
     )(in_vmem(own), split_place, *others, *[in_vmem(value) for value in last])

time: 32.8 us -> 32.7 us (level)
  starting transfers between devices: 19.9 us -> 19.2 us
  waiting for transfers between devices: 3.34 us -> 3.87 us
    ppermute x8, waiting for transfers between devices: 0.27 us -> 1.02 us  [other_core(): return lax.ppermute(value, 'lane', [(0, 1), (1, 0)])]
    ppermute x9, starting transfers between devices: 17.8 us -> 17.2 us  [meet(): return lax.ppermute(value, ('node', 'lane'), pairs)]
  transfers between devices with their start and end apart: 17 -> 17, of which waited for: 3 -> 5; matrix products, arithmetic and copies ran while one was open for 0% -> 0% of each run, Pallas kernels for 19% -> 19%
where the time goes in v7:
time: 32.7 us; the launch traced here: 32.4 us
  starting transfers between devices  19.2 us (59%)
  Pallas kernels  8.47 us (26%)
  waiting for transfers between devices  3.87 us (12%)
  between operations  0.83 us (3%)
    ppermute x9, starting transfers between devices, meet(): return lax.ppermute(value, ('node', 'lane'), pairs)  17.2 us
    ppermute x9, waiting for transfers between devices, meet(): return lax.ppermute(value, ('node', 'lane'), pairs)  2.86 us
    pallas_call x1, Pallas kernels, attend(): pl.pallas_call(attend_kernel, in_specs=[pl.BlockSpec(memory_space=pltpu.S...  2.37 us
    ppermute x8, starting transfers between devices, other_core(): return lax.ppermute(value, 'lane', [(0, 1), (1, 0)])  2.03 us
    pallas_call x1, Pallas kernels, local(): pl.pallas_call(functools.partial(other_kernel, turns), in_specs=[whole] *...  1.38 us
    pallas_call x1, Pallas kernels, local(): pl.pallas_call(own_kernel, in_specs=[whole] * (turns + 1), out_specs=whol...  1.37 us
    pallas_call x1, Pallas kernels, local(): pl.pallas_call(load_kernel, in_specs=[outside] * 4, out_specs=[whole] * 4...  1.03 us
    ppermute x8, waiting for transfers between devices, other_core(): return lax.ppermute(value, 'lane', [(0, 1), (1, 0)])  1.02 us
  transfers between devices with their start and end apart: 17, of which 5 were waited for; matrix products, arithmetic and copies ran while one was open for 0% of the time, Pallas kernels for 19%

profile of v7, /device:TPU:0, one launch (start us, length us, event | category | flops | bytes accessed | tf_op | source)
XLA Modules:
  0.0 32.4 jit_solution(6857962981647057745)
XLA Ops:
  0.6 0.5 %collective-permute-start.3 = (bf16[128,1024]{1,0:T(8,128)(2,1)}, bf16[128,1024]{1,0:T(8,128)(2,1)S(1)}, u32[]{:S(2)}, u32[]{:S(2)}) collective-permute-start(bf16[128,1024]{1,0:T(8,128)(2,1)} %bitcast.9), channel_id=1, source_target_pairs={{0,1},{1,0},{2,3},{3,2},{4,5},{5,4},{6,7},{7,6},{8,9},{9,8},{10,11... | collective-permute-start | bytes 786440 | tf_op jit(solution)/shard_map/ppermute | solution.py:299
  1.1 0.1 collective-permute-start
  1.2 0.4 %collective-permute-start.2 = (s32[8,16]{1,0:T(8,128)}, s32[8,16]{1,0:T(8,128)S(1)}, u32[]{:S(2)}, u32[]{:S(2)}) collective-permute-start(s32[8,16]{1,0:T(8,128)} %bitcast.13), channel_id=1, source_target_pairs={{0,1},{1,0},{2,3},{3,2},{4,5},{5,4},{6,7},{7,6},{8,9},{9,8},{10,11... | collective-permute-start | bytes 1544 | tf_op jit(solution)/shard_map/ppermute | solution.py:299
  1.7 0.1 collective-permute-start.1
  1.7 1.0 %load.1 = (f32[8,16]{1,0:T(8,128)S(1)}, s32[4,16]{1,0:T(4,128)S(1)}, s32[8,16]{1,0:T(8,128)S(1)}, bf16[128,1024]{1,0:T(8,128)(2,1)S(1)}) custom-call(f32[8,16]{1,0:T(8,128)} %bitcast.12, s32[4,16]{1,0:T(4,128)} %bitcast.16, s32[8,16]{1,0:T(8,128)} %bitcast.14, bf16[128,1024]{1,0:T(8,128)(2,1)} %bitcast.10), custom_call_target="tpu_custom_call" | custom-call | tf_op jit(solution)/shard_map/load/pallas_call | solution.py:324
  2.8 0.2 collective-permute-done.1.refs_5_.refs_2_
  3.0 0.0 collective-permute-done.refs_4_
  3.0 0.0 collective-permute-done.2.refs_6_.refs_3_
  3.0 0.0 collective-permute-done.3.refs_7_
  3.0 0.3 collective-permute-start.8
  3.3 0.0 slice-start
  3.3 0.0 copy-start
  3.3 0.0 copy-start.1
  3.3 0.0 copy-start.2
  3.3 0.0 copy-start.3
  3.3 0.0 copy-start.4
  3.4 0.0 slice-start.1
  3.4 0.5 %pack.1 = (bf16[16,2048]{1,0:T(8,128)(2,1)S(1)}, bf16[16,2048]{1,0:T(8,128)(2,1)S(1)}, bf16[16,2048]{1,0:T(8,128)(2,1)S(1)}, bf16[16,2048]{1,0:T(8,128)(2,1)S(1)}) custom-call(f32[8,16]{1,0:T(8,128)S(1)} %get-tuple-element.34.refs_0_, s32[4,16]{1,0:T(4,128)S(1)} %get-tuple-element.52.refs_1_.refs_0_, s32[8,16]{1,0:T(8,128)S(1)} %get-tuple-element.35.refs_2_.refs_1_, ...), custom_call_target="tpu_custom_call" | custom-call | flops 6000000000 | tf_op jit(solution)/shard_map/pack/pallas_call | solution.py:336
  3.9 4.9 %collective-permute-start.4 = (bf16[16,2048]{1,0:T(8,128)(2,1)S(1)}, bf16[16,2048]{1,0:T(8,128)(2,1)S(1)}, u32[]{:S(2)}, u32[]{:S(2)}) collective-permute-start(bf16[16,2048]{1,0:T(8,128)(2,1)S(1)} %get-tuple-element.37), channel_id=1, source_target_pairs={{0,10},{1,9},{2,8},{3,11},{4,14},{5,13},{6,12},{7,15},{8,2},{9,1},... | collective-permute-start | bytes 196616 | tf_op jit(solution)/shard_map/ppermute | solution.py:307
  8.8 1.3 %collective-permute-start.5 = (bf16[16,2048]{1,0:T(8,128)(2,1)S(1)}, bf16[16,2048]{1,0:T(8,128)(2,1)S(1)}, u32[]{:S(2)}, u32[]{:S(2)}) collective-permute-start(bf16[16,2048]{1,0:T(8,128)(2,1)S(1)} %get-tuple-element.38), channel_id=1, source_target_pairs={{0,14},{1,13},{2,12},{3,15},{4,10},{5,9},{6,8},{7,11},{8,6},{9,5},... | collective-permute-start | bytes 196616 | tf_op jit(solution)/shard_map/ppermute | solution.py:307
  10.1 0.3 collective-permute-start.6
  10.4 0.7 %collective-permute-start.7 = (bf16[16,2048]{1,0:T(8,128)(2,1)S(1)}, bf16[16,2048]{1,0:T(8,128)(2,1)S(1)}, u32[]{:S(2)}, u32[]{:S(2)}) collective-permute-start(bf16[16,2048]{1,0:T(8,128)(2,1)S(1)} %get-tuple-element.40), channel_id=1, source_target_pairs={{0,0},{1,3},{2,2},{3,1},{4,4},{5,7},{6,6},{7,5},{8,8},{9,11},{10,1... | collective-permute-start | bytes 196616 | tf_op jit(solution)/shard_map/ppermute | solution.py:307
  11.1 0.0 copy-done
  11.1 0.0 copy-done.1
  11.1 0.0 copy-done.2
  11.1 0.0 copy-done.3
  11.1 0.0 copy-done.4
  11.1 2.4 %attend.1 = bf16[8,64,512]{2,1,0:T(8,128)(2,1)} custom-call(s32[8]{0:T(128)S(1)} %copy-done.4, bf16[8,64,512]{2,1,0:T(8,128)(2,1)S(1)} %copy-done.1, bf16[8,4096]{1,0:T(8,128)(2,1)S(1)} %copy-done.3, bf16[8,128,512]{2,1,0:T(8,128)(2,1)S(1)} %copy-done, bf16[8,64,128]{2,1,0:T(8,128)(2,1)S(1)} %copy-done.2), custom_call_target="tpu_custom_call" | custom-call | tf_op jit(solution)/shard_map/attend/pallas_call | solution.py:55
  13.5 0.0 collective-permute-done.4.refs_0_
  13.5 2.5 %collective-permute-done.5.refs_1_ = bf16[16,2048]{1,0:T(8,128)(2,1)S(1)} collective-permute-done((bf16[16,2048]{1,0:T(8,128)(2,1)S(1)}, bf16[16,2048]{1,0:T(8,128)(2,1)S(1)}, u32[]{:S(2)}, u32[]{:S(2)}) %collective-permute-start.5) | collective-permute-done | bytes 65568 | tf_op jit(solution)/shard_map/ppermute | solution.py:307
  15.9 0.0 collective-permute-done.6.refs_2_
  15.9 0.0 collective-permute-done.7.refs_3_
  15.9 0.0 slice-done
  15.9 0.0 slice-done.1
  16.0 1.4 %own.1.refs_4_ = f32[64,3584]{1,0:T(8,128)S(1)} custom-call(bf16[16,2048]{1,0:T(8,128)(2,1)S(1)} %collective-permute-done.4.refs_0_, bf16[16,2048]{1,0:T(8,128)(2,1)S(1)} %collective-permute-done.5.refs_1_, bf16[16,2048]{1,0:T(8,128)(2,1)S(1)} %collective-permute-done.6.refs_2_, bf16[16,2048]{1,0:T(8,128)(2,1)S(1)} %collective-permute-done.7.refs_3_, ...), custom_call_target="tpu_custom_call" | custom-call | tf_op jit(solution)/shard_map/own/pallas_call | solution.py:351
  17.3 0.0 collective-permute-done.8.refs_5_
  17.4 1.4 %other.1 = (bf16[16,3584]{1,0:T(8,128)(2,1)S(1)}, bf16[8,3584]{1,0:T(8,128)(2,1)S(1)}, bf16[8,3584]{1,0:T(8,128)(2,1)S(1)}, bf16[16,3584]{1,0:T(8,128)(2,1)S(1)}, bf16[16,3584]{1,0:T(8,128)(2,1)S(1)}) custom-call(bf16[16,2048]{1,0:T(8,128)(2,1)S(1)} %collective-permute-done.4.refs_0_, bf16[16,2048]{1,0:T(8,128)(2,1)S(1)} %collective-permute-done.5.refs_1_, ...), custom_call_target="tpu_custom_call" | custom-call | tf_op jit(solution)/shard_map/other/pallas_call | solution.py:360
  18.7 2.4 %collective-permute-start.9 = (bf16[16,3584]{1,0:T(8,128)(2,1)S(1)}, bf16[16,3584]{1,0:T(8,128)(2,1)S(1)}, u32[]{:S(2)}, u32[]{:S(2)}) collective-permute-start(bf16[16,3584]{1,0:T(8,128)(2,1)S(1)} %get-tuple-element.54), channel_id=1, source_target_pairs={{0,10},{1,9},{2,8},{3,11},{4,14},{5,13},{6,12},{7,15},{8,2},{9,1},... | collective-permute-start | bytes 344072 | tf_op jit(solution)/shard_map/ppermute | solution.py:307
  21.2 1.6 %collective-permute-start.10 = (bf16[16,3584]{1,0:T(8,128)(2,1)S(1)}, bf16[16,3584]{1,0:T(8,128)(2,1)S(1)}, u32[]{:S(2)}, u32[]{:S(2)}) collective-permute-start(bf16[16,3584]{1,0:T(8,128)(2,1)S(1)} %get-tuple-element.55), channel_id=1, source_target_pairs={{0,4},{1,7},{2,6},{3,5},{4,0},{5,3},{6,2},{7,1},{8,12},{9,15},{10,... | collective-permute-start | bytes 344072 | tf_op jit(solution)/shard_map/ppermute | solution.py:307
  22.8 0.7 %collective-permute-start.11 = (bf16[16,3584]{1,0:T(8,128)(2,1)S(1)}, bf16[16,3584]{1,0:T(8,128)(2,1)S(1)}, u32[]{:S(2)}, u32[]{:S(2)}) collective-permute-start(bf16[16,3584]{1,0:T(8,128)(2,1)S(1)} %get-tuple-element.51), channel_id=1, source_target_pairs={{0,0},{1,3},{2,2},{3,1},{4,4},{5,7},{6,6},{7,5},{8,8},{9,11},{10,1... | collective-permute-start | bytes 344072 | tf_op jit(solution)/shard_map/ppermute | solution.py:307
  23.4 1.4 %collective-permute-start.15 = (bf16[8,3584]{1,0:T(8,128)(2,1)S(1)}, bf16[8,3584]{1,0:T(8,128)(2,1)S(1)}, u32[]{:S(2)}, u32[]{:S(2)}) collective-permute-start(bf16[8,3584]{1,0:T(8,128)(2,1)S(1)} %get-tuple-element.61), channel_id=1, source_target_pairs={{0,14},{1,13},{2,12},{3,15},{4,10},{5,9},{6,8},{7,11},{8,6},{9,5},... | collective-permute-start | bytes 172040 | tf_op jit(solution)/shard_map/ppermute | solution.py:307
  24.8 4.0 %collective-permute-start.16 = (bf16[8,3584]{1,0:T(8,128)(2,1)S(1)}, bf16[8,3584]{1,0:T(8,128)(2,1)S(1)}, u32[]{:S(2)}, u32[]{:S(2)}) collective-permute-start(bf16[8,3584]{1,0:T(8,128)(2,1)S(1)} %get-tuple-element.62), channel_id=1, source_target_pairs={{0,15},{1,12},{2,13},{3,14},{4,11},{5,8},{6,9},{7,10},{8,7},{9,4},... | collective-permute-start | bytes 172040 | tf_op jit(solution)/shard_map/ppermute | solution.py:307
  28.8 0.7 %place.1 = (f32[64,32]{1,0:T(8,128)S(1)}, f32[16,16]{1,0:T(8,128)S(1)}) custom-call(s32[4,16]{1,0:T(4,128)S(1)} %get-tuple-element.52.refs_1_.refs_0_, s32[8,16]{1,0:T(8,128)S(1)} %get-tuple-element.35.refs_2_.refs_1_, s32[4,16]{1,0:T(4,128)S(1)} %collective-permute-done.1.refs_5_.refs_2_, s32[8,16]{1,0:T(8,128)S(1)} %collective-permute-done.2.refs_6_.refs_3_), custom_call_target="tpu_custom_call" | custom-call | tf_op jit(solution)/shard_map/place/pallas_call | solution.py:372
  29.5 0.0 collective-permute-done.9.refs_0_
  29.5 0.0 collective-permute-done.10.refs_1_
  29.5 0.0 collective-permute-done.11.refs_2_
  29.5 0.2 sum.1
  29.7 0.1 collective-permute-start.14
  29.8 0.5 %collective-permute-start.12 = (bf16[16,1152]{1,0:T(8,128)(2,1)S(1)}, bf16[16,1152]{1,0:T(8,128)(2,1)S(1)}, u32[]{:S(2)}, u32[]{:S(2)}) collective-permute-start(bf16[16,1152]{1,0:T(8,128)(2,1)S(1)} %get-tuple-element.58), channel_id=1, source_target_pairs={{0,1},{1,0},{2,3},{3,2},{4,5},{5,4},{6,7},{7,6},{8,9},{9,8},{10,11... | collective-permute-start | bytes 110600 | tf_op jit(solution)/shard_map/ppermute | solution.py:299
  30.3 0.1 collective-permute-start.13
  30.4 0.4 %collective-permute-done.15.refs_3_ = bf16[8,3584]{1,0:T(8,128)(2,1)S(1)} collective-permute-done((bf16[8,3584]{1,0:T(8,128)(2,1)S(1)}, bf16[8,3584]{1,0:T(8,128)(2,1)S(1)}, u32[]{:S(2)}, u32[]{:S(2)}) %collective-permute-start.15) | collective-permute-done | bytes 57376 | tf_op jit(solution)/shard_map/ppermute | solution.py:307
  30.8 0.0 collective-permute-done.16.refs_4_
  30.8 0.4 %collective-permute-done.12.refs_0_ = bf16[16,1152]{1,0:T(8,128)(2,1)S(1)} collective-permute-done((bf16[16,1152]{1,0:T(8,128)(2,1)S(1)}, bf16[16,1152]{1,0:T(8,128)(2,1)S(1)}, u32[]{:S(2)}, u32[]{:S(2)}) %collective-permute-start.12) | collective-permute-done | bytes 36896 | tf_op jit(solution)/shard_map/ppermute | solution.py:299
  31.2 0.3 %collective-permute-done.13.refs_1_ = bf16[16,1152]{1,0:T(8,128)(2,1)S(1)} collective-permute-done((bf16[16,1152]{1,0:T(8,128)(2,1)S(1)}, bf16[16,1152]{1,0:T(8,128)(2,1)S(1)}, u32[]{:S(2)}, u32[]{:S(2)}) %collective-permute-start.13) | collective-permute-done | bytes 36896 | tf_op jit(solution)/shard_map/ppermute | solution.py:299
  31.5 0.0 collective-permute-done.14.refs_2_
  31.5 0.9 %last.1 = bf16[16,3584]{1,0:T(8,128)(2,1)} custom-call(f32[16,3584]{1,0:T(8,128)S(1)} %get-tuple-element.56.own_ref, f32[16,16]{1,0:T(8,128)S(1)} %get-tuple-element.57.place_ref, bf16[16,1152]{1,0:T(8,128)(2,1)S(1)} %collective-permute-done.12.refs_0_, bf16[16,1152]{1,0:T(8,128)(2,1)S(1)} %collective-permute-done.13.refs_1_, ...), custom_call_target="tpu_custom_call" | custom-call | tf_op jit(solution)/shard_map/last/pallas_call | solution.py:397
  (1 shorter events, 0.0 us)
Async XLA Ops:
  0.6 2.4 %collective-permute-start.3 = (bf16[128,1024]{1,0:T(8,128)(2,1)}, bf16[128,1024]{1,0:T(8,128)(2,1)S(1)}, u32[]{:S(2)}, u32[]{:S(2)}) collective-permute-start(bf16[128,1024]{1,0:T(8,128)(2,1)} %bitcast.9), channel_id=1, source_target_pairs={{0,1},{1,0},{2,3},{3,2},{4,5},{5,4},{6,7},{7,6},{8,9},{9,8},{10,11... | collective-permute-start | bytes 786440 | tf_op jit(solution)/shard_map/ppermute | solution.py:299
  1.1 1.9 %collective-permute-start = (f32[8,16]{1,0:T(8,128)}, f32[8,16]{1,0:T(8,128)S(1)}, u32[]{:S(2)}, u32[]{:S(2)}) collective-permute-start(f32[8,16]{1,0:T(8,128)} %bitcast.11), channel_id=1, source_target_pairs={{0,1},{1,0},{2,3},{3,2},{4,5},{5,4},{6,7},{7,6},{8,9},{9,8},{10,11... | collective-permute-start | bytes 1544 | tf_op jit(solution)/shard_map/ppermute | solution.py:299
  1.2 1.8 %collective-permute-start.2 = (s32[8,16]{1,0:T(8,128)}, s32[8,16]{1,0:T(8,128)S(1)}, u32[]{:S(2)}, u32[]{:S(2)}) collective-permute-start(s32[8,16]{1,0:T(8,128)} %bitcast.13), channel_id=1, source_target_pairs={{0,1},{1,0},{2,3},{3,2},{4,5},{5,4},{6,7},{7,6},{8,9},{9,8},{10,11... | collective-permute-start | bytes 1544 | tf_op jit(solution)/shard_map/ppermute | solution.py:299
  1.7 1.4 %collective-permute-start.1 = (s32[4,16]{1,0:T(4,128)}, s32[4,16]{1,0:T(4,128)S(1)}, u32[]{:S(2)}, u32[]{:S(2)}) collective-permute-start(s32[4,16]{1,0:T(4,128)} %bitcast.15), channel_id=1, source_target_pairs={{0,1},{1,0},{2,3},{3,2},{4,5},{5,4},{6,7},{7,6},{8,9},{9,8},{10,11... | collective-permute-start | bytes 776 | tf_op jit(solution)/shard_map/ppermute | solution.py:299
  3.0 14.3 %collective-permute-start.8 = (bf16[1024,3584]{1,0:T(8,128)(2,1)}, bf16[1024,3584]{1,0:T(8,128)(2,1)S(1)}, u32[]{:S(2)}, u32[]{:S(2)}) collective-permute-start(bf16[1024,3584]{1,0:T(8,128)(2,1)} %bitcast.5), channel_id=1, source_target_pairs={{0,1},{1,0},{2,3},{3,2},{4,5},{5,4},{6,7},{7,6},{8,9},{9,8},{10,11... | collective-permute-start | bytes 22020104 | tf_op jit(solution)/shard_map/ppermute | solution.py:299
  3.3 12.6 %slice-start = ((s8[7340032]{0:T(1024)(128)(4,1)}), s8[4194304]{0:T(1024)(128)(4,1)S(1)}, s32[]{:S(2)}) async-start(s8[7340032]{0:T(1024)(128)(4,1)} %bitcast.6), calls=%async_computation | async-start | bytes 8388608
  3.3 7.7 %copy-start = (bf16[8,128,512]{2,1,0:T(8,128)(2,1)S(1)}, bf16[8,128,512]{2,1,0:T(8,128)(2,1)}, u32[]{:S(2)}) copy-start(bf16[8,128,512]{2,1,0:T(8,128)(2,1)} %keys_ref) | copy-start | bytes 3145732
  3.3 7.7 %copy-start.1 = (bf16[8,64,512]{2,1,0:T(8,128)(2,1)S(1)}, bf16[8,64,512]{2,1,0:T(8,128)(2,1)}, u32[]{:S(2)}) copy-start(bf16[8,64,512]{2,1,0:T(8,128)(2,1)} %latent_ref) | copy-start | bytes 1572868
  3.3 7.8 %copy-start.2 = (bf16[8,64,128]{2,1,0:T(8,128)(2,1)S(1)}, bf16[8,64,128]{2,1,0:T(8,128)(2,1)}, u32[]{:S(2)}) copy-start(bf16[8,64,128]{2,1,0:T(8,128)(2,1)} %rope_keys_ref) | copy-start | bytes 393220
  3.3 7.8 %copy-start.3 = (bf16[8,4096]{1,0:T(8,128)(2,1)S(1)}, bf16[8,4096]{1,0:T(8,128)(2,1)}, u32[]{:S(2)}) copy-start(bf16[8,4096]{1,0:T(8,128)(2,1)} %rope_ref) | copy-start | bytes 196612
  3.3 7.8 %copy-start.4 = (s32[8]{0:T(128)S(1)}, s32[8]{0:T(128)}, u32[]{:S(2)}) copy-start(s32[8]{0:T(128)} %lengths_ref) | copy-start | bytes 100
  3.4 12.6 %slice-start.1 = ((s8[7340032]{0:T(1024)(128)(4,1)}), s8[3145728]{0:T(1024)(128)(4,1)S(1)}, s32[]{:S(2)}) async-start(s8[7340032]{0:T(1024)(128)(4,1)} %bitcast.6), calls=%async_computation.1 | async-start | bytes 6291456
  3.9 9.6 %collective-permute-start.4 = (bf16[16,2048]{1,0:T(8,128)(2,1)S(1)}, bf16[16,2048]{1,0:T(8,128)(2,1)S(1)}, u32[]{:S(2)}, u32[]{:S(2)}) collective-permute-start(bf16[16,2048]{1,0:T(8,128)(2,1)S(1)} %get-tuple-element.37), channel_id=1, source_target_pairs={{0,10},{1,9},{2,8},{3,11},{4,14},{5,13},{6,12},{7,15},{8,2},{9,1},... | collective-permute-start | bytes 196616 | tf_op jit(solution)/shard_map/ppermute | solution.py:307
  8.8 7.1 %collective-permute-start.5 = (bf16[16,2048]{1,0:T(8,128)(2,1)S(1)}, bf16[16,2048]{1,0:T(8,128)(2,1)S(1)}, u32[]{:S(2)}, u32[]{:S(2)}) collective-permute-start(bf16[16,2048]{1,0:T(8,128)(2,1)S(1)} %get-tuple-element.38), channel_id=1, source_target_pairs={{0,14},{1,13},{2,12},{3,15},{4,10},{5,9},{6,8},{7,11},{8,6},{9,5},... | collective-permute-start | bytes 196616 | tf_op jit(solution)/shard_map/ppermute | solution.py:307
  10.1 5.8 %collective-permute-start.6 = (bf16[16,2048]{1,0:T(8,128)(2,1)S(1)}, bf16[16,2048]{1,0:T(8,128)(2,1)S(1)}, u32[]{:S(2)}, u32[]{:S(2)}) collective-permute-start(bf16[16,2048]{1,0:T(8,128)(2,1)S(1)} %get-tuple-element.39), channel_id=1, source_target_pairs={{0,4},{1,7},{2,6},{3,5},{4,0},{5,3},{6,2},{7,1},{8,12},{9,15},{10,... | collective-permute-start | bytes 196616 | tf_op jit(solution)/shard_map/ppermute | solution.py:307
  10.4 5.5 %collective-permute-start.7 = (bf16[16,2048]{1,0:T(8,128)(2,1)S(1)}, bf16[16,2048]{1,0:T(8,128)(2,1)S(1)}, u32[]{:S(2)}, u32[]{:S(2)}) collective-permute-start(bf16[16,2048]{1,0:T(8,128)(2,1)S(1)} %get-tuple-element.40), channel_id=1, source_target_pairs={{0,0},{1,3},{2,2},{3,1},{4,4},{5,7},{6,6},{7,5},{8,8},{9,11},{10,1... | collective-permute-start | bytes 196616 | tf_op jit(solution)/shard_map/ppermute | solution.py:307
  18.7 10.7 %collective-permute-start.9 = (bf16[16,3584]{1,0:T(8,128)(2,1)S(1)}, bf16[16,3584]{1,0:T(8,128)(2,1)S(1)}, u32[]{:S(2)}, u32[]{:S(2)}) collective-permute-start(bf16[16,3584]{1,0:T(8,128)(2,1)S(1)} %get-tuple-element.54), channel_id=1, source_target_pairs={{0,10},{1,9},{2,8},{3,11},{4,14},{5,13},{6,12},{7,15},{8,2},{9,1},... | collective-permute-start | bytes 344072 | tf_op jit(solution)/shard_map/ppermute | solution.py:307
  21.2 8.3 %collective-permute-start.10 = (bf16[16,3584]{1,0:T(8,128)(2,1)S(1)}, bf16[16,3584]{1,0:T(8,128)(2,1)S(1)}, u32[]{:S(2)}, u32[]{:S(2)}) collective-permute-start(bf16[16,3584]{1,0:T(8,128)(2,1)S(1)} %get-tuple-element.55), channel_id=1, source_target_pairs={{0,4},{1,7},{2,6},{3,5},{4,0},{5,3},{6,2},{7,1},{8,12},{9,15},{10,... | collective-permute-start | bytes 344072 | tf_op jit(solution)/shard_map/ppermute | solution.py:307
  22.8 6.7 %collective-permute-start.11 = (bf16[16,3584]{1,0:T(8,128)(2,1)S(1)}, bf16[16,3584]{1,0:T(8,128)(2,1)S(1)}, u32[]{:S(2)}, u32[]{:S(2)}) collective-permute-start(bf16[16,3584]{1,0:T(8,128)(2,1)S(1)} %get-tuple-element.51), channel_id=1, source_target_pairs={{0,0},{1,3},{2,2},{3,1},{4,4},{5,7},{6,6},{7,5},{8,8},{9,11},{10,1... | collective-permute-start | bytes 344072 | tf_op jit(solution)/shard_map/ppermute | solution.py:307
  23.4 7.4 %collective-permute-start.15 = (bf16[8,3584]{1,0:T(8,128)(2,1)S(1)}, bf16[8,3584]{1,0:T(8,128)(2,1)S(1)}, u32[]{:S(2)}, u32[]{:S(2)}) collective-permute-start(bf16[8,3584]{1,0:T(8,128)(2,1)S(1)} %get-tuple-element.61), channel_id=1, source_target_pairs={{0,14},{1,13},{2,12},{3,15},{4,10},{5,9},{6,8},{7,11},{8,6},{9,5},... | collective-permute-start | bytes 172040 | tf_op jit(solution)/shard_map/ppermute | solution.py:307
  24.8 6.0 %collective-permute-start.16 = (bf16[8,3584]{1,0:T(8,128)(2,1)S(1)}, bf16[8,3584]{1,0:T(8,128)(2,1)S(1)}, u32[]{:S(2)}, u32[]{:S(2)}) collective-permute-start(bf16[8,3584]{1,0:T(8,128)(2,1)S(1)} %get-tuple-element.62), channel_id=1, source_target_pairs={{0,15},{1,12},{2,13},{3,14},{4,11},{5,8},{6,9},{7,10},{8,7},{9,4},... | collective-permute-start | bytes 172040 | tf_op jit(solution)/shard_map/ppermute | solution.py:307
  29.7 1.8 %collective-permute-start.14 = (bf16[16,1280]{1,0:T(8,128)(2,1)S(1)}, bf16[16,1280]{1,0:T(8,128)(2,1)S(1)}, u32[]{:S(2)}, u32[]{:S(2)}) collective-permute-start(bf16[16,1280]{1,0:T(8,128)(2,1)S(1)} %get-tuple-element.60), channel_id=1, source_target_pairs={{0,1},{1,0},{2,3},{3,2},{4,5},{5,4},{6,7},{7,6},{8,9},{9,8},{10,11... | collective-permute-start | bytes 122888 | tf_op jit(solution)/shard_map/ppermute | solution.py:299
  29.8 1.4 %collective-permute-start.12 = (bf16[16,1152]{1,0:T(8,128)(2,1)S(1)}, bf16[16,1152]{1,0:T(8,128)(2,1)S(1)}, u32[]{:S(2)}, u32[]{:S(2)}) collective-permute-start(bf16[16,1152]{1,0:T(8,128)(2,1)S(1)} %get-tuple-element.58), channel_id=1, source_target_pairs={{0,1},{1,0},{2,3},{3,2},{4,5},{5,4},{6,7},{7,6},{8,9},{9,8},{10,11... | collective-permute-start | bytes 110600 | tf_op jit(solution)/shard_map/ppermute | solution.py:299
  30.3 1.2 %collective-permute-start.13 = (bf16[16,1152]{1,0:T(8,128)(2,1)S(1)}, bf16[16,1152]{1,0:T(8,128)(2,1)S(1)}, u32[]{:S(2)}, u32[]{:S(2)}) collective-permute-start(bf16[16,1152]{1,0:T(8,128)(2,1)S(1)} %get-tuple-element.59), channel_id=1, source_target_pairs={{0,1},{1,0},{2,3},{3,2},{4,5},{5,4},{6,7},{7,6},{8,9},{9,8},{10,11... | collective-permute-start | bytes 110600 | tf_op jit(solution)/shard_map/ppermute | solution.py:299

commit v8 on v7

--- a/solution.py
+++ b/solution.py
@@ -81,7 +81,7 @@
 def turn_of(node_count, lane_count, lane, number):
     half = node_count // 2
     far_turn = (number - half) // lane_count
-    far_lane = lane_count - 1 - (number - half) % lane_count
+    far_lane = (number - half + lane_count - 1 + far_turn * (lane_count - 1)) % lane_count
     near_turn = (node_count - 1 - number) // lane_count
     turn = jnp.where(number >= half, far_turn, near_turn)
     return jnp.where(jnp.where(number >= half, far_lane, number % lane_count) == lane, turn, -1)
@@ -90,7 +90,7 @@
 def number_of(node_count, lane_count, lane, turn):
     half = node_count // 2
     if turn < half // lane_count:
-        return half + lane_count * turn + lane_count - 1 - lane
+        return half + lane_count * turn + (turn + 1 + lane) % lane_count
     return node_count - lane_count * (turn + 1) + lane
 
 

time: 32.7 us -> 32.7 us (level)
  starting transfers between devices: 19.2 us -> 19.9 us
  waiting for transfers between devices: 3.87 us -> 3.34 us
    ppermute x8, waiting for transfers between devices: 1.02 us -> 0.27 us  [other_core(): return lax.ppermute(value, 'lane', [(0, 1), (1, 0)])]
    ppermute x9, starting transfers between devices: 17.2 us -> 17.8 us  [meet(): return lax.ppermute(value, ('node', 'lane'), pairs)]
  transfers between devices with their start and end apart: 17 -> 17, of which waited for: 5 -> 3; matrix products, arithmetic and copies ran while one was open for 0% -> 0% of each run, Pallas kernels for 19% -> 19%
where the time goes in v8:
time: 32.7 us; the launch traced here: 32.5 us
  starting transfers between devices  19.9 us (61%)
  Pallas kernels  8.47 us (26%)
  waiting for transfers between devices  3.34 us (10%)
  between operations  0.83 us (3%)
    ppermute x9, starting transfers between devices, meet(): return lax.ppermute(value, ('node', 'lane'), pairs)  17.8 us
    ppermute x9, waiting for transfers between devices, meet(): return lax.ppermute(value, ('node', 'lane'), pairs)  3.07 us
    pallas_call x1, Pallas kernels, attend(): pl.pallas_call(attend_kernel, in_specs=[pl.BlockSpec(memory_space=pltpu.S...  2.37 us
    ppermute x8, starting transfers between devices, other_core(): return lax.ppermute(value, 'lane', [(0, 1), (1, 0)])  2.03 us
    pallas_call x1, Pallas kernels, local(): pl.pallas_call(functools.partial(other_kernel, turns), in_specs=[whole] *...  1.38 us
    pallas_call x1, Pallas kernels, local(): pl.pallas_call(own_kernel, in_specs=[whole] * (turns + 1), out_specs=whol...  1.37 us
    pallas_call x1, Pallas kernels, local(): pl.pallas_call(load_kernel, in_specs=[outside] * 4, out_specs=[whole] * 4...  1.03 us
    pallas_call x1, Pallas kernels, local(): pl.pallas_call(functools.partial(last_kernel, len(widths)), in_specs=[who...  0.86 us
  transfers between devices with their start and end apart: 17, of which 3 were waited for; matrix products, arithmetic and copies ran while one was open for 0% of the time, Pallas kernels for 19%

profile of v8, /device:TPU:0, one launch (start us, length us, event | category | flops | bytes accessed | tf_op | source)
XLA Modules:
  0.0 32.5 jit_solution(14579586067887226440)
XLA Ops:
  0.6 0.5 %collective-permute-start.3 = (bf16[128,1024]{1,0:T(8,128)(2,1)}, bf16[128,1024]{1,0:T(8,128)(2,1)S(1)}, u32[]{:S(2)}, u32[]{:S(2)}) collective-permute-start(bf16[128,1024]{1,0:T(8,128)(2,1)} %bitcast.9), channel_id=1, source_target_pairs={{0,1},{1,0},{2,3},{3,2},{4,5},{5,4},{6,7},{7,6},{8,9},{9,8},{10,11... | collective-permute-start | bytes 786440 | tf_op jit(solution)/shard_map/ppermute | solution.py:299
  1.1 0.1 collective-permute-start
  1.2 0.4 %collective-permute-start.2 = (s32[8,16]{1,0:T(8,128)}, s32[8,16]{1,0:T(8,128)S(1)}, u32[]{:S(2)}, u32[]{:S(2)}) collective-permute-start(s32[8,16]{1,0:T(8,128)} %bitcast.13), channel_id=1, source_target_pairs={{0,1},{1,0},{2,3},{3,2},{4,5},{5,4},{6,7},{7,6},{8,9},{9,8},{10,11... | collective-permute-start | bytes 1544 | tf_op jit(solution)/shard_map/ppermute | solution.py:299
  1.7 0.1 collective-permute-start.1
  1.7 1.0 %load.1 = (f32[8,16]{1,0:T(8,128)S(1)}, s32[4,16]{1,0:T(4,128)S(1)}, s32[8,16]{1,0:T(8,128)S(1)}, bf16[128,1024]{1,0:T(8,128)(2,1)S(1)}) custom-call(f32[8,16]{1,0:T(8,128)} %bitcast.12, s32[4,16]{1,0:T(4,128)} %bitcast.16, s32[8,16]{1,0:T(8,128)} %bitcast.14, bf16[128,1024]{1,0:T(8,128)(2,1)} %bitcast.10), custom_call_target="tpu_custom_call" | custom-call | tf_op jit(solution)/shard_map/load/pallas_call | solution.py:324
  2.8 0.2 collective-permute-done.1.refs_5_.refs_2_
  3.0 0.0 collective-permute-done.refs_4_
  3.0 0.0 collective-permute-done.2.refs_6_.refs_3_
  3.0 0.0 collective-permute-done.3.refs_7_
  3.0 0.3 collective-permute-start.8
  3.3 0.0 slice-start
  3.3 0.0 copy-start
  3.3 0.0 copy-start.1
  3.3 0.0 copy-start.2
  3.3 0.0 copy-start.3
  3.3 0.0 copy-start.4
  3.4 0.0 slice-start.1
  3.4 0.5 %pack.1 = (bf16[16,2048]{1,0:T(8,128)(2,1)S(1)}, bf16[16,2048]{1,0:T(8,128)(2,1)S(1)}, bf16[16,2048]{1,0:T(8,128)(2,1)S(1)}, bf16[16,2048]{1,0:T(8,128)(2,1)S(1)}) custom-call(f32[8,16]{1,0:T(8,128)S(1)} %get-tuple-element.34.refs_0_, s32[4,16]{1,0:T(4,128)S(1)} %get-tuple-element.52.refs_1_.refs_0_, s32[8,16]{1,0:T(8,128)S(1)} %get-tuple-element.35.refs_2_.refs_1_, ...), custom_call_target="tpu_custom_call" | custom-call | flops 6000000000 | tf_op jit(solution)/shard_map/pack/pallas_call | solution.py:336
  3.9 4.9 %collective-permute-start.4 = (bf16[16,2048]{1,0:T(8,128)(2,1)S(1)}, bf16[16,2048]{1,0:T(8,128)(2,1)S(1)}, u32[]{:S(2)}, u32[]{:S(2)}) collective-permute-start(bf16[16,2048]{1,0:T(8,128)(2,1)S(1)} %get-tuple-element.37), channel_id=1, source_target_pairs={{0,10},{1,9},{2,8},{3,11},{4,14},{5,13},{6,12},{7,15},{8,2},{9,1},... | collective-permute-start | bytes 196616 | tf_op jit(solution)/shard_map/ppermute | solution.py:307
  8.8 1.3 %collective-permute-start.5 = (bf16[16,2048]{1,0:T(8,128)(2,1)S(1)}, bf16[16,2048]{1,0:T(8,128)(2,1)S(1)}, u32[]{:S(2)}, u32[]{:S(2)}) collective-permute-start(bf16[16,2048]{1,0:T(8,128)(2,1)S(1)} %get-tuple-element.38), channel_id=1, source_target_pairs={{0,12},{1,15},{2,14},{3,13},{4,8},{5,11},{6,10},{7,9},{8,4},{9,7},... | collective-permute-start | bytes 196616 | tf_op jit(solution)/shard_map/ppermute | solution.py:307
  10.2 0.2 collective-permute-start.6
  10.4 0.7 %collective-permute-start.7 = (bf16[16,2048]{1,0:T(8,128)(2,1)S(1)}, bf16[16,2048]{1,0:T(8,128)(2,1)S(1)}, u32[]{:S(2)}, u32[]{:S(2)}) collective-permute-start(bf16[16,2048]{1,0:T(8,128)(2,1)S(1)} %get-tuple-element.40), channel_id=1, source_target_pairs={{0,0},{1,3},{2,2},{3,1},{4,4},{5,7},{6,6},{7,5},{8,8},{9,11},{10,1... | collective-permute-start | bytes 196616 | tf_op jit(solution)/shard_map/ppermute | solution.py:307
  11.1 0.0 copy-done
  11.1 0.0 copy-done.1
  11.1 0.0 copy-done.2
  11.1 0.0 copy-done.3
  11.1 0.0 copy-done.4
  11.1 2.4 %attend.1 = bf16[8,64,512]{2,1,0:T(8,128)(2,1)} custom-call(s32[8]{0:T(128)S(1)} %copy-done.4, bf16[8,64,512]{2,1,0:T(8,128)(2,1)S(1)} %copy-done.1, bf16[8,4096]{1,0:T(8,128)(2,1)S(1)} %copy-done.3, bf16[8,128,512]{2,1,0:T(8,128)(2,1)S(1)} %copy-done, bf16[8,64,128]{2,1,0:T(8,128)(2,1)S(1)} %copy-done.2), custom_call_target="tpu_custom_call" | custom-call | tf_op jit(solution)/shard_map/attend/pallas_call | solution.py:55
  13.5 0.0 collective-permute-done.4.refs_0_
  13.5 1.8 %collective-permute-done.5.refs_1_ = bf16[16,2048]{1,0:T(8,128)(2,1)S(1)} collective-permute-done((bf16[16,2048]{1,0:T(8,128)(2,1)S(1)}, bf16[16,2048]{1,0:T(8,128)(2,1)S(1)}, u32[]{:S(2)}, u32[]{:S(2)}) %collective-permute-start.5) | collective-permute-done | bytes 65568 | tf_op jit(solution)/shard_map/ppermute | solution.py:307
  15.3 0.0 collective-permute-done.6.refs_2_
  15.3 0.0 collective-permute-done.7.refs_3_
  15.3 0.0 slice-done
  15.3 0.0 slice-done.1
  15.3 1.4 %own.1.refs_4_ = f32[64,3584]{1,0:T(8,128)S(1)} custom-call(bf16[16,2048]{1,0:T(8,128)(2,1)S(1)} %collective-permute-done.4.refs_0_, bf16[16,2048]{1,0:T(8,128)(2,1)S(1)} %collective-permute-done.5.refs_1_, bf16[16,2048]{1,0:T(8,128)(2,1)S(1)} %collective-permute-done.6.refs_2_, bf16[16,2048]{1,0:T(8,128)(2,1)S(1)} %collective-permute-done.7.refs_3_, ...), custom_call_target="tpu_custom_call" | custom-call | tf_op jit(solution)/shard_map/own/pallas_call | solution.py:351
  16.7 0.0 collective-permute-done.8.refs_5_
  16.7 1.4 %other.1 = (bf16[16,3584]{1,0:T(8,128)(2,1)S(1)}, bf16[8,3584]{1,0:T(8,128)(2,1)S(1)}, bf16[8,3584]{1,0:T(8,128)(2,1)S(1)}, bf16[16,3584]{1,0:T(8,128)(2,1)S(1)}, bf16[16,3584]{1,0:T(8,128)(2,1)S(1)}) custom-call(bf16[16,2048]{1,0:T(8,128)(2,1)S(1)} %collective-permute-done.4.refs_0_, bf16[16,2048]{1,0:T(8,128)(2,1)S(1)} %collective-permute-done.5.refs_1_, ...), custom_call_target="tpu_custom_call" | custom-call | tf_op jit(solution)/shard_map/other/pallas_call | solution.py:360
  18.1 3.1 %collective-permute-start.9 = (bf16[16,3584]{1,0:T(8,128)(2,1)S(1)}, bf16[16,3584]{1,0:T(8,128)(2,1)S(1)}, u32[]{:S(2)}, u32[]{:S(2)}) collective-permute-start(bf16[16,3584]{1,0:T(8,128)(2,1)S(1)} %get-tuple-element.54), channel_id=1, source_target_pairs={{0,10},{1,9},{2,8},{3,11},{4,14},{5,13},{6,12},{7,15},{8,2},{9,1},... | collective-permute-start | bytes 344072 | tf_op jit(solution)/shard_map/ppermute | solution.py:307
  21.2 1.6 %collective-permute-start.10 = (bf16[16,3584]{1,0:T(8,128)(2,1)S(1)}, bf16[16,3584]{1,0:T(8,128)(2,1)S(1)}, u32[]{:S(2)}, u32[]{:S(2)}) collective-permute-start(bf16[16,3584]{1,0:T(8,128)(2,1)S(1)} %get-tuple-element.55), channel_id=1, source_target_pairs={{0,4},{1,7},{2,6},{3,5},{4,0},{5,3},{6,2},{7,1},{8,12},{9,15},{10,... | collective-permute-start | bytes 344072 | tf_op jit(solution)/shard_map/ppermute | solution.py:307
  22.8 0.7 %collective-permute-start.11 = (bf16[16,3584]{1,0:T(8,128)(2,1)S(1)}, bf16[16,3584]{1,0:T(8,128)(2,1)S(1)}, u32[]{:S(2)}, u32[]{:S(2)}) collective-permute-start(bf16[16,3584]{1,0:T(8,128)(2,1)S(1)} %get-tuple-element.51), channel_id=1, source_target_pairs={{0,0},{1,3},{2,2},{3,1},{4,4},{5,7},{6,6},{7,5},{8,8},{9,11},{10,1... | collective-permute-start | bytes 344072 | tf_op jit(solution)/shard_map/ppermute | solution.py:307
  23.4 0.6 %collective-permute-start.15 = (bf16[8,3584]{1,0:T(8,128)(2,1)S(1)}, bf16[8,3584]{1,0:T(8,128)(2,1)S(1)}, u32[]{:S(2)}, u32[]{:S(2)}) collective-permute-start(bf16[8,3584]{1,0:T(8,128)(2,1)S(1)} %get-tuple-element.61), channel_id=1, source_target_pairs={{0,12},{1,15},{2,14},{3,13},{4,8},{5,11},{6,10},{7,9},{8,4},{9,7},... | collective-permute-start | bytes 172040 | tf_op jit(solution)/shard_map/ppermute | solution.py:307
  24.0 4.8 %collective-permute-start.16 = (bf16[8,3584]{1,0:T(8,128)(2,1)S(1)}, bf16[8,3584]{1,0:T(8,128)(2,1)S(1)}, u32[]{:S(2)}, u32[]{:S(2)}) collective-permute-start(bf16[8,3584]{1,0:T(8,128)(2,1)S(1)} %get-tuple-element.62), channel_id=1, source_target_pairs={{0,13},{1,14},{2,15},{3,12},{4,9},{5,10},{6,11},{7,8},{8,5},{9,6},... | collective-permute-start | bytes 172040 | tf_op jit(solution)/shard_map/ppermute | solution.py:307
  28.8 0.7 %place.1 = (f32[64,32]{1,0:T(8,128)S(1)}, f32[16,16]{1,0:T(8,128)S(1)}) custom-call(s32[4,16]{1,0:T(4,128)S(1)} %get-tuple-element.52.refs_1_.refs_0_, s32[8,16]{1,0:T(8,128)S(1)} %get-tuple-element.35.refs_2_.refs_1_, s32[4,16]{1,0:T(4,128)S(1)} %collective-permute-done.1.refs_5_.refs_2_, s32[8,16]{1,0:T(8,128)S(1)} %collective-permute-done.2.refs_6_.refs_3_), custom_call_target="tpu_custom_call" | custom-call | tf_op jit(solution)/shard_map/place/pallas_call | solution.py:372
  29.5 0.0 collective-permute-done.9.refs_0_
  29.5 0.0 collective-permute-done.10.refs_1_
  29.5 0.0 collective-permute-done.11.refs_2_
  29.5 0.2 sum.1
  29.7 0.1 collective-permute-start.14
  29.8 0.5 %collective-permute-start.12 = (bf16[16,1152]{1,0:T(8,128)(2,1)S(1)}, bf16[16,1152]{1,0:T(8,128)(2,1)S(1)}, u32[]{:S(2)}, u32[]{:S(2)}) collective-permute-start(bf16[16,1152]{1,0:T(8,128)(2,1)S(1)} %get-tuple-element.58), channel_id=1, source_target_pairs={{0,1},{1,0},{2,3},{3,2},{4,5},{5,4},{6,7},{7,6},{8,9},{9,8},{10,11... | collective-permute-start | bytes 110600 | tf_op jit(solution)/shard_map/ppermute | solution.py:299
  30.3 0.1 collective-permute-start.13
  30.4 0.0 collective-permute-done.15.refs_3_
  30.4 1.2 %collective-permute-done.16.refs_4_ = bf16[8,3584]{1,0:T(8,128)(2,1)S(1)} collective-permute-done((bf16[8,3584]{1,0:T(8,128)(2,1)S(1)}, bf16[8,3584]{1,0:T(8,128)(2,1)S(1)}, u32[]{:S(2)}, u32[]{:S(2)}) %collective-permute-start.16) | collective-permute-done | bytes 57376 | tf_op jit(solution)/shard_map/ppermute | solution.py:307
  31.7 0.0 collective-permute-done.12.refs_0_
  31.7 0.0 collective-permute-done.13.refs_1_
  31.7 0.0 collective-permute-done.14.refs_2_
  31.7 0.9 %last.1 = bf16[16,3584]{1,0:T(8,128)(2,1)} custom-call(f32[16,3584]{1,0:T(8,128)S(1)} %get-tuple-element.56.own_ref, f32[16,16]{1,0:T(8,128)S(1)} %get-tuple-element.57.place_ref, bf16[16,1152]{1,0:T(8,128)(2,1)S(1)} %collective-permute-done.12.refs_0_, bf16[16,1152]{1,0:T(8,128)(2,1)S(1)} %collective-permute-done.13.refs_1_, ...), custom_call_target="tpu_custom_call" | custom-call | tf_op jit(solution)/shard_map/last/pallas_call | solution.py:397
  (1 shorter events, 0.0 us)
Async XLA Ops:
  0.6 2.4 %collective-permute-start.3 = (bf16[128,1024]{1,0:T(8,128)(2,1)}, bf16[128,1024]{1,0:T(8,128)(2,1)S(1)}, u32[]{:S(2)}, u32[]{:S(2)}) collective-permute-start(bf16[128,1024]{1,0:T(8,128)(2,1)} %bitcast.9), channel_id=1, source_target_pairs={{0,1},{1,0},{2,3},{3,2},{4,5},{5,4},{6,7},{7,6},{8,9},{9,8},{10,11... | collective-permute-start | bytes 786440 | tf_op jit(solution)/shard_map/ppermute | solution.py:299
  1.1 1.9 %collective-permute-start = (f32[8,16]{1,0:T(8,128)}, f32[8,16]{1,0:T(8,128)S(1)}, u32[]{:S(2)}, u32[]{:S(2)}) collective-permute-start(f32[8,16]{1,0:T(8,128)} %bitcast.11), channel_id=1, source_target_pairs={{0,1},{1,0},{2,3},{3,2},{4,5},{5,4},{6,7},{7,6},{8,9},{9,8},{10,11... | collective-permute-start | bytes 1544 | tf_op jit(solution)/shard_map/ppermute | solution.py:299
  1.2 1.8 %collective-permute-start.2 = (s32[8,16]{1,0:T(8,128)}, s32[8,16]{1,0:T(8,128)S(1)}, u32[]{:S(2)}, u32[]{:S(2)}) collective-permute-start(s32[8,16]{1,0:T(8,128)} %bitcast.13), channel_id=1, source_target_pairs={{0,1},{1,0},{2,3},{3,2},{4,5},{5,4},{6,7},{7,6},{8,9},{9,8},{10,11... | collective-permute-start | bytes 1544 | tf_op jit(solution)/shard_map/ppermute | solution.py:299
  1.7 1.4 %collective-permute-start.1 = (s32[4,16]{1,0:T(4,128)}, s32[4,16]{1,0:T(4,128)S(1)}, u32[]{:S(2)}, u32[]{:S(2)}) collective-permute-start(s32[4,16]{1,0:T(4,128)} %bitcast.15), channel_id=1, source_target_pairs={{0,1},{1,0},{2,3},{3,2},{4,5},{5,4},{6,7},{7,6},{8,9},{9,8},{10,11... | collective-permute-start | bytes 776 | tf_op jit(solution)/shard_map/ppermute | solution.py:299
  3.0 13.6 %collective-permute-start.8 = (bf16[1024,3584]{1,0:T(8,128)(2,1)}, bf16[1024,3584]{1,0:T(8,128)(2,1)S(1)}, u32[]{:S(2)}, u32[]{:S(2)}) collective-permute-start(bf16[1024,3584]{1,0:T(8,128)(2,1)} %bitcast.5), channel_id=1, source_target_pairs={{0,1},{1,0},{2,3},{3,2},{4,5},{5,4},{6,7},{7,6},{8,9},{9,8},{10,11... | collective-permute-start | bytes 22020104 | tf_op jit(solution)/shard_map/ppermute | solution.py:299
  3.3 12.0 %slice-start = ((s8[7340032]{0:T(1024)(128)(4,1)}), s8[4194304]{0:T(1024)(128)(4,1)S(1)}, s32[]{:S(2)}) async-start(s8[7340032]{0:T(1024)(128)(4,1)} %bitcast.6), calls=%async_computation | async-start | bytes 8388608
  3.3 7.7 %copy-start = (bf16[8,128,512]{2,1,0:T(8,128)(2,1)S(1)}, bf16[8,128,512]{2,1,0:T(8,128)(2,1)}, u32[]{:S(2)}) copy-start(bf16[8,128,512]{2,1,0:T(8,128)(2,1)} %keys_ref) | copy-start | bytes 3145732
  3.3 7.7 %copy-start.1 = (bf16[8,64,512]{2,1,0:T(8,128)(2,1)S(1)}, bf16[8,64,512]{2,1,0:T(8,128)(2,1)}, u32[]{:S(2)}) copy-start(bf16[8,64,512]{2,1,0:T(8,128)(2,1)} %latent_ref) | copy-start | bytes 1572868
  3.3 7.8 %copy-start.2 = (bf16[8,64,128]{2,1,0:T(8,128)(2,1)S(1)}, bf16[8,64,128]{2,1,0:T(8,128)(2,1)}, u32[]{:S(2)}) copy-start(bf16[8,64,128]{2,1,0:T(8,128)(2,1)} %rope_keys_ref) | copy-start | bytes 393220
  3.3 7.8 %copy-start.3 = (bf16[8,4096]{1,0:T(8,128)(2,1)S(1)}, bf16[8,4096]{1,0:T(8,128)(2,1)}, u32[]{:S(2)}) copy-start(bf16[8,4096]{1,0:T(8,128)(2,1)} %rope_ref) | copy-start | bytes 196612
  3.3 7.8 %copy-start.4 = (s32[8]{0:T(128)S(1)}, s32[8]{0:T(128)}, u32[]{:S(2)}) copy-start(s32[8]{0:T(128)} %lengths_ref) | copy-start | bytes 100
  3.4 11.9 %slice-start.1 = ((s8[7340032]{0:T(1024)(128)(4,1)}), s8[3145728]{0:T(1024)(128)(4,1)S(1)}, s32[]{:S(2)}) async-start(s8[7340032]{0:T(1024)(128)(4,1)} %bitcast.6), calls=%async_computation.1 | async-start | bytes 6291456
  3.9 9.6 %collective-permute-start.4 = (bf16[16,2048]{1,0:T(8,128)(2,1)S(1)}, bf16[16,2048]{1,0:T(8,128)(2,1)S(1)}, u32[]{:S(2)}, u32[]{:S(2)}) collective-permute-start(bf16[16,2048]{1,0:T(8,128)(2,1)S(1)} %get-tuple-element.37), channel_id=1, source_target_pairs={{0,10},{1,9},{2,8},{3,11},{4,14},{5,13},{6,12},{7,15},{8,2},{9,1},... | collective-permute-start | bytes 196616 | tf_op jit(solution)/shard_map/ppermute | solution.py:307
  8.8 6.5 %collective-permute-start.5 = (bf16[16,2048]{1,0:T(8,128)(2,1)S(1)}, bf16[16,2048]{1,0:T(8,128)(2,1)S(1)}, u32[]{:S(2)}, u32[]{:S(2)}) collective-permute-start(bf16[16,2048]{1,0:T(8,128)(2,1)S(1)} %get-tuple-element.38), channel_id=1, source_target_pairs={{0,12},{1,15},{2,14},{3,13},{4,8},{5,11},{6,10},{7,9},{8,4},{9,7},... | collective-permute-start | bytes 196616 | tf_op jit(solution)/shard_map/ppermute | solution.py:307
  10.2 5.1 %collective-permute-start.6 = (bf16[16,2048]{1,0:T(8,128)(2,1)S(1)}, bf16[16,2048]{1,0:T(8,128)(2,1)S(1)}, u32[]{:S(2)}, u32[]{:S(2)}) collective-permute-start(bf16[16,2048]{1,0:T(8,128)(2,1)S(1)} %get-tuple-element.39), channel_id=1, source_target_pairs={{0,4},{1,7},{2,6},{3,5},{4,0},{5,3},{6,2},{7,1},{8,12},{9,15},{10,... | collective-permute-start | bytes 196616 | tf_op jit(solution)/shard_map/ppermute | solution.py:307
  10.4 4.9 %collective-permute-start.7 = (bf16[16,2048]{1,0:T(8,128)(2,1)S(1)}, bf16[16,2048]{1,0:T(8,128)(2,1)S(1)}, u32[]{:S(2)}, u32[]{:S(2)}) collective-permute-start(bf16[16,2048]{1,0:T(8,128)(2,1)S(1)} %get-tuple-element.40), channel_id=1, source_target_pairs={{0,0},{1,3},{2,2},{3,1},{4,4},{5,7},{6,6},{7,5},{8,8},{9,11},{10,1... | collective-permute-start | bytes 196616 | tf_op jit(solution)/shard_map/ppermute | solution.py:307
  18.1 11.4 %collective-permute-start.9 = (bf16[16,3584]{1,0:T(8,128)(2,1)S(1)}, bf16[16,3584]{1,0:T(8,128)(2,1)S(1)}, u32[]{:S(2)}, u32[]{:S(2)}) collective-permute-start(bf16[16,3584]{1,0:T(8,128)(2,1)S(1)} %get-tuple-element.54), channel_id=1, source_target_pairs={{0,10},{1,9},{2,8},{3,11},{4,14},{5,13},{6,12},{7,15},{8,2},{9,1},... | collective-permute-start | bytes 344072 | tf_op jit(solution)/shard_map/ppermute | solution.py:307
  21.2 8.3 %collective-permute-start.10 = (bf16[16,3584]{1,0:T(8,128)(2,1)S(1)}, bf16[16,3584]{1,0:T(8,128)(2,1)S(1)}, u32[]{:S(2)}, u32[]{:S(2)}) collective-permute-start(bf16[16,3584]{1,0:T(8,128)(2,1)S(1)} %get-tuple-element.55), channel_id=1, source_target_pairs={{0,4},{1,7},{2,6},{3,5},{4,0},{5,3},{6,2},{7,1},{8,12},{9,15},{10,... | collective-permute-start | bytes 344072 | tf_op jit(solution)/shard_map/ppermute | solution.py:307
  22.8 6.7 %collective-permute-start.11 = (bf16[16,3584]{1,0:T(8,128)(2,1)S(1)}, bf16[16,3584]{1,0:T(8,128)(2,1)S(1)}, u32[]{:S(2)}, u32[]{:S(2)}) collective-permute-start(bf16[16,3584]{1,0:T(8,128)(2,1)S(1)} %get-tuple-element.51), channel_id=1, source_target_pairs={{0,0},{1,3},{2,2},{3,1},{4,4},{5,7},{6,6},{7,5},{8,8},{9,11},{10,1... | collective-permute-start | bytes 344072 | tf_op jit(solution)/shard_map/ppermute | solution.py:307
  23.4 7.0 %collective-permute-start.15 = (bf16[8,3584]{1,0:T(8,128)(2,1)S(1)}, bf16[8,3584]{1,0:T(8,128)(2,1)S(1)}, u32[]{:S(2)}, u32[]{:S(2)}) collective-permute-start(bf16[8,3584]{1,0:T(8,128)(2,1)S(1)} %get-tuple-element.61), channel_id=1, source_target_pairs={{0,12},{1,15},{2,14},{3,13},{4,8},{5,11},{6,10},{7,9},{8,4},{9,7},... | collective-permute-start | bytes 172040 | tf_op jit(solution)/shard_map/ppermute | solution.py:307
  24.0 7.7 %collective-permute-start.16 = (bf16[8,3584]{1,0:T(8,128)(2,1)S(1)}, bf16[8,3584]{1,0:T(8,128)(2,1)S(1)}, u32[]{:S(2)}, u32[]{:S(2)}) collective-permute-start(bf16[8,3584]{1,0:T(8,128)(2,1)S(1)} %get-tuple-element.62), channel_id=1, source_target_pairs={{0,13},{1,14},{2,15},{3,12},{4,9},{5,10},{6,11},{7,8},{8,5},{9,6},... | collective-permute-start | bytes 172040 | tf_op jit(solution)/shard_map/ppermute | solution.py:307
  29.7 1.9 %collective-permute-start.14 = (bf16[16,1280]{1,0:T(8,128)(2,1)S(1)}, bf16[16,1280]{1,0:T(8,128)(2,1)S(1)}, u32[]{:S(2)}, u32[]{:S(2)}) collective-permute-start(bf16[16,1280]{1,0:T(8,128)(2,1)S(1)} %get-tuple-element.60), channel_id=1, source_target_pairs={{0,1},{1,0},{2,3},{3,2},{4,5},{5,4},{6,7},{7,6},{8,9},{9,8},{10,11... | collective-permute-start | bytes 122888 | tf_op jit(solution)/shard_map/ppermute | solution.py:299
  29.8 1.8 %collective-permute-start.12 = (bf16[16,1152]{1,0:T(8,128)(2,1)S(1)}, bf16[16,1152]{1,0:T(8,128)(2,1)S(1)}, u32[]{:S(2)}, u32[]{:S(2)}) collective-permute-start(bf16[16,1152]{1,0:T(8,128)(2,1)S(1)} %get-tuple-element.58), channel_id=1, source_target_pairs={{0,1},{1,0},{2,3},{3,2},{4,5},{5,4},{6,7},{7,6},{8,9},{9,8},{10,11... | collective-permute-start | bytes 110600 | tf_op jit(solution)/shard_map/ppermute | solution.py:299
  30.3 1.3 %collective-permute-start.13 = (bf16[16,1152]{1,0:T(8,128)(2,1)S(1)}, bf16[16,1152]{1,0:T(8,128)(2,1)S(1)}, u32[]{:S(2)}, u32[]{:S(2)}) collective-permute-start(bf16[16,1152]{1,0:T(8,128)(2,1)S(1)} %get-tuple-element.59), channel_id=1, source_target_pairs={{0,1},{1,0},{2,3},{3,2},{4,5},{5,4},{6,7},{7,6},{8,9},{9,8},{10,11... | collective-permute-start | bytes 110600 | tf_op jit(solution)/shard_map/ppermute | solution.py:299
